TPU v7x, 32 devices: a whole 2x2x4 slice. The times are simulated.
32 devices in a mesh: row: 8 (over z, x), col: 4 (over y, core).
Axes of the slice: x: 2, y: 2, z: 4, core: 2. Of those that a mesh axis runs over, the one named last changes fastest.
Arguments:
- normed: bfloat16 [64, 6144], P('row', 'col'), may hold values from -6 to 6
- out_grad: bfloat16 [64, 6144], P('row', 'col'), may hold values from -6 to 6
- up_weight: bfloat16 [6144, 24576], P('col', 'row'), may hold values from -0.078125 to 0.078125
- up_bias: bfloat16 [24576], P('row'), may hold values from -3 to 3
- down_weight: bfloat16 [24576, 6144], P('row', 'col'), may hold values from -0.0390625 to 0.0390625
Outputs:
- in_grad: bfloat16 [64, 6144], P('row', 'col')
- up_grad: float32 [6144, 24576], P('col', 'row')
- bias_grad: float32 [24576], P('row')
- down_grad: float32 [24576, 6144], P('row', 'col')
All inputs are finite; a program needn't handle non-finite values.
Results may differ from a plain program's by a relative error of at most 0.0049.
Values may be sent and summed in bfloat16 or wider, within the bound.
No kernel may reach another device: no remote copies, remote signals or barrier semaphores. Data moves between devices by JAX's collectives and lax.ppermute only.
A program may use at most 128 MiB of HBM per device.

v0:
```python
import math

import jax
import jax.numpy as jnp
from jax import lax
from jax.sharding import PartitionSpec as P


def gelu_parts(pre):
    cdf = 0.5 * (1.0 + jax.scipy.special.erf(pre / math.sqrt(2.0)))
    dens = jnp.exp(-0.5 * pre * pre) / math.sqrt(2.0 * math.pi)
    return (pre * cdf, cdf + pre * dens)


def on_device(normed, out_grad, up_weight, up_bias, down_weight):
    inputs_all, grads_all = (
        lax.all_gather(normed, "row", axis=0, tiled=True),
        lax.all_gather(out_grad, "row", axis=0, tiled=True),
    )
    part_pre = jnp.dot(inputs_all, up_weight, preferred_element_type=jnp.float32)
    part_hidden = lax.dot_general(
        grads_all, down_weight, (((1,), (1,)), ((), ())), preferred_element_type=jnp.float32
    )
    bias_f = up_bias.astype(jnp.float32)
    pre_share, hidden_share = (
        lax.psum_scatter(part_pre, "col", scatter_dimension=0, tiled=True),
        lax.psum_scatter(part_hidden, "col", scatter_dimension=0, tiled=True),
    )
    act, slope = gelu_parts(pre_share + bias_f)
    act_share = act.astype(jnp.bfloat16)
    grad_share = (hidden_share * slope).astype(jnp.bfloat16)
    hidden, pre_grad = (
        lax.all_gather(act_share, "col", axis=0, tiled=True),
        lax.all_gather(grad_share, "col", axis=0, tiled=True),
    )
    up_grad = lax.dot_general(
        inputs_all, pre_grad, (((0,), (0,)), ((), ())), preferred_element_type=jnp.float32
    )
    down_grad = lax.dot_general(
        hidden, grads_all, (((0,), (0,)), ((), ())), preferred_element_type=jnp.float32
    )
    bias_grad = jnp.sum(pre_grad, axis=0, dtype=jnp.float32)
    part_input = lax.dot_general(
        pre_grad, up_weight, (((1,), (1,)), ((), ())), preferred_element_type=jnp.float32
    )
    in_grad = lax.psum_scatter(part_input, "row", scatter_dimension=0, tiled=True).astype(
        jnp.bfloat16
    )
    return (in_grad, up_grad, bias_grad, down_grad)


def solution(mesh):
    in_specs = (P("row", "col"), P("row", "col"), P("col", "row"), P("row"), P("row", "col"))
    out_specs = (P("row", "col"), P("col", "row"), P("row"), P("row", "col"))
    return jax.shard_map(
        on_device, mesh=mesh, in_specs=in_specs, out_specs=out_specs, check_vma=False
    )
```

profile of v0, /device:TPU:0, one launch (start us, length us, event | category | flops | bytes accessed | tf_op | source)
XLA Modules:
  0.0 208.1 jit_solution(11364030695310954467)
XLA Ops:
  7.2 0.0 reduce-scatter.4.cloned.1.call-start
  7.2 32.6 %all_gather.12 = bf16[64,1536]{1,0:T(8,128)(2,1)S(1)} all-gather(bf16[8,1536]{1,0:T(8,128)(2,1)} %param.6), channel_id=1, replica_groups=mesh['row'=8,'col'=4] {'row'}, dimensions={0}, use_global_device_ids=true | all-gather | bytes 221184 | tf_op jit(solution)/shard_map/all_gather | solution.py:18
  39.9 7.5 %fusion.6 = f32[64,3072]{1,0:T(8,128)} fusion(bf16[64,1536]{1,0:T(8,128)(2,1)S(1)} %all_gather.12, bf16[3072,1536]{1,0:T(8,128)(2,1)} %param.9), kind=kOutput, calls=%fused_computation.11 | convolution fusion | flops 603979776 | bytes 10420224 | tf_op jit(solution)/shard_map/dot_general | solution.py:21
  47.3 0.0 reduce-scatter.4.cloned.1.call-update
  47.4 0.0 reduce-scatter.6.cloned.1.call-start
  47.4 0.0 copy-done
  47.4 30.6 %all_gather.13 = bf16[64,1536]{1,0:T(8,128)(2,1)S(1)} all-gather(bf16[8,1536]{1,0:T(8,128)(2,1)S(1)} %copy-done), channel_id=1, replica_groups=mesh['row'=8,'col'=4] {'row'}, dimensions={0}, use_global_device_ids=true | all-gather | bytes 221184 | tf_op jit(solution)/shard_map/all_gather | solution.py:17
  78.1 6.3 %fusion.7 = f32[64,3072]{1,0:T(8,128)} fusion(bf16[64,1536]{1,0:T(8,128)(2,1)S(1)} %all_gather.13, bf16[1536,3072]{1,0:T(8,128)(2,1)} %param.7), kind=kOutput, calls=%fused_computation.12 | convolution fusion | flops 603979776 | bytes 10420224 | tf_op jit(solution)/shard_map/dot_general | solution.py:20
  84.4 0.0 reduce-scatter.6.cloned.1.call-update
  84.4 0.0 reduce-scatter.8.cloned.1.call-start
  84.4 0.0 copy-done.1
  84.5 0.0 reduce-scatter.4.cloned.1.call-done
  84.5 24.2 %reduce-scatter.6.cloned.1.call-done = f32[16,3072]{1,0:T(8,128)} async-done(((f32[64,3072]{1,0:T(8,128)}), f32[16,3072]{1,0:T(8,128)}) %reduce-scatter.6.cloned.1.call-update) | async-done | bytes 196624 | tf_op jit(solution)/shard_map/reduce_scatter | solution.py:26
  108.7 1.1 multiply_convert_fusion
  109.9 6.1 %all_gather.14 = bf16[64,3072]{1,0:T(8,128)(2,1)S(1)} all-gather(bf16[16,3072]{1,0:T(8,128)(2,1)S(1)} %get-tuple-element.9), channel_id=1, replica_groups=mesh['row'=8,'col'=4] {'col'}, dimensions={0}, use_global_device_ids=true | all-gather | bytes 491520 | tf_op jit(solution)/shard_map/all_gather | solution.py:34
  116.0 7.4 %fusion.8 = f32[64,1536]{1,0:T(8,128)} fusion(bf16[64,3072]{1,0:T(8,128)(2,1)S(1)} %all_gather.14, bf16[1536,3072]{1,0:T(8,128)(2,1)} %param.7), kind=kOutput, calls=%fused_computation.13 | convolution fusion | flops 603979776 | bytes 10223616 | tf_op jit(solution)/shard_map/dot_general | solution.py:43
  123.4 8.3 %convolution_bitcast_fusion = f32[1536,3072]{0,1:T(8,128)} fusion(bf16[64,3072]{1,0:T(8,128)(2,1)S(1)} %all_gather.14, bf16[64,1536]{1,0:T(8,128)(2,1)S(1)} %all_gather.13), kind=kOutput, calls=%fused_computation | convolution fusion | flops 603979776 | bytes 19464192 | tf_op jit(solution)/shard_map/dot_general | solution.py:36
  131.7 6.6 %all_gather.15 = bf16[64,3072]{1,0:T(8,128)(2,1)S(1)} all-gather(bf16[16,3072]{1,0:T(8,128)(2,1)S(1)} %get-tuple-element.8), channel_id=1, replica_groups=mesh['row'=8,'col'=4] {'col'}, dimensions={0}, use_global_device_ids=true | all-gather | bytes 491520 | tf_op jit(solution)/shard_map/all_gather | solution.py:33
  138.2 0.0 reduce-scatter.8.cloned.1.call-update
  138.3 18.7 %copy.9 = f32[1536,3072]{1,0:T(8,128)} copy(f32[1536,3072]{0,1:T(8,128)} %convolution_bitcast_fusion) | data formatting | bytes 37748736
  156.9 0.7 convert_reduce_fusion
  157.6 8.3 %fusion.9 = f32[3072,1536]{1,0:T(8,128)} fusion(bf16[64,3072]{1,0:T(8,128)(2,1)S(1)} %all_gather.15, bf16[64,1536]{1,0:T(8,128)(2,1)S(1)} %all_gather.12), kind=kOutput, calls=%fused_computation.14 | convolution fusion | flops 603979776 | bytes 19464192 | tf_op jit(solution)/shard_map/dot_general | solution.py:39
  165.9 34.3 %reduce-scatter.8.cloned.1.call-done = f32[8,1536]{1,0:T(8,128)} async-done(((f32[64,1536]{1,0:T(8,128)}), f32[8,1536]{1,0:T(8,128)}) %reduce-scatter.8.cloned.1.call-update) | async-done | bytes 49168 | tf_op jit(solution)/shard_map/reduce_scatter | solution.py:46
  200.1 1.4 convert_element_type.17
  (3 shorter events, 0.0 us)
Async XLA Ops:
  7.2 40.3 %copy-start = (bf16[8,1536]{1,0:T(8,128)(2,1)S(1)}, bf16[8,1536]{1,0:T(8,128)(2,1)}, u32[]{:S(2)}) copy-start(bf16[8,1536]{1,0:T(8,128)(2,1)} %param.5) | copy-start | bytes 73732
  7.2 77.3 %reduce-scatter.4.cloned.1.call-start = ((), (), s32[]{:S(2)}) async-start(), calls=%async_computation.3 | async-start | bytes 983040 | tf_op jit(solution)/shard_map/reduce_scatter | solution.py:27
  47.3 37.1 %copy-start.1 = (bf16[3072]{0:T(1024)(128)(2,1)S(1)}, bf16[3072]{0:T(1024)(128)(2,1)}, u32[]{:S(2)}) copy-start(bf16[3072]{0:T(1024)(128)(2,1)} %param.8) | copy-start | bytes 18436
  47.4 61.4 %reduce-scatter.6.cloned.1.call-start = ((), (), s32[]{:S(2)}) async-start(), calls=%async_computation.4 | async-start | bytes 983040 | tf_op jit(solution)/shard_map/reduce_scatter | solution.py:26
  84.4 115.7 %reduce-scatter.8.cloned.1.call-start = ((), (), s32[]{:S(2)}) async-start(), calls=%async_computation.5 | async-start | bytes 442368 | tf_op jit(solution)/shard_map/reduce_scatter | solution.py:46
Sparse Core Ops, SparseCore 0:
  47.5 24.1 reduce-scatter.3
  84.5 24.1 reduce-scatter.5
  138.4 61.7 reduce-scatter.7
where the time goes:
time: 209 us; the launch traced here: 208 us
  blocking collectives  76 us (36%)
  waiting for transfers between devices  58.6 us (28%)
  matrix products  37.7 us (18%)
  local copies, waits for them, and re-layouts  18.7 us (9%)
  between operations  13.8 us (7%)
  other arithmetic  3.21 us (2%)
    reduce_scatter x1, waiting for transfers between devices, on_device(): lax.psum_scatter(part_input, 'row', scatter_dimension=0, tiled=True)  34.3 us
    all_gather x1, blocking collectives, on_device(): lax.all_gather(out_grad, 'row', axis=0, tiled=True)  32.6 us
    all_gather x1, blocking collectives, on_device(): lax.all_gather(normed, 'row', axis=0, tiled=True)  30.6 us
    reduce_scatter x1, waiting for transfers between devices, on_device(): lax.psum_scatter(part_pre, 'col', scatter_dimension=0, tiled=True)  24.2 us
    unnamed x5, local copies, waits for them, and re-layouts  18.7 us
    dot_general x1, matrix products, on_device(): lax.dot_general(inputs_all, pre_grad, (((0,), (0,)), ((), ())), preferred...  8.26 us
    dot_general x1, matrix products, on_device(): lax.dot_general(hidden, grads_all, (((0,), (0,)), ((), ())), preferred_el...  8.26 us
    dot_general x1, matrix products, on_device(): lax.dot_general(grads_all, down_weight, (((1,), (1,)), ((), ())), preferr...  7.5 us
  transfers between devices with their start and end apart: 3, of which 2 were waited for; matrix products, arithmetic and copies ran while one was open for 16% of the time, Pallas kernels for 0%

commit v1 on v0

v1 whole, which is shorter than its diff:
```python
import functools
import math

import jax
import jax.numpy as jnp
from jax import lax
from jax.experimental import pallas as pl
from jax.experimental.pallas import tpu as pltpu
from jax.sharding import PartitionSpec as P

F32 = jnp.float32
BF16 = jnp.bfloat16
MIB = 1024 * 1024


def whole():
    return pl.BlockSpec(memory_space=pltpu.VMEM)


def call(kernel, out_shape, args, flops, nbytes, *, limit=24, grid=None, in_specs=None, out_specs=None, name=None):
    extra = {} if grid is None else {"grid": grid}
    return pl.pallas_call(
        kernel,
        out_shape=out_shape,
        in_specs=in_specs if in_specs is not None else [whole()] * len(args),
        out_specs=out_specs if out_specs is not None else jax.tree.map(lambda _: whole(), out_shape),
        compiler_params=pltpu.CompilerParams(vmem_limit_bytes=limit * MIB),
        cost_estimate=pl.CostEstimate(flops=flops, bytes_accessed=nbytes, transcendentals=0),
        name=name,
        **extra,
    )(*args)


def tree_sum(terms):
    while len(terms) > 1:
        terms = [terms[i] + terms[i + 1] for i in range(0, len(terms), 2)]
    return terms[0]


def divisor(size, most):
    tile = min(size, most)
    while size % tile:
        tile -= 128
    return tile


def core_of():
    return lax.rem(lax.axis_index("col"), 2)


def pre_kernel(core_ref, x_ref, w_ref, keep_ref, send_ref):
    core = core_ref[0]
    half = x_ref.shape[1]
    x = jnp.concatenate([x_ref[core], x_ref[1 - core]], axis=0)
    out = jnp.dot(x, w_ref[...], preferred_element_type=F32)
    keep_ref[...] = out[:half]
    send_ref[...] = out[half:].astype(BF16)


def hid_kernel(core_ref, g_ref, w_ref, keep_ref, send_ref):
    core = core_ref[0]
    half = g_ref.shape[1]
    g = jnp.concatenate([g_ref[core], g_ref[1 - core]], axis=0)
    out = lax.dot_general(g, w_ref[...], (((1,), (1,)), ((), ())), preferred_element_type=F32)
    keep_ref[...] = out[:half]
    send_ref[...] = out[half:].astype(BF16)


def add_kernel(a_ref, b_ref, o_ref):
    o_ref[...] = (a_ref[...] + b_ref[...].astype(F32)).astype(BF16)


def act_kernel(*refs):
    parts, bias_ref, act_ref, slope_ref = refs[:-3], refs[-3], refs[-2], refs[-1]
    pre = tree_sum([r[...].astype(F32) for r in parts]) + bias_ref[...].astype(F32)
    cdf = 0.5 * (1.0 + lax.erf(pre * (1.0 / math.sqrt(2.0))))
    dens = jnp.exp(-0.5 * pre * pre) * (1.0 / math.sqrt(2.0 * math.pi))
    act_ref[...] = (pre * cdf).astype(BF16)
    slope_ref[...] = cdf + pre * dens


def grad_kernel(*refs):
    parts, slope_ref, out_ref = refs[:-2], refs[-2], refs[-1]
    hid = tree_sum([r[...].astype(F32) for r in parts])
    out_ref[...] = (hid * slope_ref[...]).astype(BF16)


def down_kernel(core_ref, h0_ref, h1_ref, g_ref, out_ref):
    core = core_ref[0]
    g = jnp.concatenate([g_ref[core], g_ref[1 - core]], axis=0)
    h = jnp.concatenate([h0_ref[...], h1_ref[...]], axis=0)
    out_ref[...] = lax.dot_general(h, g, (((0,), (0,)), ((), ())), preferred_element_type=F32)


def up_kernel(core_ref, p0_ref, p1_ref, x_ref, out_ref):
    core = core_ref[0]
    x = jnp.concatenate([x_ref[core], x_ref[1 - core]], axis=0)
    p = jnp.concatenate([p0_ref[...], p1_ref[...]], axis=0)
    out_ref[...] = lax.dot_general(x, p, (((0,), (0,)), ((), ())), preferred_element_type=F32)


def in_kernel(core_ref, p0_ref, p1_ref, w_ref, keep_ref, send_ref, bias_ref):
    core = core_ref[0]
    half = p0_ref.shape[0]
    p = jnp.concatenate([p0_ref[...], p1_ref[...]], axis=0)
    out = lax.dot_general(p, w_ref[...], (((1,), (1,)), ((), ())), preferred_element_type=F32)
    own, other = out[:half], out[half:]
    near = core == 0
    keep_ref[...] = jnp.where(near, own, other)
    send_ref[...] = jnp.where(near, other, own).astype(BF16)

    @pl.when(pl.program_id(0) == 0)
    def _():
        own_sum = jnp.sum(p0_ref[...].astype(F32), axis=0, keepdims=True)
        other_sum = jnp.sum(p1_ref[...].astype(F32), axis=0, keepdims=True)
        bias_ref[...] = own_sum + other_sum


def on_device(rows, cols, normed, out_grad, up_weight, up_bias, down_weight):
    mine, feats = normed.shape
    units = up_weight.shape[1]
    half = mine * rows // 2
    core = core_of().astype(jnp.int32).reshape(1)
    smem = pl.BlockSpec(memory_space=pltpu.SMEM)

    def row_swap(x, k):
        return lax.ppermute(x, "row", [(i, i ^ k) for i in range(rows)])

    def col_swap(x, k):
        return lax.ppermute(x, "col", [(i, i ^ k) for i in range(cols)])

    stack = jnp.concatenate([normed, out_grad], axis=0)
    near = jnp.stack([stack] + [row_swap(stack, k) for k in range(2, rows, 2)])
    near = near.reshape(rows // 2, 2, mine, feats).transpose(1, 0, 2, 3).reshape(2, half, feats)
    far = row_swap(near, 1)
    inputs = jnp.stack([near[0], far[0]])
    grads = jnp.stack([near[1], far[1]])

    flops = 4 * half * feats * units
    wbytes = 2 * feats * units
    ft = divisor(units, 512)
    keep_t = jax.ShapeDtypeStruct((half, units), F32)
    send_t = jax.ShapeDtypeStruct((half, units), BF16)
    acts_spec = pl.BlockSpec((2, half, feats), lambda i: (0, 0, 0))
    unit_out = pl.BlockSpec((half, ft), lambda i: (0, i))
    keep_pre, send_pre = call(
        pre_kernel, (keep_t, send_t), (core, inputs, up_weight), flops, wbytes, grid=(units // ft,),
        in_specs=[smem, acts_spec, pl.BlockSpec((feats, ft), lambda i: (0, i))],
        out_specs=(unit_out, unit_out), name="pre",
    )
    other_pre = col_swap(send_pre, 1)
    keep_hid, send_hid = call(
        hid_kernel, (keep_t, send_t), (core, grads, down_weight), flops, wbytes, grid=(units // ft,),
        in_specs=[smem, acts_spec, pl.BlockSpec((ft, feats), lambda i: (i, 0))],
        out_specs=(unit_out, unit_out), name="hid",
    )
    other_hid = col_swap(send_hid, 1)

    chip_pre = call(add_kernel, send_t, (keep_pre, other_pre), half * units, 8 * half * units, name="add_pre")
    pre_parts = [chip_pre] + [col_swap(chip_pre, k) for k in range(2, cols, 2)]
    chip_hid = call(add_kernel, send_t, (keep_hid, other_hid), half * units, 8 * half * units, name="add_hid")
    hid_parts = [chip_hid] + [col_swap(chip_hid, k) for k in range(2, cols, 2)]

    act, slope = call(
        act_kernel, (send_t, keep_t), (*pre_parts, up_bias.reshape(1, units)), 20 * half * units, 10 * half * units, name="act"
    )
    act_far = col_swap(act, 1)
    pg = call(grad_kernel, send_t, (*hid_parts, slope), 3 * half * units, 8 * half * units, name="pre_grad")
    pg_far = col_swap(pg, 1)

    rt = divisor(units, 256)
    tok_block = pl.BlockSpec((half, rt), lambda i: (0, i))
    down_grad = call(
        down_kernel, jax.ShapeDtypeStruct((units, feats), F32), (core, act, act_far, grads), flops, 2 * wbytes,
        grid=(units // rt,), in_specs=[smem, tok_block, tok_block, acts_spec],
        out_specs=pl.BlockSpec((rt, feats), lambda i: (i, 0)), name="down_grad",
    )

    dt = divisor(feats, 256)
    whole_units = pl.BlockSpec((half, units), lambda i: (0, 0))
    feat_out = pl.BlockSpec((half, dt), lambda i: (0, i))
    keep_in, send_in, bias_grad = call(
        in_kernel,
        (
            jax.ShapeDtypeStruct((half, feats), F32),
            jax.ShapeDtypeStruct((half, feats), BF16),
            jax.ShapeDtypeStruct((1, units), F32),
        ),
        (core, pg, pg_far, up_weight), flops, wbytes, grid=(feats // dt,),
        in_specs=[smem, whole_units, whole_units, pl.BlockSpec((dt, units), lambda i: (i, 0))],
        out_specs=(feat_out, feat_out, pl.BlockSpec((1, units), lambda i: (0, 0))), name="in_part",
    )
    far_in = row_swap(send_in, 1)

    ut = divisor(feats, 128)
    up_grad = call(
        up_kernel, jax.ShapeDtypeStruct((feats, units), F32), (core, pg, pg_far, inputs), flops, 2 * wbytes,
        grid=(feats // ut,),
        in_specs=[smem, whole_units, whole_units, pl.BlockSpec((2, half, ut), lambda i: (0, 0, i))],
        out_specs=pl.BlockSpec((ut, units), lambda i: (i, 0)), name="up_grad",
    )

    share = (keep_in + far_in.astype(F32)).reshape(rows // 2, mine, feats)
    sends = share.astype(BF16)
    terms = [share[0]] + [row_swap(sends[k // 2], k).astype(F32) for k in range(2, rows, 2)]
    in_grad = tree_sum(terms).astype(BF16)
    return (in_grad, up_grad, bias_grad.reshape(units), down_grad)


def solution(mesh):
    in_specs = (P("row", "col"), P("row", "col"), P("col", "row"), P("row"), P("row", "col"))
    out_specs = (P("row", "col"), P("col", "row"), P("row"), P("row", "col"))
    body = functools.partial(on_device, mesh.shape["row"], mesh.shape["col"])
    return jax.shard_map(body, mesh=mesh, in_specs=in_specs, out_specs=out_specs, check_vma=False)
```

time: 209 us -> 75.6 us (0.36)
  blocking collectives: 76 us -> 0 us
  waiting for transfers between devices: 58.6 us -> 18.3 us
  matrix products: 37.7 us -> 0 us
  Pallas kernels: 0 us -> 31 us
  starting transfers between devices: 0.12 us -> 15.5 us
  between operations: 13.8 us -> 0.79 us
  local copies, waits for them, and re-layouts: 18.7 us -> 8.99 us
  other arithmetic: 3.21 us -> 0.73 us
    all_gather x4 -> x0, blocking collectives: 76 us -> none  [the longest x1 32.6 us: on_device(): lax.all_gather(out_grad, 'row', axis=0, tiled=True)]
    reduce_scatter x3 -> x0, waiting for transfers between devices: 58.5 us -> none  [the longest x1 34.3 us: on_device(): lax.psum_scatter(part_input, 'row', scatter_dimension=0, tiled=True)]
    dot_general x5 -> x0, matrix products: 37.7 us -> none  [the longest x1 8.26 us: on_device(): lax.dot_general(inputs_all, pre_grad, (((0,), (0,)), ((), ())), preferred...]
    pallas_call x0 -> x9, Pallas kernels: none -> 31 us  [call(): pl.pallas_call(kernel, out_shape=out_shape, in_specs=in_specs if in_specs...]
    ppermute x0 -> x14, waiting for transfers between devices: none -> 18.3 us  [the longest x6 9.64 us: col_swap(): return lax.ppermute(x, 'col', [(i, i ^ k) for i in range(cols)])]
    ppermute x0 -> x14, starting transfers between devices: none -> 15.5 us  [the longest x8 12.2 us: row_swap(): return lax.ppermute(x, 'row', [(i, i ^ k) for i in range(rows)])]
    unnamed x5 -> x13, local copies, waits for them, and re-layouts: 18.7 us -> 8.2 us
  transfers between devices with their start and end apart: 3 -> 14, of which waited for: 2 -> 6; matrix products, arithmetic and copies ran while one was open for 16% -> 0% of each run, Pallas kernels for 0% -> 31%
where the time goes in v1:
time: 75.6 us; the launch traced here: 75.4 us
  Pallas kernels  31 us (41%)
  waiting for transfers between devices  18.3 us (24%)
  starting transfers between devices  15.5 us (21%)
  local copies, waits for them, and re-layouts  8.99 us (12%)
  between operations  0.79 us (1%)
    pallas_call x9, Pallas kernels, call(): pl.pallas_call(kernel, out_shape=out_shape, in_specs=in_specs if in_specs...  31 us
    ppermute x8, starting transfers between devices, row_swap(): return lax.ppermute(x, 'row', [(i, i ^ k) for i in range(rows)])  12.2 us
    ppermute x6, waiting for transfers between devices, col_swap(): return lax.ppermute(x, 'col', [(i, i ^ k) for i in range(cols)])  9.64 us
    ppermute x8, waiting for transfers between devices, row_swap(): return lax.ppermute(x, 'row', [(i, i ^ k) for i in range(rows)])  8.68 us
    unnamed x13, local copies, waits for them, and re-layouts  8.2 us
    ppermute x6, starting transfers between devices, col_swap(): return lax.ppermute(x, 'col', [(i, i ^ k) for i in range(cols)])  3.32 us
  transfers between devices with their start and end apart: 14, of which 6 were waited for; matrix products, arithmetic and copies ran while one was open for 0% of the time, Pallas kernels for 31%

profile of v1, /device:TPU:0, one launch (start us, length us, event | category | flops | bytes accessed | tf_op | source)
XLA Modules:
  0.0 75.4 jit_solution(8856665214493777970)
XLA Ops:
  0.7 0.8 %constant_dynamic-update-slice_fusion.1 = bf16[16,1536]{1,0:T(8,128)(2,1)S(1)} fusion(bf16[8,1536]{1,0:T(8,128)(2,1)} %param.5), kind=kLoop, calls=%fused_computation.12 | loop fusion | bytes 49152
  1.5 0.7 constant_dynamic-update-slice_fusion
  2.2 5.0 %collective-permute-start.2 = (bf16[16,1536]{1,0:T(8,128)(2,1)S(1)}, bf16[16,1536]{1,0:T(8,128)(2,1)S(1)}, u32[]{:S(2)}, u32[]{:S(2)}) collective-permute-start(bf16[16,1536]{1,0:T(8,128)(2,1)S(1)} %constant_dynamic-update-slice_fusion), channel_id=1, source_target_pairs={{0,24},{4,28},{8,16},{12,20},{16,8},{20,12},{24,0},{28,4},{1,25},{... | collective-permute-start | bytes 147464 | tf_op jit(solution)/shard_map/ppermute | solution.py:127
  7.3 0.6 collective-permute-start
  7.8 1.6 %collective-permute-done.2 = bf16[16,1536]{1,0:T(8,128)(2,1)S(1)} collective-permute-done((bf16[16,1536]{1,0:T(8,128)(2,1)S(1)}, bf16[16,1536]{1,0:T(8,128)(2,1)S(1)}, u32[]{:S(2)}, u32[]{:S(2)}) %collective-permute-start.2) | collective-permute-done | bytes 49184 | tf_op jit(solution)/shard_map/ppermute | solution.py:127
  9.5 2.8 %collective-permute-done.1 = bf16[16,1536]{1,0:T(8,128)(2,1)S(1)} collective-permute-done((bf16[16,1536]{1,0:T(8,128)(2,1)S(1)}, bf16[16,1536]{1,0:T(8,128)(2,1)S(1)}, u32[]{:S(2)}, u32[]{:S(2)}) %collective-permute-start.1) | collective-permute-done | bytes 49184 | tf_op jit(solution)/shard_map/ppermute | solution.py:127
  12.3 1.6 %collective-permute-start.3 = (bf16[2,32,1536]{2,1,0:T(8,128)(2,1)S(1)}, bf16[2,32,1536]{2,1,0:T(8,128)(2,1)S(1)}, u32[]{:S(2)}, u32[]{:S(2)}) collective-permute-start(bf16[2,32,1536]{2,1,0:T(8,128)(2,1)S(1)} %get-tuple-element.29), channel_id=1, source_target_pairs={{0,4},{4,0},{8,12},{12,8},{16,20},{20,16},{24,28},{28,24},{1,5},{5... | collective-permute-start | bytes 589832 | tf_op jit(solution)/shard_map/ppermute | solution.py:127
  13.9 4.2 %collective-permute-done.3 = bf16[2,32,1536]{2,1,0:T(8,128)(2,1)S(1)} collective-permute-done((bf16[2,32,1536]{2,1,0:T(8,128)(2,1)S(1)}, bf16[2,32,1536]{2,1,0:T(8,128)(2,1)S(1)}, u32[]{:S(2)}, u32[]{:S(2)}) %collective-permute-start.3) | collective-permute-done | bytes 196640 | tf_op jit(solution)/shard_map/ppermute | solution.py:127
  18.2 3.7 %copy-done = bf16[1536,3072]{1,0:T(8,128)(2,1)S(1)} copy-done((bf16[1536,3072]{1,0:T(8,128)(2,1)S(1)}, bf16[1536,3072]{1,0:T(8,128)(2,1)}, u32[]{:S(2)}) %copy-start) | copy-done | bytes 9437208
  21.9 3.1 %pre.1 = (f32[32,3072]{1,0:T(8,128)S(1)}, bf16[32,3072]{1,0:T(8,128)(2,1)S(1)}) custom-call(s32[1]{0:T(128)} %bitcast.core_ref, bf16[2,32,1536]{2,1,0:T(8,128)(2,1)S(1)} %pad_maximum_fusion.2.x_ref, bf16[1536,3072]{1,0:T(8,128)(2,1)S(1)} %copy-done), custom_call_target="tpu_custom_call" | custom-call | flops 603979776 | bytes 9437184 | tf_op jit(solution)/shard_map/pre/pallas_call | solution.py:22
  25.1 3.7 %copy-done.1 = bf16[3072,1536]{1,0:T(8,128)(2,1)S(1)} copy-done((bf16[3072,1536]{1,0:T(8,128)(2,1)S(1)}, bf16[3072,1536]{1,0:T(8,128)(2,1)}, u32[]{:S(2)}) %copy-start.1) | copy-done | bytes 9437208
  28.8 3.6 %hid.1 = (f32[32,3072]{1,0:T(8,128)S(1)}, bf16[32,3072]{1,0:T(8,128)(2,1)S(1)}) custom-call(s32[1]{0:T(128)} %bitcast.core_ref, bf16[2,32,1536]{2,1,0:T(8,128)(2,1)S(1)} %pad_maximum_fusion.1.g_ref, bf16[3072,1536]{1,0:T(8,128)(2,1)S(1)} %copy-done.1), custom_call_target="tpu_custom_call" | custom-call | flops 603979776 | bytes 9437184 | tf_op jit(solution)/shard_map/hid/pallas_call | solution.py:22
  33.0 1.6 %collective-permute-start.7 = (bf16[32,3072]{1,0:T(8,128)(2,1)S(1)}, bf16[32,3072]{1,0:T(8,128)(2,1)S(1)}, u32[]{:S(2)}, u32[]{:S(2)}) collective-permute-start(bf16[32,3072]{1,0:T(8,128)(2,1)S(1)} %add_pre.1.refs_0_), channel_id=1, source_target_pairs={{0,2},{1,3},{2,0},{3,1},{4,6},{5,7},{6,4},{7,5},{8,10},{9,11},{10,... | collective-permute-start | bytes 589832 | tf_op jit(solution)/shard_map/ppermute | solution.py:130
  34.6 1.0 %collective-permute-start.5 = (bf16[32,3072]{1,0:T(8,128)(2,1)S(1)}, bf16[32,3072]{1,0:T(8,128)(2,1)S(1)}, u32[]{:S(2)}, u32[]{:S(2)}) collective-permute-start(bf16[32,3072]{1,0:T(8,128)(2,1)S(1)} %add_hid.1.refs_0_), channel_id=1, source_target_pairs={{0,2},{1,3},{2,0},{3,1},{4,6},{5,7},{6,4},{7,5},{8,10},{9,11},{10,... | collective-permute-start | bytes 589832 | tf_op jit(solution)/shard_map/ppermute | solution.py:130
  35.7 5.1 %collective-permute-done.7.refs_1_ = bf16[32,3072]{1,0:T(8,128)(2,1)S(1)} collective-permute-done((bf16[32,3072]{1,0:T(8,128)(2,1)S(1)}, bf16[32,3072]{1,0:T(8,128)(2,1)S(1)}, u32[]{:S(2)}, u32[]{:S(2)}) %collective-permute-start.7) | collective-permute-done | bytes 196640 | tf_op jit(solution)/shard_map/ppermute | solution.py:130
  41.1 3.0 %collective-permute-done.5.refs_1_ = bf16[32,3072]{1,0:T(8,128)(2,1)S(1)} collective-permute-done((bf16[32,3072]{1,0:T(8,128)(2,1)S(1)}, bf16[32,3072]{1,0:T(8,128)(2,1)S(1)}, u32[]{:S(2)}, u32[]{:S(2)}) %collective-permute-start.5) | collective-permute-done | bytes 196640 | tf_op jit(solution)/shard_map/ppermute | solution.py:130
  44.3 1.4 %collective-permute-done.8.p1_ref = bf16[32,3072]{1,0:T(8,128)(2,1)S(1)} collective-permute-done((bf16[32,3072]{1,0:T(8,128)(2,1)S(1)}, bf16[32,3072]{1,0:T(8,128)(2,1)S(1)}, u32[]{:S(2)}, u32[]{:S(2)}) %collective-permute-start.8) | collective-permute-done | bytes 196640 | tf_op jit(solution)/shard_map/ppermute | solution.py:130
  45.7 4.4 %in_part.1 = (f32[32,1536]{1,0:T(8,128)S(1)}, bf16[32,1536]{1,0:T(8,128)(2,1)S(1)}, f32[1,3072]{1,0:T(1,128)}) custom-call(s32[1]{0:T(128)} %bitcast.core_ref, bf16[32,3072]{1,0:T(8,128)(2,1)S(1)} %pre_grad.1.p0_ref, bf16[32,3072]{1,0:T(8,128)(2,1)S(1)} %collective-permute-done.8.p1_ref, bf16[1536,3072]{1,0:T(8,128)(2,1)S(1)} %bitcast.24), custom_call_target="tpu_custom_call" | custom-call | flops 603979776 | bytes 9437184 | tf_op jit(solution)/shard_map/in_part/pallas_call | solution.py:22
  50.1 1.5 %collective-permute-start.9 = (bf16[32,1536]{1,0:T(8,128)(2,1)S(1)}, bf16[32,1536]{1,0:T(8,128)(2,1)S(1)}, u32[]{:S(2)}, u32[]{:S(2)}) collective-permute-start(bf16[32,1536]{1,0:T(8,128)(2,1)S(1)} %get-tuple-element.19), channel_id=1, source_target_pairs={{0,4},{4,0},{8,12},{12,8},{16,20},{20,16},{24,28},{28,24},{1,5},{5... | collective-permute-start | bytes 294920 | tf_op jit(solution)/shard_map/ppermute | solution.py:127
  51.6 9.8 %up_grad.1 = f32[1536,3072]{1,0:T(8,128)} custom-call(s32[1]{0:T(128)} %bitcast.core_ref, bf16[32,3072]{1,0:T(8,128)(2,1)S(1)} %pre_grad.1.p0_ref, bf16[32,3072]{1,0:T(8,128)(2,1)S(1)} %collective-permute-done.8.p1_ref, bf16[2,32,1536]{2,1,0:T(8,128)(2,1)S(1)} %pad_maximum_fusion.2.x_ref), custom_call_target="tpu_custom_call" | custom-call | flops 603979776 | bytes 18874368 | tf_op jit(solution)/shard_map/up_grad/pallas_call | solution.py:22
  61.5 0.8 %collective-permute-start.10 = (bf16[8,1536]{1,0:T(8,128)(2,1)S(1)}, bf16[8,1536]{1,0:T(8,128)(2,1)S(1)}, u32[]{:S(2)}, u32[]{:S(2)}) collective-permute-start(bf16[8,1536]{1,0:T(8,128)(2,1)S(1)} %get-tuple-element.30), channel_id=1, source_target_pairs={{0,8},{4,12},{8,0},{12,4},{16,24},{20,28},{24,16},{28,20},{1,9},{5... | collective-permute-start | bytes 73736 | tf_op jit(solution)/shard_map/ppermute | solution.py:127
  62.2 2.7 %collective-permute-start.12 = (bf16[8,1536]{1,0:T(8,128)(2,1)S(1)}, bf16[8,1536]{1,0:T(8,128)(2,1)S(1)}, u32[]{:S(2)}, u32[]{:S(2)}) collective-permute-start(bf16[8,1536]{1,0:T(8,128)(2,1)S(1)} %get-tuple-element.31), channel_id=1, source_target_pairs={{0,24},{4,28},{8,16},{12,20},{16,8},{20,12},{24,0},{28,4},{1,25},{... | collective-permute-start | bytes 73736 | tf_op jit(solution)/shard_map/ppermute | solution.py:127
  65.0 9.7 %down_grad.1 = f32[3072,1536]{1,0:T(8,128)} custom-call(s32[1]{0:T(128)} %bitcast.core_ref, bf16[32,3072]{1,0:T(8,128)(2,1)S(1)} %get-tuple-element.21.h0_ref, bf16[32,3072]{1,0:T(8,128)(2,1)S(1)} %collective-permute-done.13.h1_ref, bf16[2,32,1536]{2,1,0:T(8,128)(2,1)S(1)} %pad_maximum_fusion.1.g_ref), custom_call_target="tpu_custom_call" | custom-call | flops 603979776 | bytes 18874368 | tf_op jit(solution)/shard_map/down_grad/pallas_call | solution.py:22
  74.8 0.6 fusion.1
  (37 shorter events, 1.4 us)
Async XLA Ops:
  0.6 45.1 %slice-start = ((s8[9437184]{0:T(1024)(128)(4,1)}), s8[1048576]{0:T(1024)(128)(4,1)S(1)}, s32[]{:S(2)}) async-start(s8[9437184]{0:T(1024)(128)(4,1)} %bitcast.23), calls=%async_computation | async-start | bytes 2097152
  0.6 35.0 %copy-start.2 = (bf16[3072]{0:T(1024)(128)(2,1)S(1)}, bf16[3072]{0:T(1024)(128)(2,1)}, u32[]{:S(2)}) copy-start(bf16[3072]{0:T(1024)(128)(2,1)} %param.8) | copy-start | bytes 18436
  2.2 7.3 %collective-permute-start.2 = (bf16[16,1536]{1,0:T(8,128)(2,1)S(1)}, bf16[16,1536]{1,0:T(8,128)(2,1)S(1)}, u32[]{:S(2)}, u32[]{:S(2)}) collective-permute-start(bf16[16,1536]{1,0:T(8,128)(2,1)S(1)} %constant_dynamic-update-slice_fusion), channel_id=1, source_target_pairs={{0,24},{4,28},{8,16},{12,20},{16,8},{20,12},{24,0},{28,4},{1,25},{... | collective-permute-start | bytes 147464 | tf_op jit(solution)/shard_map/ppermute | solution.py:127
  7.3 5.0 %collective-permute-start.1 = (bf16[16,1536]{1,0:T(8,128)(2,1)S(1)}, bf16[16,1536]{1,0:T(8,128)(2,1)S(1)}, u32[]{:S(2)}, u32[]{:S(2)}) collective-permute-start(bf16[16,1536]{1,0:T(8,128)(2,1)S(1)} %constant_dynamic-update-slice_fusion), channel_id=1, source_target_pairs={{0,16},{4,20},{8,24},{12,28},{16,0},{20,4},{24,8},{28,12},{1,17},{... | collective-permute-start | bytes 147464 | tf_op jit(solution)/shard_map/ppermute | solution.py:127
  7.3 5.0 %collective-permute-start = (bf16[16,1536]{1,0:T(8,128)(2,1)S(1)}, bf16[16,1536]{1,0:T(8,128)(2,1)S(1)}, u32[]{:S(2)}, u32[]{:S(2)}) collective-permute-start(bf16[16,1536]{1,0:T(8,128)(2,1)S(1)} %constant_dynamic-update-slice_fusion), channel_id=1, source_target_pairs={{0,8},{4,12},{8,0},{12,4},{16,24},{20,28},{24,16},{28,20},{1,9},{5... | collective-permute-start | bytes 147464 | tf_op jit(solution)/shard_map/ppermute | solution.py:127
  12.3 5.8 %collective-permute-start.3 = (bf16[2,32,1536]{2,1,0:T(8,128)(2,1)S(1)}, bf16[2,32,1536]{2,1,0:T(8,128)(2,1)S(1)}, u32[]{:S(2)}, u32[]{:S(2)}) collective-permute-start(bf16[2,32,1536]{2,1,0:T(8,128)(2,1)S(1)} %get-tuple-element.29), channel_id=1, source_target_pairs={{0,4},{4,0},{8,12},{12,8},{16,20},{20,16},{24,28},{28,24},{1,5},{5... | collective-permute-start | bytes 589832 | tf_op jit(solution)/shard_map/ppermute | solution.py:127
  18.2 3.7 %copy-start = (bf16[1536,3072]{1,0:T(8,128)(2,1)S(1)}, bf16[1536,3072]{1,0:T(8,128)(2,1)}, u32[]{:S(2)}) copy-start(bf16[1536,3072]{1,0:T(8,128)(2,1)} %w_ref.5) | copy-start | bytes 28311556
  21.9 23.8 %slice-start.1 = ((s8[9437184]{0:T(1024)(128)(4,1)}), s8[4194304]{0:T(1024)(128)(4,1)S(1)}, s32[]{:S(2)}) async-start(s8[9437184]{0:T(1024)(128)(4,1)} %bitcast.23), calls=%async_computation.1 | async-start | bytes 8388608
  25.0 8.0 %collective-permute-start.6 = (bf16[32,3072]{1,0:T(8,128)(2,1)S(1)}, bf16[32,3072]{1,0:T(8,128)(2,1)S(1)}, u32[]{:S(2)}, u32[]{:S(2)}) collective-permute-start(bf16[32,3072]{1,0:T(8,128)(2,1)S(1)} %get-tuple-element.16), channel_id=1, source_target_pairs={{0,1},{1,0},{2,3},{3,2},{4,5},{5,4},{6,7},{7,6},{8,9},{9,8},{10,11... | collective-permute-start | bytes 589832 | tf_op jit(solution)/shard_map/ppermute | solution.py:130
  25.1 3.7 %copy-start.1 = (bf16[3072,1536]{1,0:T(8,128)(2,1)S(1)}, bf16[3072,1536]{1,0:T(8,128)(2,1)}, u32[]{:S(2)}) copy-start(bf16[3072,1536]{1,0:T(8,128)(2,1)} %w_ref.3) | copy-start | bytes 28311556
  28.7 16.9 %slice-start.2 = ((s8[9437184]{0:T(1024)(128)(4,1)}), s8[4194304]{0:T(1024)(128)(4,1)S(1)}, s32[]{:S(2)}) async-start(s8[9437184]{0:T(1024)(128)(4,1)} %bitcast.23), calls=%async_computation.2 | async-start | bytes 8388608
  32.4 2.2 %collective-permute-start.4 = (bf16[32,3072]{1,0:T(8,128)(2,1)S(1)}, bf16[32,3072]{1,0:T(8,128)(2,1)S(1)}, u32[]{:S(2)}, u32[]{:S(2)}) collective-permute-start(bf16[32,3072]{1,0:T(8,128)(2,1)S(1)} %get-tuple-element.14), channel_id=1, source_target_pairs={{0,1},{1,0},{2,3},{3,2},{4,5},{5,4},{6,7},{7,6},{8,9},{9,8},{10,11... | collective-permute-start | bytes 589832 | tf_op jit(solution)/shard_map/ppermute | solution.py:130
  33.0 7.8 %collective-permute-start.7 = (bf16[32,3072]{1,0:T(8,128)(2,1)S(1)}, bf16[32,3072]{1,0:T(8,128)(2,1)S(1)}, u32[]{:S(2)}, u32[]{:S(2)}) collective-permute-start(bf16[32,3072]{1,0:T(8,128)(2,1)S(1)} %add_pre.1.refs_0_), channel_id=1, source_target_pairs={{0,2},{1,3},{2,0},{3,1},{4,6},{5,7},{6,4},{7,5},{8,10},{9,11},{10,... | collective-permute-start | bytes 589832 | tf_op jit(solution)/shard_map/ppermute | solution.py:130
  34.6 9.5 %collective-permute-start.5 = (bf16[32,3072]{1,0:T(8,128)(2,1)S(1)}, bf16[32,3072]{1,0:T(8,128)(2,1)S(1)}, u32[]{:S(2)}, u32[]{:S(2)}) collective-permute-start(bf16[32,3072]{1,0:T(8,128)(2,1)S(1)} %add_hid.1.refs_0_), channel_id=1, source_target_pairs={{0,2},{1,3},{2,0},{3,1},{4,6},{5,7},{6,4},{7,5},{8,10},{9,11},{10,... | collective-permute-start | bytes 589832 | tf_op jit(solution)/shard_map/ppermute | solution.py:130
  44.2 1.5 %collective-permute-start.8 = (bf16[32,3072]{1,0:T(8,128)(2,1)S(1)}, bf16[32,3072]{1,0:T(8,128)(2,1)S(1)}, u32[]{:S(2)}, u32[]{:S(2)}) collective-permute-start(bf16[32,3072]{1,0:T(8,128)(2,1)S(1)} %pre_grad.1.p0_ref), channel_id=1, source_target_pairs={{0,1},{1,0},{2,3},{3,2},{4,5},{5,4},{6,7},{7,6},{8,9},{9,8},{10,11... | collective-permute-start | bytes 589832 | tf_op jit(solution)/shard_map/ppermute | solution.py:130
  50.1 11.3 %collective-permute-start.9 = (bf16[32,1536]{1,0:T(8,128)(2,1)S(1)}, bf16[32,1536]{1,0:T(8,128)(2,1)S(1)}, u32[]{:S(2)}, u32[]{:S(2)}) collective-permute-start(bf16[32,1536]{1,0:T(8,128)(2,1)S(1)} %get-tuple-element.19), channel_id=1, source_target_pairs={{0,4},{4,0},{8,12},{12,8},{16,20},{20,16},{24,28},{28,24},{1,5},{5... | collective-permute-start | bytes 294920 | tf_op jit(solution)/shard_map/ppermute | solution.py:127
  51.6 13.4 %collective-permute-start.13 = (bf16[32,3072]{1,0:T(8,128)(2,1)S(1)}, bf16[32,3072]{1,0:T(8,128)(2,1)S(1)}, u32[]{:S(2)}, u32[]{:S(2)}) collective-permute-start(bf16[32,3072]{1,0:T(8,128)(2,1)S(1)} %get-tuple-element.21.h0_ref), channel_id=1, source_target_pairs={{0,1},{1,0},{2,3},{3,2},{4,5},{5,4},{6,7},{7,6},{8,9},{9,8},{10,11... | collective-permute-start | bytes 589832 | tf_op jit(solution)/shard_map/ppermute | solution.py:130
  61.5 13.3 %collective-permute-start.10 = (bf16[8,1536]{1,0:T(8,128)(2,1)S(1)}, bf16[8,1536]{1,0:T(8,128)(2,1)S(1)}, u32[]{:S(2)}, u32[]{:S(2)}) collective-permute-start(bf16[8,1536]{1,0:T(8,128)(2,1)S(1)} %get-tuple-element.30), channel_id=1, source_target_pairs={{0,8},{4,12},{8,0},{12,4},{16,24},{20,28},{24,16},{28,20},{1,9},{5... | collective-permute-start | bytes 73736 | tf_op jit(solution)/shard_map/ppermute | solution.py:127
  62.2 12.5 %collective-permute-start.12 = (bf16[8,1536]{1,0:T(8,128)(2,1)S(1)}, bf16[8,1536]{1,0:T(8,128)(2,1)S(1)}, u32[]{:S(2)}, u32[]{:S(2)}) collective-permute-start(bf16[8,1536]{1,0:T(8,128)(2,1)S(1)} %get-tuple-element.31), channel_id=1, source_target_pairs={{0,24},{4,28},{8,16},{12,20},{16,8},{20,12},{24,0},{28,4},{1,25},{... | collective-permute-start | bytes 73736 | tf_op jit(solution)/shard_map/ppermute | solution.py:127
  64.9 9.8 %collective-permute-start.11 = (bf16[8,1536]{1,0:T(8,128)(2,1)S(1)}, bf16[8,1536]{1,0:T(8,128)(2,1)S(1)}, u32[]{:S(2)}, u32[]{:S(2)}) collective-permute-start(bf16[8,1536]{1,0:T(8,128)(2,1)S(1)} %get-tuple-element.32), channel_id=1, source_target_pairs={{0,16},{4,20},{8,24},{12,28},{16,0},{20,4},{24,8},{28,12},{1,17},{... | collective-permute-start | bytes 73736 | tf_op jit(solution)/shard_map/ppermute | solution.py:127

commit v2 on v0

v2 whole, which is shorter than its diff:
```python
import functools
import math

import jax
import jax.numpy as jnp
from jax import lax
from jax.experimental import pallas as pl
from jax.experimental.pallas import tpu as pltpu
from jax.sharding import PartitionSpec as P

F32 = jnp.float32
BF16 = jnp.bfloat16
MIB = 1024 * 1024
SLOTS = 4


def vmem():
    return pl.BlockSpec(memory_space=pltpu.VMEM)


def smem():
    return pl.BlockSpec(memory_space=pltpu.SMEM)


def anywhere():
    return pl.BlockSpec(memory_space=pl.ANY)


def call(kernel, name, out_shape, args, *, flops=0, nbytes=0, limit=16, in_specs=None, out_specs=None, scratch=(), aliases=None, after=()):
    in_specs = in_specs if in_specs is not None else [vmem()] * len(args)
    body = kernel
    if after:
        n, m = len(args), len(args) + len(after)

        def body(*refs):
            kernel(*refs[:n], *refs[m:])

    return pl.pallas_call(
        body,
        out_shape=out_shape,
        in_specs=in_specs + [anywhere()] * len(after),
        out_specs=out_specs if out_specs is not None else jax.tree.map(lambda _: vmem(), out_shape),
        scratch_shapes=list(scratch),
        input_output_aliases=aliases or {},
        compiler_params=pltpu.CompilerParams(vmem_limit_bytes=limit * MIB),
        cost_estimate=pl.CostEstimate(flops=0, bytes_accessed=0, transcendentals=0),
        name=name,
    )(*args, *after)


def tree_sum(terms):
    while len(terms) > 1:
        terms = [terms[i] + terms[i + 1] for i in range(0, len(terms), 2)]
    return terms[0]


def divisor(size, most):
    tile = min(size, most)
    while size % tile:
        tile -= 128
    return tile


def stack_kernel(a_ref, b_ref, o_ref, sems):
    copies = [pltpu.make_async_copy(r, o_ref.at[i], sems.at[i]) for i, r in enumerate((a_ref, b_ref))]
    for c in copies:
        c.start()
    for c in copies:
        c.wait()


def load_kernel(w_ref, o_ref, sem):
    copy = pltpu.make_async_copy(w_ref, o_ref, sem)
    copy.start()
    copy.wait()


def load(weight, name, limit, after=()):
    return call(
        load_kernel, name, pltpu.VMEM(weight.shape, weight.dtype), (weight,), nbytes=2 * weight.size, limit=limit,
        in_specs=[pl.BlockSpec(memory_space=pltpu.HBM)], out_specs=vmem(), scratch=[pltpu.SemaphoreType.DMA(())],
        after=after,
    )


def local_tokens(core, near_ref, far_ref):
    first = core == 0
    near, far = near_ref[...], far_ref[...]
    return jnp.concatenate([jnp.where(first, near, far), jnp.where(first, far, near)], axis=0)


def pre_kernel(core_ref, near_ref, far_ref, w_ref, keep_ref, send_ref):
    half, units = keep_ref.shape
    x = local_tokens(core_ref[0], near_ref, far_ref)
    tile = divisor(units, 512)
    for i in range(0, units, tile):
        out = jnp.dot(x, w_ref[:, i : i + tile], preferred_element_type=F32)
        keep_ref[:, i : i + tile] = out[:half]
        send_ref[:, i : i + tile] = out[half:]


def hid_kernel(start, core_ref, near_ref, far_ref, w_ref, keep_ref, send_ref):
    half, units = keep_ref.shape
    g = local_tokens(core_ref[0], near_ref, far_ref)
    tile = divisor(units, 512)
    for i in range(0, units, tile):
        w = w_ref[start + i : start + i + tile, :]
        out = lax.dot_general(w, g, (((1,), (1,)), ((), ())), preferred_element_type=F32).T
        keep_ref[:, i : i + tile] = out[:half]
        send_ref[:, i : i + tile] = out[half:]


def add_kernel(*refs):
    n, out_ref = len(refs) // 2, refs[-1]
    at = 0
    for a, b in zip(refs[:n], refs[n : 2 * n]):
        width = a.shape[1]
        out_ref[:, at : at + width] = (a[...] + b[...]).astype(BF16)
        at += width


def sum_kernel(a_ref, b_ref, out_ref):
    out_ref[...] = a_ref[...] + b_ref[...]


def act_kernel(*refs):
    parts, bias_ref, act_ref, slope_ref = refs[:-3], refs[-3], refs[-2], refs[-1]
    pre = tree_sum([r[...].astype(F32) for r in parts]) + bias_ref[...].astype(F32)
    cdf = 0.5 * (1.0 + lax.erf(pre * (1.0 / math.sqrt(2.0))))
    dens = jnp.exp(-0.5 * pre * pre) * (1.0 / math.sqrt(2.0 * math.pi))
    act_ref[...] = (pre * cdf).astype(BF16)
    slope_ref[...] = cdf + pre * dens


def grad_kernel(*refs):
    parts, slope_ref, out_ref = refs[:-2], refs[-2], refs[-1]
    hid = tree_sum([r[...].astype(F32) for r in parts])
    out_ref[...] = (hid * slope_ref[...]).astype(BF16)


def write_tiles(first, last, rows, make, out_ref, buf, sems, between=()):
    def copy(t):
        s = (t - first) % SLOTS
        return pltpu.make_async_copy(buf.at[s], out_ref.at[pl.ds(t * rows, rows), :], sems.at[s])

    work = list(between)
    count = last - first
    for t in range(first, last):
        if t - first >= SLOTS:
            copy(t - SLOTS).wait()
        buf[(t - first) % SLOTS] = make(t * rows)
        copy(t).start()
        left = len(between) * (last - 1 - t) // count
        while len(work) > left:
            work.pop(0)()
    for t in range(max(first, last - SLOTS), last):
        copy(t).wait()


def outer(a, b):
    return lax.dot_general(a, b, (((0,), (0,)), ((), ())), preferred_element_type=F32)


def down_kernel(first, last, rows, core_ref, h0_ref, h1_ref, near_ref, far_ref, *refs):
    out_ref, buf, sems = refs[-3:]
    g = local_tokens(core_ref[0], near_ref, far_ref)

    def make(at):
        return outer(jnp.concatenate([h0_ref[:, at : at + rows], h1_ref[:, at : at + rows]], axis=0), g)

    write_tiles(first, last, rows, make, out_ref, buf, sems)


def down_in_kernel(
    first, last, rows, core_ref, h0_ref, h1_ref, near_ref, far_ref, p0_ref, p1_ref, w_ref, _, out_ref, keep_ref, send_ref,
    bias_ref, buf, sems,
):
    near_first = core_ref[0] == 0
    g = local_tokens(core_ref[0], near_ref, far_ref)
    half = p0_ref.shape[0]
    p = jnp.concatenate([p0_ref[...], p1_ref[...]], axis=0)

    def make(at):
        return outer(jnp.concatenate([h0_ref[:, at : at + rows], h1_ref[:, at : at + rows]], axis=0), g)

    feats = w_ref.shape[0]
    tile = divisor(feats, 256)

    def part(i):
        w = w_ref[i : i + tile, :]
        out = lax.dot_general(w, p, (((1,), (1,)), ((), ())), preferred_element_type=F32).T
        own, other = out[:half], out[half:]
        keep_ref[:, i : i + tile] = jnp.where(near_first, own, other)
        send_ref[:, i : i + tile] = jnp.where(near_first, other, own)

    def bias():
        own = jnp.sum(p0_ref[...].astype(F32), axis=0, keepdims=True)
        bias_ref[...] = own + jnp.sum(p1_ref[...].astype(F32), axis=0, keepdims=True)

    work = [functools.partial(part, i) for i in range(0, feats, tile)] + [bias]
    write_tiles(first, last, rows, make, out_ref, buf, sems, work)


def up_kernel(first, last, rows, core_ref, p0_ref, p1_ref, near_ref, far_ref, *refs):
    out_ref, done_ref, buf, sems = refs[-4:]
    done_ref[...] = jnp.zeros_like(done_ref)
    p = local_tokens(core_ref[0], p0_ref, p1_ref)

    def make(at):
        return outer(jnp.concatenate([near_ref[:, at : at + rows], far_ref[:, at : at + rows]], axis=0), p)

    write_tiles(first, last, rows, make, out_ref, buf, sems)


def on_device(rows, cols, normed, out_grad, up_weight, up_bias, down_weight):
    mine, feats = normed.shape
    units = up_weight.shape[1]
    half = mine * rows // 2
    core = lax.rem(lax.axis_index("col"), 2).astype(jnp.int32).reshape(1)

    def row_swap(x, k):
        return lax.ppermute(x, "row", [(i, i ^ k) for i in range(rows)])

    def col_swap(x, k):
        return lax.ppermute(x, "col", [(i, i ^ k) for i in range(cols)])

    stack = call(
        stack_kernel, "stack", pltpu.VMEM((2, mine, feats), BF16), (normed, out_grad), nbytes=8 * mine * feats,
        in_specs=[anywhere()] * 2, out_specs=vmem(), scratch=[pltpu.SemaphoreType.DMA((2,))], limit=60,
    )
    near = jnp.stack([stack] + [row_swap(stack, k) for k in range(2, rows, 2)], axis=1)
    near = near.reshape(2, half, feats)
    far = row_swap(near, 1)
    w_up = load(up_weight, "load_up", 44)
    w_down = load(down_weight, "load_down", 38, (near,))

    flops = 4 * half * feats * units
    wbytes = 2 * feats * units
    keep_t = jax.ShapeDtypeStruct((half, units), F32)
    bf_t = jax.ShapeDtypeStruct((half, units), BF16)
    x_near, x_far, g_near, g_far = near[0], far[0], near[1], far[1]

    keep_pre, send_pre = call(
        pre_kernel, "pre", (keep_t, keep_t), (core, x_near, x_far, w_up), flops=flops, nbytes=wbytes,
        in_specs=[smem()] + [vmem()] * 3, after=(w_down,),
    )
    other_pre = col_swap(send_pre, 1)
    pieces = 2 if units % 256 == 0 else 1
    width = units // pieces
    piece_t = jax.ShapeDtypeStruct((half, width), F32)

    def hid_piece(i, after):
        return call(
            functools.partial(hid_kernel, i * width), "hid", (piece_t, piece_t), (core, g_near, g_far, w_down),
            flops=flops // pieces, nbytes=wbytes // pieces, in_specs=[smem()] + [vmem()] * 3, after=after,
        )

    hids = [hid_piece(0, ())]
    chip_pre = call(add_kernel, "add_pre", bf_t, (keep_pre, other_pre), nbytes=10 * half * units)
    pre_parts = [chip_pre] + [col_swap(chip_pre, k) for k in range(2, cols, 2)]
    hids += [hid_piece(i, (chip_pre,)) for i in range(1, pieces)]
    others = [col_swap(send, 1) for _, send in hids]
    chip_hid = call(add_kernel, "add_hid", bf_t, (*[k for k, _ in hids], *others), nbytes=10 * half * units)
    hid_parts = [chip_hid] + [col_swap(chip_hid, k) for k in range(2, cols, 2)]

    act, slope = call(act_kernel, "act", (bf_t, keep_t), (*pre_parts, up_bias.reshape(1, units)), nbytes=10 * half * units)
    act_far = col_swap(act, 1)
    pg = call(grad_kernel, "pre_grad", bf_t, (*hid_parts, slope), nbytes=10 * half * units)
    pg_far = col_swap(pg, 1)

    rt = divisor(units, 256)
    tiles = units // rt
    cut = tiles // 2
    down_t = jax.ShapeDtypeStruct((units, feats), F32)
    slots = [pltpu.VMEM((SLOTS, rt, feats), F32), pltpu.SemaphoreType.DMA((SLOTS,))]
    down_half = call(
        functools.partial(down_kernel, 0, cut, rt), "down_first", down_t, (core, act, act_far, g_near, g_far),
        flops=flops // 2, nbytes=wbytes, in_specs=[smem()] + [vmem()] * 4, out_specs=anywhere(), scratch=slots,
    )
    part_t = jax.ShapeDtypeStruct((half, feats), F32)
    down_grad, keep_in, send_in, bias_grad = call(
        functools.partial(down_in_kernel, cut, tiles, rt), "down_last_in",
        (down_t, part_t, part_t, jax.ShapeDtypeStruct((1, units), F32)),
        (core, act, act_far, g_near, g_far, pg, pg_far, w_up, down_half),
        flops=2 * flops, nbytes=2 * wbytes, in_specs=[smem()] + [vmem()] * 7 + [anywhere()],
        out_specs=(anywhere(), vmem(), vmem(), vmem()), scratch=slots, aliases={8: 0}, limit=24,
    )
    far_in = row_swap(send_in, 1)

    dt = divisor(feats, 128)
    dtiles = feats // dt
    dcut = dtiles // 2
    up_t = jax.ShapeDtypeStruct((feats, units), F32)
    slots = [pltpu.VMEM((SLOTS, dt, units), F32), pltpu.SemaphoreType.DMA((SLOTS,))]
    token_t = jax.ShapeDtypeStruct((8, 128), F32)
    up_half, wrote = call(
        functools.partial(up_kernel, 0, dcut, dt), "up_first", (up_t, token_t), (core, pg, pg_far, x_near, x_far),
        flops=flops // 2, nbytes=wbytes, in_specs=[smem()] + [vmem()] * 4, out_specs=(anywhere(), vmem()), scratch=slots,
    )
    share = call(sum_kernel, "share", part_t, (keep_in, far_in), nbytes=12 * half * feats, after=(wrote,))
    share = share.reshape(rows // 2, mine, feats)
    terms = [share[0]] + [row_swap(share[k // 2], k) for k in range(2, rows, 2)]
    up_grad, _ = call(
        functools.partial(up_kernel, dcut, dtiles, dt), "up_last", (up_t, token_t), (core, pg, pg_far, x_near, x_far, up_half),
        flops=flops // 2, nbytes=wbytes, in_specs=[smem()] + [vmem()] * 4 + [anywhere()], out_specs=(anywhere(), vmem()),
        scratch=slots, aliases={5: 0},
    )
    in_grad = tree_sum(terms).astype(BF16)
    return (in_grad, up_grad, bias_grad.reshape(units), down_grad)


def solution(mesh):
    in_specs = (P("row", "col"), P("row", "col"), P("col", "row"), P("row"), P("row", "col"))
    out_specs = (P("row", "col"), P("col", "row"), P("row"), P("row", "col"))
    body = functools.partial(on_device, mesh.shape["row"], mesh.shape["col"])
    return jax.shard_map(body, mesh=mesh, in_specs=in_specs, out_specs=out_specs, check_vma=False)
```

time: 209 us -> 63.5 us (0.30)
  blocking collectives: 76 us -> 0 us
  waiting for transfers between devices: 58.6 us -> 11.1 us
  matrix products: 37.7 us -> 0 us
  Pallas kernels: 0 us -> 33.5 us
  local copies, waits for them, and re-layouts: 18.7 us -> 0.05 us
  starting transfers between devices: 0.12 us -> 17.2 us
  between operations: 13.8 us -> 0.83 us
  other arithmetic: 3.21 us -> 0.66 us
    all_gather x4 -> x0, blocking collectives: 76 us -> none  [the longest x1 32.6 us: on_device(): lax.all_gather(out_grad, 'row', axis=0, tiled=True)]
    reduce_scatter x3 -> x0, waiting for transfers between devices: 58.5 us -> none  [the longest x1 34.3 us: on_device(): lax.psum_scatter(part_input, 'row', scatter_dimension=0, tiled=True)]
    dot_general x5 -> x0, matrix products: 37.7 us -> none  [the longest x1 8.26 us: on_device(): lax.dot_general(inputs_all, pre_grad, (((0,), (0,)), ((), ())), preferred...]
    pallas_call x0 -> x15, Pallas kernels: none -> 33.5 us  [call(): pl.pallas_call(body, out_shape=out_shape, in_specs=in_specs + [anywhere()...]
    unnamed x5 -> x2, local copies, waits for them, and re-layouts: 18.7 us -> 0.01 us
    ppermute x0 -> x15, starting transfers between devices: none -> 17.2 us  [the longest x8 13.3 us: row_swap(): return lax.ppermute(x, 'row', [(i, i ^ k) for i in range(rows)])]
    ppermute x0 -> x15, waiting for transfers between devices: none -> 11.1 us  [the longest x7 8.16 us: col_swap(): return lax.ppermute(x, 'col', [(i, i ^ k) for i in range(cols)])]
  transfers between devices with their start and end apart: 3 -> 15, of which waited for: 2 -> 5; matrix products, arithmetic and copies ran while one was open for 16% -> 0% of each run, Pallas kernels for 0% -> 37%
where the time goes in v2:
time: 63.5 us; the launch traced here: 63.3 us
  Pallas kernels  33.5 us (53%)
  starting transfers between devices  17.2 us (27%)
  waiting for transfers between devices  11.1 us (17%)
  between operations  0.83 us (1%)
  other arithmetic  0.66 us (1%)
    pallas_call x15, Pallas kernels, call(): pl.pallas_call(body, out_shape=out_shape, in_specs=in_specs + [anywhere()...  33.5 us
    ppermute x8, starting transfers between devices, row_swap(): return lax.ppermute(x, 'row', [(i, i ^ k) for i in range(rows)])  13.3 us
    ppermute x7, waiting for transfers between devices, col_swap(): return lax.ppermute(x, 'col', [(i, i ^ k) for i in range(cols)])  8.16 us
    ppermute x7, starting transfers between devices, col_swap(): return lax.ppermute(x, 'col', [(i, i ^ k) for i in range(cols)])  3.85 us
    ppermute x8, waiting for transfers between devices, row_swap(): return lax.ppermute(x, 'row', [(i, i ^ k) for i in range(rows)])  2.93 us
  transfers between devices with their start and end apart: 15, of which 5 were waited for; matrix products, arithmetic and copies ran while one was open for 0% of the time, Pallas kernels for 37%

profile of v2, /device:TPU:0, one launch (start us, length us, event | category | flops | bytes accessed | tf_op | source)
XLA Modules:
  0.0 63.3 jit_solution(13820313727628017067)
XLA Ops:
  0.6 0.8 %stack.21 = bf16[2,8,1536]{2,1,0:T(8,128)(2,1)S(1)} custom-call(bf16[8,1536]{1,0:T(8,128)(2,1)} %a_ref.1, bf16[8,1536]{1,0:T(8,128)(2,1)} %b_ref.1), custom_call_target="tpu_custom_call" | custom-call | tf_op jit(solution)/shard_map/stack/pallas_call | solution.py:38
  1.4 5.1 %collective-permute-start.2 = (bf16[2,8,1536]{2,1,0:T(8,128)(2,1)S(1)}, bf16[2,8,1536]{2,1,0:T(8,128)(2,1)S(1)}, u32[]{:S(2)}, u32[]{:S(2)}) collective-permute-start(bf16[2,8,1536]{2,1,0:T(8,128)(2,1)S(1)} %stack.21), channel_id=1, source_target_pairs={{0,24},{4,28},{8,16},{12,20},{16,8},{20,12},{24,0},{28,4},{1,25},{... | collective-permute-start | bytes 147464 | tf_op jit(solution)/shard_map/ppermute | solution.py:222
  6.5 0.6 %collective-permute-start = (bf16[2,8,1536]{2,1,0:T(8,128)(2,1)S(1)}, bf16[2,8,1536]{2,1,0:T(8,128)(2,1)S(1)}, u32[]{:S(2)}, u32[]{:S(2)}) collective-permute-start(bf16[2,8,1536]{2,1,0:T(8,128)(2,1)S(1)} %stack.21), channel_id=1, source_target_pairs={{0,8},{4,12},{8,0},{12,4},{16,24},{20,28},{24,16},{28,20},{1,9},{5... | collective-permute-start | bytes 147464 | tf_op jit(solution)/shard_map/ppermute | solution.py:222
  7.2 3.7 %load_up.1.refs_3_.w_ref = bf16[1536,3072]{1,0:T(8,128)(2,1)S(1)} custom-call(bf16[1536,3072]{1,0:T(8,128)(2,1)} %w_ref.1), custom_call_target="tpu_custom_call" | custom-call | tf_op jit(solution)/shard_map/load_up/pallas_call | solution.py:38
  10.9 0.6 %collective-permute-done.1 = bf16[2,8,1536]{2,1,0:T(8,128)(2,1)S(1)} collective-permute-done((bf16[2,8,1536]{2,1,0:T(8,128)(2,1)S(1)}, bf16[2,8,1536]{2,1,0:T(8,128)(2,1)S(1)}, u32[]{:S(2)}, u32[]{:S(2)}) %collective-permute-start.1) | collective-permute-done | bytes 49184 | tf_op jit(solution)/shard_map/ppermute | solution.py:222
  11.6 1.6 %collective-permute-start.3 = (bf16[2,32,1536]{2,1,0:T(8,128)(2,1)S(1)}, bf16[2,32,1536]{2,1,0:T(8,128)(2,1)S(1)}, u32[]{:S(2)}, u32[]{:S(2)}) collective-permute-start(bf16[2,32,1536]{2,1,0:T(8,128)(2,1)S(1)} %copy_bitcast_fusion.refs_1_), channel_id=1, source_target_pairs={{0,4},{4,0},{8,12},{12,8},{16,20},{20,16},{24,28},{28,24},{1,5},{5... | collective-permute-start | bytes 589832 | tf_op jit(solution)/shard_map/ppermute | solution.py:222
  13.1 3.7 %load_down.1.refs_4_.w_ref.refs_3_ = bf16[3072,1536]{1,0:T(8,128)(2,1)S(1)} custom-call(bf16[3072,1536]{1,0:T(8,128)(2,1)} %refs_0_.1, bf16[2,32,1536]{2,1,0:T(8,128)(2,1)S(1)} %copy_bitcast_fusion.refs_1_), custom_call_target="tpu_custom_call" | custom-call | tf_op jit(solution)/shard_map/load_down/pallas_call | solution.py:38
  17.4 1.7 %pre.1 = (f32[32,3072]{1,0:T(8,128)S(1)}, f32[32,3072]{1,0:T(8,128)S(1)}) custom-call(s32[1]{0:T(128)} %bitcast.refs_0_.core_ref, bf16[32,1536]{1,0:T(8,128)(2,1)S(1)} %get-tuple-element.40.refs_1_.near_ref, bf16[32,1536]{1,0:T(8,128)(2,1)S(1)} %get-tuple-element.38.refs_2_.far_ref, bf16[1536,3072]{1,0:T(8,128)(2,1)S(1)} %load_up.1.refs_3_.w_ref, ...), custom_call_target="tpu_custom_call" | custom-call | tf_op jit(solution)/shard_map/pre/pallas_call | solution.py:38
  19.3 1.5 %hid.2 = (f32[32,1536]{1,0:T(8,128)S(1)}, f32[32,1536]{1,0:T(8,128)S(1)}) custom-call(s32[1]{0:T(128)} %bitcast.refs_0_.core_ref, bf16[32,1536]{1,0:T(8,128)(2,1)S(1)} %get-tuple-element.39.near_ref.refs_1_, bf16[32,1536]{1,0:T(8,128)(2,1)S(1)} %get-tuple-element.37.far_ref.refs_2_, bf16[3072,1536]{1,0:T(8,128)(2,1)S(1)} %load_down.1.refs_4_.w_ref.refs_3_), custom_call_target="tpu_custom_call" | custom-call | tf_op jit(solution)/shard_map/hid/pallas_call | solution.py:38
  20.7 0.6 collective-permute-start.7
  21.3 1.4 %hid.3 = (f32[32,1536]{1,0:T(8,128)S(1)}, f32[32,1536]{1,0:T(8,128)S(1)}) custom-call(s32[1]{0:T(128)} %bitcast.refs_0_.core_ref, bf16[32,1536]{1,0:T(8,128)(2,1)S(1)} %get-tuple-element.39.near_ref.refs_1_, bf16[32,1536]{1,0:T(8,128)(2,1)S(1)} %get-tuple-element.37.far_ref.refs_2_, bf16[3072,1536]{1,0:T(8,128)(2,1)S(1)} %load_down.1.refs_4_.w_ref.refs_3_, ...), custom_call_target="tpu_custom_call" | custom-call | tf_op jit(solution)/shard_map/hid/pallas_call | solution.py:38
  22.9 1.6 %collective-permute-start.5 = (bf16[32,3072]{1,0:T(8,128)(2,1)S(1)}, bf16[32,3072]{1,0:T(8,128)(2,1)S(1)}, u32[]{:S(2)}, u32[]{:S(2)}) collective-permute-start(bf16[32,3072]{1,0:T(8,128)(2,1)S(1)} %add_pre.1.refs_0_.refs_4_), channel_id=1, source_target_pairs={{0,2},{1,3},{2,0},{3,1},{4,6},{5,7},{6,4},{7,5},{8,10},{9,11},{10,... | collective-permute-start | bytes 589832 | tf_op jit(solution)/shard_map/ppermute | solution.py:225
  24.5 1.4 %collective-permute-start.9 = (bf16[32,3072]{1,0:T(8,128)(2,1)S(1)}, bf16[32,3072]{1,0:T(8,128)(2,1)S(1)}, u32[]{:S(2)}, u32[]{:S(2)}) collective-permute-start(bf16[32,3072]{1,0:T(8,128)(2,1)S(1)} %add_hid.1.refs_0_), channel_id=1, source_target_pairs={{0,2},{1,3},{2,0},{3,1},{4,6},{5,7},{6,4},{7,5},{8,10},{9,11},{10,... | collective-permute-start | bytes 589832 | tf_op jit(solution)/shard_map/ppermute | solution.py:225
  25.9 4.7 %collective-permute-done.5.refs_1_ = bf16[32,3072]{1,0:T(8,128)(2,1)S(1)} collective-permute-done((bf16[32,3072]{1,0:T(8,128)(2,1)S(1)}, bf16[32,3072]{1,0:T(8,128)(2,1)S(1)}, u32[]{:S(2)}, u32[]{:S(2)}) %collective-permute-start.5) | collective-permute-done | bytes 196640 | tf_op jit(solution)/shard_map/ppermute | solution.py:225
  30.9 3.5 %collective-permute-done.9.refs_1_ = bf16[32,3072]{1,0:T(8,128)(2,1)S(1)} collective-permute-done((bf16[32,3072]{1,0:T(8,128)(2,1)S(1)}, bf16[32,3072]{1,0:T(8,128)(2,1)S(1)}, u32[]{:S(2)}, u32[]{:S(2)}) %collective-permute-start.9) | collective-permute-done | bytes 196640 | tf_op jit(solution)/shard_map/ppermute | solution.py:225
  34.5 4.1 %down_first.1._ = f32[3072,1536]{1,0:T(8,128)} custom-call(s32[1]{0:T(128)} %bitcast.refs_0_.core_ref, bf16[32,3072]{1,0:T(8,128)(2,1)S(1)} %get-tuple-element.21.h0_ref, bf16[32,3072]{1,0:T(8,128)(2,1)S(1)} %collective-permute-done.6.h1_ref, bf16[32,1536]{1,0:T(8,128)(2,1)S(1)} %get-tuple-element.39.near_ref.refs_1_, ...), custom_call_target="tpu_custom_call" | custom-call | tf_op jit(solution)/shard_map/down_first/pallas_call | solution.py:38
  38.6 7.5 %down_last_in.1 = (f32[3072,1536]{1,0:T(8,128)}, f32[32,1536]{1,0:T(8,128)S(1)}, f32[32,1536]{1,0:T(8,128)S(1)}, f32[1,3072]{1,0:T(1,128)}) custom-call(s32[1]{0:T(128)} %bitcast.refs_0_.core_ref, bf16[32,3072]{1,0:T(8,128)(2,1)S(1)} %get-tuple-element.21.h0_ref, ...), custom_call_target="tpu_custom_call", output_to_operand_aliasing={{0}: (8, {})} | custom-call | tf_op jit(solution)/shard_map/down_last_in/pallas_call | solution.py:38
  46.1 1.6 %collective-permute-start.11 = (f32[32,1536]{1,0:T(8,128)S(1)}, f32[32,1536]{1,0:T(8,128)S(1)}, u32[]{:S(2)}, u32[]{:S(2)}) collective-permute-start(f32[32,1536]{1,0:T(8,128)S(1)} %get-tuple-element.28), channel_id=1, source_target_pairs={{0,4},{4,0},{8,12},{12,8},{16,20},{20,16},{24,28},{28,24},{1,5},{5... | collective-permute-start | bytes 589832 | tf_op jit(solution)/shard_map/ppermute | solution.py:222
  47.7 4.1 %up_first.1 = (f32[1536,3072]{1,0:T(8,128)}, f32[8,128]{1,0:T(8,128)S(1)}) custom-call(s32[1]{0:T(128)} %bitcast.refs_0_.core_ref, bf16[32,3072]{1,0:T(8,128)(2,1)S(1)} %pre_grad.1.p0_ref, bf16[32,3072]{1,0:T(8,128)(2,1)S(1)} %collective-permute-done.10.p1_ref, bf16[32,1536]{1,0:T(8,128)(2,1)S(1)} %get-tuple-element.40.refs_1_.near_ref, ...), custom_call_target="tpu_custom_call" | custom-call | tf_op jit(solution)/shard_map/up_first/pallas_call | solution.py:38
  51.7 1.7 %collective-permute-done.11.refs_1_ = f32[32,1536]{1,0:T(8,128)S(1)} collective-permute-done((f32[32,1536]{1,0:T(8,128)S(1)}, f32[32,1536]{1,0:T(8,128)S(1)}, u32[]{:S(2)}, u32[]{:S(2)}) %collective-permute-start.11) | collective-permute-done | bytes 196640 | tf_op jit(solution)/shard_map/ppermute | solution.py:222
  53.5 3.2 %collective-permute-start.14 = (f32[8,1536]{1,0:T(8,128)S(1)}, f32[8,1536]{1,0:T(8,128)S(1)}, u32[]{:S(2)}, u32[]{:S(2)}) collective-permute-start(f32[8,1536]{1,0:T(8,128)S(1)} %get-tuple-element.34), channel_id=1, source_target_pairs={{0,24},{4,28},{8,16},{12,20},{16,8},{20,12},{24,0},{28,4},{1,25},{... | collective-permute-start | bytes 147464 | tf_op jit(solution)/shard_map/ppermute | solution.py:222
  56.8 1.2 %collective-permute-start.12 = (f32[8,1536]{1,0:T(8,128)S(1)}, f32[8,1536]{1,0:T(8,128)S(1)}, u32[]{:S(2)}, u32[]{:S(2)}) collective-permute-start(f32[8,1536]{1,0:T(8,128)S(1)} %get-tuple-element.36), channel_id=1, source_target_pairs={{0,8},{4,12},{8,0},{12,4},{16,24},{20,28},{24,16},{28,20},{1,9},{5... | collective-permute-start | bytes 147464 | tf_op jit(solution)/shard_map/ppermute | solution.py:222
  58.0 4.7 %up_last.1 = (f32[1536,3072]{1,0:T(8,128)}, f32[8,128]{1,0:T(8,128)}) custom-call(s32[1]{0:T(128)} %bitcast.refs_0_.core_ref, bf16[32,3072]{1,0:T(8,128)(2,1)S(1)} %pre_grad.1.p0_ref, bf16[32,3072]{1,0:T(8,128)(2,1)S(1)} %collective-permute-done.10.p1_ref, bf16[32,1536]{1,0:T(8,128)(2,1)S(1)} %get-tuple-element.40.refs_1_.near_ref, ...), custom_call_target="tpu_custom_call", output_to_operand_aliasing={{0}: (5, {})} | custom-call | tf_op jit(solution)/shard_map/up_last/pallas_call | solution.py:38
  62.7 0.6 fusion.1
  (30 shorter events, 1.4 us)
Async XLA Ops:
  1.4 9.5 %collective-permute-start.2 = (bf16[2,8,1536]{2,1,0:T(8,128)(2,1)S(1)}, bf16[2,8,1536]{2,1,0:T(8,128)(2,1)S(1)}, u32[]{:S(2)}, u32[]{:S(2)}) collective-permute-start(bf16[2,8,1536]{2,1,0:T(8,128)(2,1)S(1)} %stack.21), channel_id=1, source_target_pairs={{0,24},{4,28},{8,16},{12,20},{16,8},{20,12},{24,0},{28,4},{1,25},{... | collective-permute-start | bytes 147464 | tf_op jit(solution)/shard_map/ppermute | solution.py:222
  6.5 5.0 %collective-permute-start.1 = (bf16[2,8,1536]{2,1,0:T(8,128)(2,1)S(1)}, bf16[2,8,1536]{2,1,0:T(8,128)(2,1)S(1)}, u32[]{:S(2)}, u32[]{:S(2)}) collective-permute-start(bf16[2,8,1536]{2,1,0:T(8,128)(2,1)S(1)} %stack.21), channel_id=1, source_target_pairs={{0,16},{4,20},{8,24},{12,28},{16,0},{20,4},{24,8},{28,12},{1,17},{... | collective-permute-start | bytes 147464 | tf_op jit(solution)/shard_map/ppermute | solution.py:222
  6.5 5.0 %collective-permute-start = (bf16[2,8,1536]{2,1,0:T(8,128)(2,1)S(1)}, bf16[2,8,1536]{2,1,0:T(8,128)(2,1)S(1)}, u32[]{:S(2)}, u32[]{:S(2)}) collective-permute-start(bf16[2,8,1536]{2,1,0:T(8,128)(2,1)S(1)} %stack.21), channel_id=1, source_target_pairs={{0,8},{4,12},{8,0},{12,4},{16,24},{20,28},{24,16},{28,20},{1,9},{5... | collective-permute-start | bytes 147464 | tf_op jit(solution)/shard_map/ppermute | solution.py:222
  11.6 5.8 %collective-permute-start.3 = (bf16[2,32,1536]{2,1,0:T(8,128)(2,1)S(1)}, bf16[2,32,1536]{2,1,0:T(8,128)(2,1)S(1)}, u32[]{:S(2)}, u32[]{:S(2)}) collective-permute-start(bf16[2,32,1536]{2,1,0:T(8,128)(2,1)S(1)} %copy_bitcast_fusion.refs_1_), channel_id=1, source_target_pairs={{0,4},{4,0},{8,12},{12,8},{16,20},{20,16},{24,28},{28,24},{1,5},{5... | collective-permute-start | bytes 589832 | tf_op jit(solution)/shard_map/ppermute | solution.py:222
  17.4 8.5 %copy-start = (bf16[3072]{0:T(1024)(128)(2,1)S(1)}, bf16[3072]{0:T(1024)(128)(2,1)}, u32[]{:S(2)}) copy-start(bf16[3072]{0:T(1024)(128)(2,1)} %param.8) | copy-start | bytes 18436
  19.2 2.1 %collective-permute-start.4 = (f32[32,3072]{1,0:T(8,128)S(1)}, f32[32,3072]{1,0:T(8,128)S(1)}, u32[]{:S(2)}, u32[]{:S(2)}) collective-permute-start(f32[32,3072]{1,0:T(8,128)S(1)} %get-tuple-element.20), channel_id=1, source_target_pairs={{0,1},{1,0},{2,3},{3,2},{4,5},{5,4},{6,7},{7,6},{8,9},{9,8},{10,11... | collective-permute-start | bytes 1179656 | tf_op jit(solution)/shard_map/ppermute | solution.py:225
  20.7 3.7 %collective-permute-start.7 = (f32[32,1536]{1,0:T(8,128)S(1)}, f32[32,1536]{1,0:T(8,128)S(1)}, u32[]{:S(2)}, u32[]{:S(2)}) collective-permute-start(f32[32,1536]{1,0:T(8,128)S(1)} %get-tuple-element.24), channel_id=1, source_target_pairs={{0,1},{1,0},{2,3},{3,2},{4,5},{5,4},{6,7},{7,6},{8,9},{9,8},{10,11... | collective-permute-start | bytes 589832 | tf_op jit(solution)/shard_map/ppermute | solution.py:225
  22.8 1.7 %collective-permute-start.8 = (f32[32,1536]{1,0:T(8,128)S(1)}, f32[32,1536]{1,0:T(8,128)S(1)}, u32[]{:S(2)}, u32[]{:S(2)}) collective-permute-start(f32[32,1536]{1,0:T(8,128)S(1)} %get-tuple-element.25), channel_id=1, source_target_pairs={{0,1},{1,0},{2,3},{3,2},{4,5},{5,4},{6,7},{7,6},{8,9},{9,8},{10,11... | collective-permute-start | bytes 589832 | tf_op jit(solution)/shard_map/ppermute | solution.py:225
  22.9 7.8 %collective-permute-start.5 = (bf16[32,3072]{1,0:T(8,128)(2,1)S(1)}, bf16[32,3072]{1,0:T(8,128)(2,1)S(1)}, u32[]{:S(2)}, u32[]{:S(2)}) collective-permute-start(bf16[32,3072]{1,0:T(8,128)(2,1)S(1)} %add_pre.1.refs_0_.refs_4_), channel_id=1, source_target_pairs={{0,2},{1,3},{2,0},{3,1},{4,6},{5,7},{6,4},{7,5},{8,10},{9,11},{10,... | collective-permute-start | bytes 589832 | tf_op jit(solution)/shard_map/ppermute | solution.py:225
  24.5 9.9 %collective-permute-start.9 = (bf16[32,3072]{1,0:T(8,128)(2,1)S(1)}, bf16[32,3072]{1,0:T(8,128)(2,1)S(1)}, u32[]{:S(2)}, u32[]{:S(2)}) collective-permute-start(bf16[32,3072]{1,0:T(8,128)(2,1)S(1)} %add_hid.1.refs_0_), channel_id=1, source_target_pairs={{0,2},{1,3},{2,0},{3,1},{4,6},{5,7},{6,4},{7,5},{8,10},{9,11},{10,... | collective-permute-start | bytes 589832 | tf_op jit(solution)/shard_map/ppermute | solution.py:225
  30.9 3.7 %collective-permute-start.6 = (bf16[32,3072]{1,0:T(8,128)(2,1)S(1)}, bf16[32,3072]{1,0:T(8,128)(2,1)S(1)}, u32[]{:S(2)}, u32[]{:S(2)}) collective-permute-start(bf16[32,3072]{1,0:T(8,128)(2,1)S(1)} %get-tuple-element.21.h0_ref), channel_id=1, source_target_pairs={{0,1},{1,0},{2,3},{3,2},{4,5},{5,4},{6,7},{7,6},{8,9},{9,8},{10,11... | collective-permute-start | bytes 589832 | tf_op jit(solution)/shard_map/ppermute | solution.py:225
  34.5 4.2 %collective-permute-start.10 = (bf16[32,3072]{1,0:T(8,128)(2,1)S(1)}, bf16[32,3072]{1,0:T(8,128)(2,1)S(1)}, u32[]{:S(2)}, u32[]{:S(2)}) collective-permute-start(bf16[32,3072]{1,0:T(8,128)(2,1)S(1)} %pre_grad.1.p0_ref), channel_id=1, source_target_pairs={{0,1},{1,0},{2,3},{3,2},{4,5},{5,4},{6,7},{7,6},{8,9},{9,8},{10,11... | collective-permute-start | bytes 589832 | tf_op jit(solution)/shard_map/ppermute | solution.py:225
  46.1 7.4 %collective-permute-start.11 = (f32[32,1536]{1,0:T(8,128)S(1)}, f32[32,1536]{1,0:T(8,128)S(1)}, u32[]{:S(2)}, u32[]{:S(2)}) collective-permute-start(f32[32,1536]{1,0:T(8,128)S(1)} %get-tuple-element.28), channel_id=1, source_target_pairs={{0,4},{4,0},{8,12},{12,8},{16,20},{20,16},{24,28},{28,24},{1,5},{5... | collective-permute-start | bytes 589832 | tf_op jit(solution)/shard_map/ppermute | solution.py:222
  53.5 9.1 %collective-permute-start.14 = (f32[8,1536]{1,0:T(8,128)S(1)}, f32[8,1536]{1,0:T(8,128)S(1)}, u32[]{:S(2)}, u32[]{:S(2)}) collective-permute-start(f32[8,1536]{1,0:T(8,128)S(1)} %get-tuple-element.34), channel_id=1, source_target_pairs={{0,24},{4,28},{8,16},{12,20},{16,8},{20,12},{24,0},{28,4},{1,25},{... | collective-permute-start | bytes 147464 | tf_op jit(solution)/shard_map/ppermute | solution.py:222
  56.8 5.9 %collective-permute-start.13 = (f32[8,1536]{1,0:T(8,128)S(1)}, f32[8,1536]{1,0:T(8,128)S(1)}, u32[]{:S(2)}, u32[]{:S(2)}) collective-permute-start(f32[8,1536]{1,0:T(8,128)S(1)} %get-tuple-element.35), channel_id=1, source_target_pairs={{0,16},{4,20},{8,24},{12,28},{16,0},{20,4},{24,8},{28,12},{1,17},{... | collective-permute-start | bytes 147464 | tf_op jit(solution)/shard_map/ppermute | solution.py:222
  56.8 5.9 %collective-permute-start.12 = (f32[8,1536]{1,0:T(8,128)S(1)}, f32[8,1536]{1,0:T(8,128)S(1)}, u32[]{:S(2)}, u32[]{:S(2)}) collective-permute-start(f32[8,1536]{1,0:T(8,128)S(1)} %get-tuple-element.36), channel_id=1, source_target_pairs={{0,8},{4,12},{8,0},{12,4},{16,24},{20,28},{24,16},{28,20},{1,9},{5... | collective-permute-start | bytes 147464 | tf_op jit(solution)/shard_map/ppermute | solution.py:222

commit v3 on v2

v3 whole, which is shorter than its diff:
```python
import functools
import math

import jax
import jax.numpy as jnp
from jax import lax
from jax.experimental import pallas as pl
from jax.experimental.pallas import tpu as pltpu
from jax.sharding import PartitionSpec as P

F32 = jnp.float32
BF16 = jnp.bfloat16
MIB = 1024 * 1024
SLOTS = 4
EARLY = 16 * MIB
SCALE = 1000


def vmem():
    return pl.BlockSpec(memory_space=pltpu.VMEM)


def smem():
    return pl.BlockSpec(memory_space=pltpu.SMEM)


def anywhere():
    return pl.BlockSpec(memory_space=pl.ANY)


def call(kernel, name, out_shape, args, *, limit=16, in_specs=None, out_specs=None, scratch=(), aliases=None, after=(), cost=0):
    in_specs = in_specs if in_specs is not None else [vmem()] * len(args)
    body = kernel
    if after:
        n, m = len(args), len(args) + len(after)

        def body(*refs):
            kernel(*refs[:n], *refs[m:])

    return pl.pallas_call(
        body,
        out_shape=out_shape,
        in_specs=in_specs + [anywhere()] * len(after),
        out_specs=out_specs if out_specs is not None else jax.tree.map(lambda _: vmem(), out_shape),
        scratch_shapes=list(scratch),
        input_output_aliases=aliases or {},
        compiler_params=pltpu.CompilerParams(vmem_limit_bytes=limit * MIB),
        cost_estimate=pl.CostEstimate(flops=cost * SCALE, bytes_accessed=cost, transcendentals=0),
        name=name,
    )(*args, *after)


def tree_sum(terms):
    while len(terms) > 1:
        terms = [terms[i] + terms[i + 1] for i in range(0, len(terms), 2)]
    return terms[0]


def divisor(size, most):
    tile = min(size, most)
    while size % tile:
        tile -= 128
    return tile


def load_kernel(w_ref, o_ref, sem):
    copy = pltpu.make_async_copy(w_ref, o_ref, sem)
    copy.start()
    copy.wait()


def load(weight, name, limit, after):
    return call(
        load_kernel, name, pltpu.VMEM(weight.shape, weight.dtype), (weight,), limit=limit,
        in_specs=[anywhere()], out_specs=vmem(), scratch=[pltpu.SemaphoreType.DMA(())], after=after,
    )


def stack_kernel(a_ref, b_ref, o_ref, sems):
    copies = [pltpu.make_async_copy(r, o_ref.at[i], sems.at[i]) for i, r in enumerate((a_ref, b_ref))]
    for c in copies:
        c.start()
    for c in copies:
        c.wait()


def local_tokens(core, near_ref, far_ref):
    first = core == 0
    near, far = near_ref[...], far_ref[...]
    return jnp.concatenate([jnp.where(first, near, far), jnp.where(first, far, near)], axis=0)


def pre_kernel(core_ref, near_ref, far_ref, w_ref, keep_ref, send_ref):
    half, units = keep_ref.shape
    x = local_tokens(core_ref[0], near_ref, far_ref)
    tile = divisor(units, 512)
    for i in range(0, units, tile):
        out = jnp.dot(x, w_ref[:, i : i + tile], preferred_element_type=F32)
        keep_ref[:, i : i + tile] = out[:half]
        send_ref[:, i : i + tile] = out[half:]


def hid_kernel(start, core_ref, near_ref, far_ref, w_ref, keep_ref, send_ref):
    half, units = keep_ref.shape
    g = local_tokens(core_ref[0], near_ref, far_ref)
    tile = divisor(units, 512)
    for i in range(0, units, tile):
        w = w_ref[start + i : start + i + tile, :]
        out = lax.dot_general(w, g, (((1,), (1,)), ((), ())), preferred_element_type=F32).T
        keep_ref[:, i : i + tile] = out[:half]
        send_ref[:, i : i + tile] = out[half:]


def add_kernel(*refs):
    n, out_ref = len(refs) // 2, refs[-1]
    at = 0
    for a, b in zip(refs[:n], refs[n : 2 * n]):
        width = a.shape[1]
        out_ref[:, at : at + width] = (a[...] + b[...]).astype(BF16)
        at += width


def sum_kernel(a_ref, b_ref, out_ref):
    out_ref[...] = a_ref[...] + b_ref[...]


def act_kernel(*refs):
    parts, bias_ref, act_ref, slope_ref = refs[:-3], refs[-3], refs[-2], refs[-1]
    pre = tree_sum([r[...].astype(F32) for r in parts]) + bias_ref[...].astype(F32)
    cdf = 0.5 * (1.0 + lax.erf(pre * (1.0 / math.sqrt(2.0))))
    dens = jnp.exp(-0.5 * pre * pre) * (1.0 / math.sqrt(2.0 * math.pi))
    act_ref[...] = (pre * cdf).astype(BF16)
    slope_ref[...] = cdf + pre * dens


def grad_kernel(*refs):
    parts, slope_ref, out_ref = refs[:-2], refs[-2], refs[-1]
    hid = tree_sum([r[...].astype(F32) for r in parts])
    out_ref[...] = (hid * slope_ref[...]).astype(BF16)


def write_tiles(first, last, rows, make, out_ref, buf, sems):
    def copy(t):
        s = (t - first) % SLOTS
        return pltpu.make_async_copy(buf.at[s], out_ref.at[pl.ds(t * rows, rows), :], sems.at[s])

    for t in range(first, last):
        if t - first >= SLOTS:
            copy(t - SLOTS).wait()
        buf[(t - first) % SLOTS] = make(t * rows)
        copy(t).start()
    for t in range(max(first, last - SLOTS), last):
        copy(t).wait()


def outer(a, b):
    return lax.dot_general(a, b, (((0,), (0,)), ((), ())), preferred_element_type=F32)


def down_kernel(first, last, rows, core_ref, h0_ref, h1_ref, near_ref, far_ref, *refs):
    out_ref, done_ref, buf, sems = refs[-4:]
    done_ref[...] = jnp.zeros_like(done_ref)
    g = local_tokens(core_ref[0], near_ref, far_ref)

    def make(at):
        return outer(jnp.concatenate([h0_ref[:, at : at + rows], h1_ref[:, at : at + rows]], axis=0), g)

    write_tiles(first, last, rows, make, out_ref, buf, sems)


def in_kernel(core_ref, p0_ref, p1_ref, w_ref, keep_ref, send_ref, bias_ref):
    near_first = core_ref[0] == 0
    half = p0_ref.shape[0]
    p0, p1 = p0_ref[...], p1_ref[...]
    p = jnp.concatenate([jnp.where(near_first, p0, p1), jnp.where(near_first, p1, p0)], axis=0)
    feats = w_ref.shape[0]
    tile = divisor(feats, 512)
    for i in range(0, feats, tile):
        out = lax.dot_general(w_ref[i : i + tile, :], p, (((1,), (1,)), ((), ())), preferred_element_type=F32).T
        keep_ref[:, i : i + tile] = out[:half]
        send_ref[:, i : i + tile] = out[half:]
    own = jnp.sum(p0.astype(F32), axis=0, keepdims=True)
    bias_ref[...] = own + jnp.sum(p1.astype(F32), axis=0, keepdims=True)


def up_kernel(first, last, rows, core_ref, p0_ref, p1_ref, near_ref, far_ref, *refs):
    out_ref, done_ref, buf, sems = refs[-4:]
    done_ref[...] = jnp.zeros_like(done_ref)
    p = local_tokens(core_ref[0], p0_ref, p1_ref)

    def make(at):
        return outer(jnp.concatenate([near_ref[:, at : at + rows], far_ref[:, at : at + rows]], axis=0), p)

    write_tiles(first, last, rows, make, out_ref, buf, sems)


def on_device(rows, cols, normed, out_grad, up_weight, up_bias, down_weight):
    mine, feats = normed.shape
    units = up_weight.shape[1]
    half = mine * rows // 2
    core = lax.rem(lax.axis_index("col"), 2).astype(jnp.int32).reshape(1)

    def row_swap(x, k):
        return lax.ppermute(x, "row", [(i, i ^ k) for i in range(rows)])

    def col_swap(x, k):
        return lax.ppermute(x, "col", [(i, i ^ k) for i in range(cols)])

    blocks = rows // 2
    stack = call(
        stack_kernel, "stack", pltpu.VMEM((2, mine, feats), BF16), (normed, out_grad),
        in_specs=[anywhere()] * 2, out_specs=vmem(), scratch=[pltpu.SemaphoreType.DMA((2,))], limit=58,
    )
    near = jnp.stack([stack] + [row_swap(stack, k) for k in range(2, rows, 2)], axis=1)
    near = near.reshape(2, half, feats)
    far = row_swap(near, 1)
    up_weight = load(up_weight, "load_up", 44, ())
    down_weight = load(down_weight, "load_down", 38, (near,))
    x_near, x_far, g_near, g_far = near[0], far[0], near[1], far[1]

    keep_t = jax.ShapeDtypeStruct((half, units), F32)
    bf_t = jax.ShapeDtypeStruct((half, units), BF16)
    keep_pre, send_pre = call(
        pre_kernel, "pre", (keep_t, keep_t), (core, x_near, x_far, up_weight), in_specs=[smem()] + [vmem()] * 3,
        after=(down_weight,),
    )
    other_pre = col_swap(send_pre, 1)

    cut = units * 2 // 3 // 128 * 128

    def hid_piece(start, width, after):
        piece_t = jax.ShapeDtypeStruct((half, width), F32)
        return call(
            functools.partial(hid_kernel, start), "hid", (piece_t, piece_t), (core, g_near, g_far, down_weight),
            in_specs=[smem()] + [vmem()] * 3, after=after,
        )

    hids = [hid_piece(0, cut, ())]
    chip_pre = call(add_kernel, "add_pre", bf_t, (keep_pre, other_pre), after=(hids[0][1],), cost=EARLY)
    pre_parts = [chip_pre] + [col_swap(chip_pre, k) for k in range(2, cols, 2)]
    hids.append(hid_piece(cut, units - cut, (chip_pre,)))
    act, slope = call(act_kernel, "act", (bf_t, keep_t), (*pre_parts, up_bias.reshape(1, units)), cost=EARLY)
    act_far = col_swap(act, 1)
    others = [col_swap(send, 1) for _, send in hids]
    chip_hid = call(add_kernel, "add_hid", bf_t, (*[k for k, _ in hids], *others))
    hid_parts = [chip_hid] + [col_swap(chip_hid, k) for k in range(2, cols, 2)]
    pg = call(grad_kernel, "pre_grad", bf_t, (*hid_parts, slope), after=(act_far,))
    pg_far = col_swap(pg, 1)

    part_t = jax.ShapeDtypeStruct((half, feats), F32)
    token_t = jax.ShapeDtypeStruct((8, 128), F32)
    keep_in, send_in, bias_grad = call(
        in_kernel, "in_part", (part_t, part_t, jax.ShapeDtypeStruct((1, units), F32)), (core, pg, pg_far, up_weight),
        in_specs=[smem()] + [vmem()] * 3,
    )
    far_in = row_swap(send_in, 1)

    rt = divisor(units, 256)
    down_grad, wrote = call(
        functools.partial(down_kernel, 0, units // rt, rt), "down_grad",
        (jax.ShapeDtypeStruct((units, feats), F32), token_t), (core, act, act_far, g_near, g_far),
        in_specs=[smem()] + [vmem()] * 4, out_specs=(anywhere(), vmem()),
        scratch=[pltpu.VMEM((SLOTS, rt, feats), F32), pltpu.SemaphoreType.DMA((SLOTS,))], after=(send_in,),
    )
    share = call(sum_kernel, "share", part_t, (keep_in, far_in), after=(wrote,)).reshape(blocks, mine, feats)
    terms = [share[0]] + [row_swap(share[k // 2], k) for k in range(2, rows, 2)]

    dt = divisor(feats, 128)
    up_grad, _ = call(
        functools.partial(up_kernel, 0, feats // dt, dt), "up_grad",
        (jax.ShapeDtypeStruct((feats, units), F32), token_t), (core, pg, pg_far, x_near, x_far),
        in_specs=[smem()] + [vmem()] * 4, out_specs=(anywhere(), vmem()),
        scratch=[pltpu.VMEM((SLOTS, dt, units), F32), pltpu.SemaphoreType.DMA((SLOTS,))], after=(share,),
    )
    in_grad = tree_sum(terms).astype(BF16)
    return (in_grad, up_grad, bias_grad.reshape(units), down_grad)


def solution(mesh):
    in_specs = (P("row", "col"), P("row", "col"), P("col", "row"), P("row"), P("row", "col"))
    out_specs = (P("row", "col"), P("col", "row"), P("row"), P("row", "col"))
    body = functools.partial(on_device, mesh.shape["row"], mesh.shape["col"])
    return jax.shard_map(body, mesh=mesh, in_specs=in_specs, out_specs=out_specs, check_vma=False)
```

time: 63.5 us -> 60.3 us (0.950)
  Pallas kernels: 33.5 us -> 30.8 us
  starting transfers between devices: 17.2 us -> 16.2 us
    pallas_call x15 -> x14, Pallas kernels: 33.5 us -> 30.8 us  [call(): pl.pallas_call(body, out_shape=out_shape, in_specs=in_specs + [anywhere()...]
    ppermute x7, starting transfers between devices: 3.85 us -> 2.98 us  [col_swap(): return lax.ppermute(x, 'col', [(i, i ^ k) for i in range(cols)])]
    ppermute x7, waiting for transfers between devices: 8.16 us -> 8.89 us  [col_swap(): return lax.ppermute(x, 'col', [(i, i ^ k) for i in range(cols)])]
  transfers between devices with their start and end apart: 15 -> 15, of which waited for: 5 -> 6; matrix products, arithmetic and copies ran while one was open for 0% -> 0% of each run, Pallas kernels for 37% -> 42%
where the time goes in v3:
time: 60.3 us; the launch traced here: 60.1 us
  Pallas kernels  30.8 us (51%)
  starting transfers between devices  16.2 us (27%)
  waiting for transfers between devices  11.5 us (19%)
  between operations  0.85 us (1%)
  other arithmetic  0.66 us (1%)
    pallas_call x14, Pallas kernels, call(): pl.pallas_call(body, out_shape=out_shape, in_specs=in_specs + [anywhere()...  30.8 us
    ppermute x8, starting transfers between devices, row_swap(): return lax.ppermute(x, 'row', [(i, i ^ k) for i in range(rows)])  13.2 us
    ppermute x7, waiting for transfers between devices, col_swap(): return lax.ppermute(x, 'col', [(i, i ^ k) for i in range(cols)])  8.89 us
    ppermute x7, starting transfers between devices, col_swap(): return lax.ppermute(x, 'col', [(i, i ^ k) for i in range(cols)])  2.98 us
    ppermute x8, waiting for transfers between devices, row_swap(): return lax.ppermute(x, 'row', [(i, i ^ k) for i in range(rows)])  2.65 us
  transfers between devices with their start and end apart: 15, of which 6 were waited for; matrix products, arithmetic and copies ran while one was open for 0% of the time, Pallas kernels for 42%

profile of v3, /device:TPU:0, one launch (start us, length us, event | category | flops | bytes accessed | tf_op | source)
XLA Modules:
  0.0 60.1 jit_solution(3579014250041542756)
XLA Ops:
  0.6 0.8 %stack.21 = bf16[2,8,1536]{2,1,0:T(8,128)(2,1)S(1)} custom-call(bf16[8,1536]{1,0:T(8,128)(2,1)} %a_ref.1, bf16[8,1536]{1,0:T(8,128)(2,1)} %b_ref.1), custom_call_target="tpu_custom_call" | custom-call | tf_op jit(solution)/shard_map/stack/pallas_call | solution.py:40
  1.4 3.1 %collective-permute-start = (bf16[2,8,1536]{2,1,0:T(8,128)(2,1)S(1)}, bf16[2,8,1536]{2,1,0:T(8,128)(2,1)S(1)}, u32[]{:S(2)}, u32[]{:S(2)}) collective-permute-start(bf16[2,8,1536]{2,1,0:T(8,128)(2,1)S(1)} %stack.21), channel_id=1, source_target_pairs={{0,8},{4,12},{8,0},{12,4},{16,24},{20,28},{24,16},{28,20},{1,9},{5... | collective-permute-start | bytes 147464 | tf_op jit(solution)/shard_map/ppermute | solution.py:204
  4.5 2.6 %collective-permute-start.1 = (bf16[2,8,1536]{2,1,0:T(8,128)(2,1)S(1)}, bf16[2,8,1536]{2,1,0:T(8,128)(2,1)S(1)}, u32[]{:S(2)}, u32[]{:S(2)}) collective-permute-start(bf16[2,8,1536]{2,1,0:T(8,128)(2,1)S(1)} %stack.21), channel_id=1, source_target_pairs={{0,16},{4,20},{8,24},{12,28},{16,0},{20,4},{24,8},{28,12},{1,17},{... | collective-permute-start | bytes 147464 | tf_op jit(solution)/shard_map/ppermute | solution.py:204
  7.1 3.7 %load_up.1.refs_3_.w_ref = bf16[1536,3072]{1,0:T(8,128)(2,1)S(1)} custom-call(bf16[1536,3072]{1,0:T(8,128)(2,1)} %w_ref.1), custom_call_target="tpu_custom_call" | custom-call | tf_op jit(solution)/shard_map/load_up/pallas_call | solution.py:40
  10.8 2.2 %collective-permute-done.2 = bf16[2,8,1536]{2,1,0:T(8,128)(2,1)S(1)} collective-permute-done((bf16[2,8,1536]{2,1,0:T(8,128)(2,1)S(1)}, bf16[2,8,1536]{2,1,0:T(8,128)(2,1)S(1)}, u32[]{:S(2)}, u32[]{:S(2)}) %collective-permute-start.2) | collective-permute-done | bytes 49184 | tf_op jit(solution)/shard_map/ppermute | solution.py:204
  13.0 1.6 %collective-permute-start.3 = (bf16[2,32,1536]{2,1,0:T(8,128)(2,1)S(1)}, bf16[2,32,1536]{2,1,0:T(8,128)(2,1)S(1)}, u32[]{:S(2)}, u32[]{:S(2)}) collective-permute-start(bf16[2,32,1536]{2,1,0:T(8,128)(2,1)S(1)} %copy_bitcast_fusion.refs_1_), channel_id=1, source_target_pairs={{0,4},{4,0},{8,12},{12,8},{16,20},{20,16},{24,28},{28,24},{1,5},{5... | collective-permute-start | bytes 589832 | tf_op jit(solution)/shard_map/ppermute | solution.py:204
  14.6 3.7 %load_down.1.w_ref.refs_4_.refs_3_ = bf16[3072,1536]{1,0:T(8,128)(2,1)S(1)} custom-call(bf16[3072,1536]{1,0:T(8,128)(2,1)} %refs_0_.1, bf16[2,32,1536]{2,1,0:T(8,128)(2,1)S(1)} %copy_bitcast_fusion.refs_1_), custom_call_target="tpu_custom_call" | custom-call | tf_op jit(solution)/shard_map/load_down/pallas_call | solution.py:40
  18.8 1.7 %pre.1 = (f32[32,3072]{1,0:T(8,128)S(1)}, f32[32,3072]{1,0:T(8,128)S(1)}) custom-call(s32[1]{0:T(128)} %bitcast.core_ref.refs_0_, bf16[32,1536]{1,0:T(8,128)(2,1)S(1)} %get-tuple-element.37.refs_1_.refs_3_, bf16[32,1536]{1,0:T(8,128)(2,1)S(1)} %get-tuple-element.35.refs_2_.refs_4_, bf16[1536,3072]{1,0:T(8,128)(2,1)S(1)} %load_up.1.refs_3_.w_ref, ...), custom_call_target="tpu_custom_call" | custom-call | tf_op jit(solution)/shard_map/pre/pallas_call | solution.py:40
  20.6 1.9 %hid.2 = (f32[32,2048]{1,0:T(8,128)S(1)}, f32[32,2048]{1,0:T(8,128)S(1)}) custom-call(s32[1]{0:T(128)} %bitcast.core_ref.refs_0_, bf16[32,1536]{1,0:T(8,128)(2,1)S(1)} %get-tuple-element.38.near_ref.refs_1_.refs_3_, bf16[32,1536]{1,0:T(8,128)(2,1)S(1)} %get-tuple-element.36.far_ref.refs_2_.refs_4_, bf16[3072,1536]{1,0:T(8,128)(2,1)S(1)} %load_down.1.w_ref.refs_4_.refs_3_), custom_call_target="tpu_custom_call" | custom-call | tf_op jit(solution)/shard_map/hid/pallas_call | solution.py:40
  22.5 0.5 collective-permute-start.5
  23.1 1.6 %collective-permute-start.8 = (bf16[32,3072]{1,0:T(8,128)(2,1)S(1)}, bf16[32,3072]{1,0:T(8,128)(2,1)S(1)}, u32[]{:S(2)}, u32[]{:S(2)}) collective-permute-start(bf16[32,3072]{1,0:T(8,128)(2,1)S(1)} %add_pre.1.refs_4_.refs_0_), channel_id=1, source_target_pairs={{0,2},{1,3},{2,0},{3,1},{4,6},{5,7},{6,4},{7,5},{8,10},{9,11},{10,... | collective-permute-start | bytes 589832 | tf_op jit(solution)/shard_map/ppermute | solution.py:207
  24.7 1.0 %hid.3 = (f32[32,1024]{1,0:T(8,128)S(1)}, f32[32,1024]{1,0:T(8,128)S(1)}) custom-call(s32[1]{0:T(128)} %bitcast.core_ref.refs_0_, bf16[32,1536]{1,0:T(8,128)(2,1)S(1)} %get-tuple-element.38.near_ref.refs_1_.refs_3_, bf16[32,1536]{1,0:T(8,128)(2,1)S(1)} %get-tuple-element.36.far_ref.refs_2_.refs_4_, bf16[3072,1536]{1,0:T(8,128)(2,1)S(1)} %load_down.1.w_ref.refs_4_.refs_3_, ...), custom_call_target="tpu_custom_call" | custom-call | tf_op jit(solution)/shard_map/hid/pallas_call | solution.py:40
  25.8 1.3 %collective-permute-done.6.refs_3_ = f32[32,1024]{1,0:T(8,128)S(1)} collective-permute-done((f32[32,1024]{1,0:T(8,128)S(1)}, f32[32,1024]{1,0:T(8,128)S(1)}, u32[]{:S(2)}, u32[]{:S(2)}) %collective-permute-start.6) | collective-permute-done | bytes 131104 | tf_op jit(solution)/shard_map/ppermute | solution.py:207
  27.2 0.6 collective-permute-start.7
  27.8 2.2 %collective-permute-done.8.refs_1_ = bf16[32,3072]{1,0:T(8,128)(2,1)S(1)} collective-permute-done((bf16[32,3072]{1,0:T(8,128)(2,1)S(1)}, bf16[32,3072]{1,0:T(8,128)(2,1)S(1)}, u32[]{:S(2)}, u32[]{:S(2)}) %collective-permute-start.8) | collective-permute-done | bytes 196640 | tf_op jit(solution)/shard_map/ppermute | solution.py:207
  30.3 3.9 %collective-permute-done.7.refs_1_ = bf16[32,3072]{1,0:T(8,128)(2,1)S(1)} collective-permute-done((bf16[32,3072]{1,0:T(8,128)(2,1)S(1)}, bf16[32,3072]{1,0:T(8,128)(2,1)S(1)}, u32[]{:S(2)}, u32[]{:S(2)}) %collective-permute-start.7) | collective-permute-done | bytes 196640 | tf_op jit(solution)/shard_map/ppermute | solution.py:207
  34.4 1.4 %collective-permute-done.10.p1_ref.refs_2_ = bf16[32,3072]{1,0:T(8,128)(2,1)S(1)} collective-permute-done((bf16[32,3072]{1,0:T(8,128)(2,1)S(1)}, bf16[32,3072]{1,0:T(8,128)(2,1)S(1)}, u32[]{:S(2)}, u32[]{:S(2)}) %collective-permute-start.10) | collective-permute-done | bytes 196640 | tf_op jit(solution)/shard_map/ppermute | solution.py:207
  35.8 3.2 %in_part.1 = (f32[32,1536]{1,0:T(8,128)S(1)}, f32[32,1536]{1,0:T(8,128)S(1)}, f32[1,3072]{1,0:T(1,128)}) custom-call(s32[1]{0:T(128)} %bitcast.core_ref.refs_0_, bf16[32,3072]{1,0:T(8,128)(2,1)S(1)} %pre_grad.1.p0_ref.refs_1_, bf16[32,3072]{1,0:T(8,128)(2,1)S(1)} %collective-permute-done.10.p1_ref.refs_2_, bf16[1536,3072]{1,0:T(8,128)(2,1)S(1)} %load_up.1.refs_3_.w_ref), custom_call_target="tpu_custom_call" | custom-call | tf_op jit(solution)/shard_map/in_part/pallas_call | solution.py:40
  39.0 1.5 %collective-permute-start.11 = (f32[32,1536]{1,0:T(8,128)S(1)}, f32[32,1536]{1,0:T(8,128)S(1)}, u32[]{:S(2)}, u32[]{:S(2)}) collective-permute-start(f32[32,1536]{1,0:T(8,128)S(1)} %get-tuple-element.27.refs_5_), channel_id=1, source_target_pairs={{0,4},{4,0},{8,12},{12,8},{16,20},{20,16},{24,28},{28,24},{1,5},{5... | collective-permute-start | bytes 589832 | tf_op jit(solution)/shard_map/ppermute | solution.py:204
  40.5 6.9 %down_grad.1 = (f32[3072,1536]{1,0:T(8,128)}, f32[8,128]{1,0:T(8,128)S(1)}) custom-call(s32[1]{0:T(128)} %bitcast.core_ref.refs_0_, bf16[32,3072]{1,0:T(8,128)(2,1)S(1)} %get-tuple-element.25.refs_1_, bf16[32,3072]{1,0:T(8,128)(2,1)S(1)} %collective-permute-done.9.refs_3_.refs_2_, bf16[32,1536]{1,0:T(8,128)(2,1)S(1)} %get-tuple-element.38.near_ref.refs_1_.refs_3_, ...), custom_call_target="tpu_custom_call" | custom-call | tf_op jit(solution)/shard_map/down_grad/pallas_call | solution.py:40
  47.6 2.3 %collective-permute-start.13 = (f32[8,1536]{1,0:T(8,128)S(1)}, f32[8,1536]{1,0:T(8,128)S(1)}, u32[]{:S(2)}, u32[]{:S(2)}) collective-permute-start(f32[8,1536]{1,0:T(8,128)S(1)} %get-tuple-element.33), channel_id=1, source_target_pairs={{0,16},{4,20},{8,24},{12,28},{16,0},{20,4},{24,8},{28,12},{1,17},{... | collective-permute-start | bytes 147464 | tf_op jit(solution)/shard_map/ppermute | solution.py:204
  49.9 2.0 %collective-permute-start.14 = (f32[8,1536]{1,0:T(8,128)S(1)}, f32[8,1536]{1,0:T(8,128)S(1)}, u32[]{:S(2)}, u32[]{:S(2)}) collective-permute-start(f32[8,1536]{1,0:T(8,128)S(1)} %get-tuple-element.32), channel_id=1, source_target_pairs={{0,24},{4,28},{8,16},{12,20},{16,8},{20,12},{24,0},{28,4},{1,25},{... | collective-permute-start | bytes 147464 | tf_op jit(solution)/shard_map/ppermute | solution.py:204
  51.9 7.5 %up_grad.1 = (f32[1536,3072]{1,0:T(8,128)}, f32[8,128]{1,0:T(8,128)}) custom-call(s32[1]{0:T(128)} %bitcast.core_ref.refs_0_, bf16[32,3072]{1,0:T(8,128)(2,1)S(1)} %pre_grad.1.p0_ref.refs_1_, bf16[32,3072]{1,0:T(8,128)(2,1)S(1)} %collective-permute-done.10.p1_ref.refs_2_, bf16[32,1536]{1,0:T(8,128)(2,1)S(1)} %get-tuple-element.37.refs_1_.refs_3_, ...), custom_call_target="tpu_custom_call" | custom-call | tf_op jit(solution)/shard_map/up_grad/pallas_call | solution.py:40
  59.5 0.6 %fusion.1 = bf16[8,1536]{1,0:T(8,128)(2,1)} fusion(f32[8,1536]{1,0:T(8,128)S(1)} %collective-permute-done.12, f32[32,1536]{1,0:T(8,128)S(1)} %share.1, f32[8,1536]{1,0:T(8,128)S(1)} %collective-permute-done.13, f32[8,1536]{1,0:T(8,128)S(1)} %collective-permute-done.14), kind=kLoop, calls=%fused_computation.8 | loop fusion | flops 49152 | bytes 221184 | tf_op jit(solution)/shard_map/convert_element_type | solution.py:275
  (29 shorter events, 1.4 us)
Async XLA Ops:
  1.4 9.4 %collective-permute-start = (bf16[2,8,1536]{2,1,0:T(8,128)(2,1)S(1)}, bf16[2,8,1536]{2,1,0:T(8,128)(2,1)S(1)}, u32[]{:S(2)}, u32[]{:S(2)}) collective-permute-start(bf16[2,8,1536]{2,1,0:T(8,128)(2,1)S(1)} %stack.21), channel_id=1, source_target_pairs={{0,8},{4,12},{8,0},{12,4},{16,24},{20,28},{24,16},{28,20},{1,9},{5... | collective-permute-start | bytes 147464 | tf_op jit(solution)/shard_map/ppermute | solution.py:204
  4.5 6.3 %collective-permute-start.1 = (bf16[2,8,1536]{2,1,0:T(8,128)(2,1)S(1)}, bf16[2,8,1536]{2,1,0:T(8,128)(2,1)S(1)}, u32[]{:S(2)}, u32[]{:S(2)}) collective-permute-start(bf16[2,8,1536]{2,1,0:T(8,128)(2,1)S(1)} %stack.21), channel_id=1, source_target_pairs={{0,16},{4,20},{8,24},{12,28},{16,0},{20,4},{24,8},{28,12},{1,17},{... | collective-permute-start | bytes 147464 | tf_op jit(solution)/shard_map/ppermute | solution.py:204
  7.1 5.9 %collective-permute-start.2 = (bf16[2,8,1536]{2,1,0:T(8,128)(2,1)S(1)}, bf16[2,8,1536]{2,1,0:T(8,128)(2,1)S(1)}, u32[]{:S(2)}, u32[]{:S(2)}) collective-permute-start(bf16[2,8,1536]{2,1,0:T(8,128)(2,1)S(1)} %stack.21), channel_id=1, source_target_pairs={{0,24},{4,28},{8,16},{12,20},{16,8},{20,12},{24,0},{28,4},{1,25},{... | collective-permute-start | bytes 147464 | tf_op jit(solution)/shard_map/ppermute | solution.py:204
  13.0 5.7 %collective-permute-start.3 = (bf16[2,32,1536]{2,1,0:T(8,128)(2,1)S(1)}, bf16[2,32,1536]{2,1,0:T(8,128)(2,1)S(1)}, u32[]{:S(2)}, u32[]{:S(2)}) collective-permute-start(bf16[2,32,1536]{2,1,0:T(8,128)(2,1)S(1)} %copy_bitcast_fusion.refs_1_), channel_id=1, source_target_pairs={{0,4},{4,0},{8,12},{12,8},{16,20},{20,16},{24,28},{28,24},{1,5},{5... | collective-permute-start | bytes 589832 | tf_op jit(solution)/shard_map/ppermute | solution.py:204
  20.5 2.5 %collective-permute-start.4 = (f32[32,3072]{1,0:T(8,128)S(1)}, f32[32,3072]{1,0:T(8,128)S(1)}, u32[]{:S(2)}, u32[]{:S(2)}) collective-permute-start(f32[32,3072]{1,0:T(8,128)S(1)} %get-tuple-element.20), channel_id=1, source_target_pairs={{0,1},{1,0},{2,3},{3,2},{4,5},{5,4},{6,7},{7,6},{8,9},{9,8},{10,11... | collective-permute-start | bytes 1179656 | tf_op jit(solution)/shard_map/ppermute | solution.py:207
  22.5 3.4 %collective-permute-start.5 = (f32[32,2048]{1,0:T(8,128)S(1)}, f32[32,2048]{1,0:T(8,128)S(1)}, u32[]{:S(2)}, u32[]{:S(2)}) collective-permute-start(f32[32,2048]{1,0:T(8,128)S(1)} %get-tuple-element.21.refs_2_), channel_id=1, source_target_pairs={{0,1},{1,0},{2,3},{3,2},{4,5},{5,4},{6,7},{7,6},{8,9},{9,8},{10,11... | collective-permute-start | bytes 786440 | tf_op jit(solution)/shard_map/ppermute | solution.py:207
  23.1 2.7 %copy-start = (bf16[3072]{0:T(1024)(128)(2,1)S(1)}, bf16[3072]{0:T(1024)(128)(2,1)}, u32[]{:S(2)}) copy-start(bf16[3072]{0:T(1024)(128)(2,1)} %param.8) | copy-start | bytes 18436
  23.1 6.9 %collective-permute-start.8 = (bf16[32,3072]{1,0:T(8,128)(2,1)S(1)}, bf16[32,3072]{1,0:T(8,128)(2,1)S(1)}, u32[]{:S(2)}, u32[]{:S(2)}) collective-permute-start(bf16[32,3072]{1,0:T(8,128)(2,1)S(1)} %add_pre.1.refs_4_.refs_0_), channel_id=1, source_target_pairs={{0,2},{1,3},{2,0},{3,1},{4,6},{5,7},{6,4},{7,5},{8,10},{9,11},{10,... | collective-permute-start | bytes 589832 | tf_op jit(solution)/shard_map/ppermute | solution.py:207
  25.7 1.4 %collective-permute-start.6 = (f32[32,1024]{1,0:T(8,128)S(1)}, f32[32,1024]{1,0:T(8,128)S(1)}, u32[]{:S(2)}, u32[]{:S(2)}) collective-permute-start(f32[32,1024]{1,0:T(8,128)S(1)} %get-tuple-element.23), channel_id=1, source_target_pairs={{0,1},{1,0},{2,3},{3,2},{4,5},{5,4},{6,7},{7,6},{8,9},{9,8},{10,11... | collective-permute-start | bytes 393224 | tf_op jit(solution)/shard_map/ppermute | solution.py:207
  27.2 7.0 %collective-permute-start.7 = (bf16[32,3072]{1,0:T(8,128)(2,1)S(1)}, bf16[32,3072]{1,0:T(8,128)(2,1)S(1)}, u32[]{:S(2)}, u32[]{:S(2)}) collective-permute-start(bf16[32,3072]{1,0:T(8,128)(2,1)S(1)} %add_hid.1.refs_0_), channel_id=1, source_target_pairs={{0,2},{1,3},{2,0},{3,1},{4,6},{5,7},{6,4},{7,5},{8,10},{9,11},{10,... | collective-permute-start | bytes 589832 | tf_op jit(solution)/shard_map/ppermute | solution.py:207
  30.2 4.0 %collective-permute-start.9 = (bf16[32,3072]{1,0:T(8,128)(2,1)S(1)}, bf16[32,3072]{1,0:T(8,128)(2,1)S(1)}, u32[]{:S(2)}, u32[]{:S(2)}) collective-permute-start(bf16[32,3072]{1,0:T(8,128)(2,1)S(1)} %get-tuple-element.25.refs_1_), channel_id=1, source_target_pairs={{0,1},{1,0},{2,3},{3,2},{4,5},{5,4},{6,7},{7,6},{8,9},{9,8},{10,11... | collective-permute-start | bytes 589832 | tf_op jit(solution)/shard_map/ppermute | solution.py:207
  34.3 1.5 %collective-permute-start.10 = (bf16[32,3072]{1,0:T(8,128)(2,1)S(1)}, bf16[32,3072]{1,0:T(8,128)(2,1)S(1)}, u32[]{:S(2)}, u32[]{:S(2)}) collective-permute-start(bf16[32,3072]{1,0:T(8,128)(2,1)S(1)} %pre_grad.1.p0_ref.refs_1_), channel_id=1, source_target_pairs={{0,1},{1,0},{2,3},{3,2},{4,5},{5,4},{6,7},{7,6},{8,9},{9,8},{10,11... | collective-permute-start | bytes 589832 | tf_op jit(solution)/shard_map/ppermute | solution.py:207
  39.0 8.4 %collective-permute-start.11 = (f32[32,1536]{1,0:T(8,128)S(1)}, f32[32,1536]{1,0:T(8,128)S(1)}, u32[]{:S(2)}, u32[]{:S(2)}) collective-permute-start(f32[32,1536]{1,0:T(8,128)S(1)} %get-tuple-element.27.refs_5_), channel_id=1, source_target_pairs={{0,4},{4,0},{8,12},{12,8},{16,20},{20,16},{24,28},{28,24},{1,5},{5... | collective-permute-start | bytes 589832 | tf_op jit(solution)/shard_map/ppermute | solution.py:204
  47.5 12.0 %collective-permute-start.12 = (f32[8,1536]{1,0:T(8,128)S(1)}, f32[8,1536]{1,0:T(8,128)S(1)}, u32[]{:S(2)}, u32[]{:S(2)}) collective-permute-start(f32[8,1536]{1,0:T(8,128)S(1)} %get-tuple-element.34), channel_id=1, source_target_pairs={{0,8},{4,12},{8,0},{12,4},{16,24},{20,28},{24,16},{28,20},{1,9},{5... | collective-permute-start | bytes 147464 | tf_op jit(solution)/shard_map/ppermute | solution.py:204
  47.6 11.9 %collective-permute-start.13 = (f32[8,1536]{1,0:T(8,128)S(1)}, f32[8,1536]{1,0:T(8,128)S(1)}, u32[]{:S(2)}, u32[]{:S(2)}) collective-permute-start(f32[8,1536]{1,0:T(8,128)S(1)} %get-tuple-element.33), channel_id=1, source_target_pairs={{0,16},{4,20},{8,24},{12,28},{16,0},{20,4},{24,8},{28,12},{1,17},{... | collective-permute-start | bytes 147464 | tf_op jit(solution)/shard_map/ppermute | solution.py:204
  49.9 9.5 %collective-permute-start.14 = (f32[8,1536]{1,0:T(8,128)S(1)}, f32[8,1536]{1,0:T(8,128)S(1)}, u32[]{:S(2)}, u32[]{:S(2)}) collective-permute-start(f32[8,1536]{1,0:T(8,128)S(1)} %get-tuple-element.32), channel_id=1, source_target_pairs={{0,24},{4,28},{8,16},{12,20},{16,8},{20,12},{24,0},{28,4},{1,25},{... | collective-permute-start | bytes 147464 | tf_op jit(solution)/shard_map/ppermute | solution.py:204

commit v4 on v3

--- a/solution.py
+++ b/solution.py
@@ -12,6 +12,7 @@
 BF16 = jnp.bfloat16
 MIB = 1024 * 1024
 SLOTS = 4
+DOWN_EARLY = 8
 EARLY = 16 * MIB
 SCALE = 1000
 
@@ -121,7 +122,7 @@
 
 
 def sum_kernel(a_ref, b_ref, out_ref):
-    out_ref[...] = a_ref[...] + b_ref[...]
+    out_ref[...] = a_ref[...] + b_ref[...].astype(F32)
 
 
 def act_kernel(*refs):
@@ -168,30 +169,42 @@
     write_tiles(first, last, rows, make, out_ref, buf, sems)
 
 
-def in_kernel(core_ref, p0_ref, p1_ref, w_ref, keep_ref, send_ref, bias_ref):
+def down_in_kernel(
+    last, rows, core_ref, p0_ref, p1_ref, w_ref, h0_ref, h1_ref, near_ref, far_ref, out_ref, keep_ref, send_ref, bias_ref, p_ref,
+    buf, sems,
+):
     near_first = core_ref[0] == 0
+    g = local_tokens(core_ref[0], near_ref, far_ref)
+    copies = [
+        pltpu.make_async_copy(buf.at[t], out_ref.at[pl.ds(t * rows, rows), :], sems.at[t]) for t in range(last)
+    ]
+    for t in range(last):
+        at = t * rows
+        buf[t] = outer(jnp.concatenate([h0_ref[:, at : at + rows], h1_ref[:, at : at + rows]], axis=0), g)
+        copies[t].start()
     half = p0_ref.shape[0]
     p0, p1 = p0_ref[...], p1_ref[...]
     p = jnp.concatenate([jnp.where(near_first, p0, p1), jnp.where(near_first, p1, p0)], axis=0)
+    p_ref[...] = p
     feats = w_ref.shape[0]
     tile = divisor(feats, 512)
     for i in range(0, feats, tile):
         out = lax.dot_general(w_ref[i : i + tile, :], p, (((1,), (1,)), ((), ())), preferred_element_type=F32).T
         keep_ref[:, i : i + tile] = out[:half]
-        send_ref[:, i : i + tile] = out[half:]
+        send_ref[:, i : i + tile] = out[half:].astype(BF16)
     own = jnp.sum(p0.astype(F32), axis=0, keepdims=True)
     bias_ref[...] = own + jnp.sum(p1.astype(F32), axis=0, keepdims=True)
-
-
-def up_kernel(first, last, rows, core_ref, p0_ref, p1_ref, near_ref, far_ref, *refs):
-    out_ref, done_ref, buf, sems = refs[-4:]
-    done_ref[...] = jnp.zeros_like(done_ref)
-    p = local_tokens(core_ref[0], p0_ref, p1_ref)
+    for t in range(last):
+        copies[t].wait()
+
+
+def up_kernel(rows, p_ref, near_ref, far_ref, out_ref, buf, sems):
+    p = p_ref[...]
 
     def make(at):
         return outer(jnp.concatenate([near_ref[:, at : at + rows], far_ref[:, at : at + rows]], axis=0), p)
 
-    write_tiles(first, last, rows, make, out_ref, buf, sems)
+    write_tiles(0, out_ref.shape[0] // rows, rows, make, out_ref, buf, sems)
 
 
 def on_device(rows, cols, normed, out_grad, up_weight, up_bias, down_weight):
@@ -247,29 +260,34 @@
     pg = call(grad_kernel, "pre_grad", bf_t, (*hid_parts, slope), after=(act_far,))
     pg_far = col_swap(pg, 1)
 
+    rt = divisor(units, 256)
+    tiles = units // rt
+    early = max(1, tiles * DOWN_EARLY // 12)
     part_t = jax.ShapeDtypeStruct((half, feats), F32)
     token_t = jax.ShapeDtypeStruct((8, 128), F32)
-    keep_in, send_in, bias_grad = call(
-        in_kernel, "in_part", (part_t, part_t, jax.ShapeDtypeStruct((1, units), F32)), (core, pg, pg_far, up_weight),
-        in_specs=[smem()] + [vmem()] * 3,
+    down_t = jax.ShapeDtypeStruct((units, feats), F32)
+    down_early, keep_in, send_in, bias_grad, pg_all = call(
+        functools.partial(down_in_kernel, early, rt), "down_in",
+        (down_t, part_t, jax.ShapeDtypeStruct((half, feats), BF16), jax.ShapeDtypeStruct((1, units), F32), jax.ShapeDtypeStruct((2 * half, units), BF16)),
+        (core, pg, pg_far, up_weight, act, act_far, g_near, g_far), in_specs=[smem()] + [vmem()] * 7,
+        out_specs=(anywhere(),) + (vmem(),) * 4, limit=24,
+        scratch=[pltpu.VMEM((early, rt, feats), F32), pltpu.SemaphoreType.DMA((early,))],
     )
     far_in = row_swap(send_in, 1)
 
-    rt = divisor(units, 256)
     down_grad, wrote = call(
-        functools.partial(down_kernel, 0, units // rt, rt), "down_grad",
-        (jax.ShapeDtypeStruct((units, feats), F32), token_t), (core, act, act_far, g_near, g_far),
-        in_specs=[smem()] + [vmem()] * 4, out_specs=(anywhere(), vmem()),
-        scratch=[pltpu.VMEM((SLOTS, rt, feats), F32), pltpu.SemaphoreType.DMA((SLOTS,))], after=(send_in,),
+        functools.partial(down_kernel, early, tiles, rt), "down_grad", (down_t, token_t),
+        (core, act, act_far, g_near, g_far, down_early), in_specs=[smem()] + [vmem()] * 4 + [anywhere()],
+        out_specs=(anywhere(), vmem()), scratch=[pltpu.VMEM((SLOTS, rt, feats), F32), pltpu.SemaphoreType.DMA((SLOTS,))],
+        aliases={5: 0}, after=(send_in,),
     )
     share = call(sum_kernel, "share", part_t, (keep_in, far_in), after=(wrote,)).reshape(blocks, mine, feats)
     terms = [share[0]] + [row_swap(share[k // 2], k) for k in range(2, rows, 2)]
 
     dt = divisor(feats, 128)
-    up_grad, _ = call(
-        functools.partial(up_kernel, 0, feats // dt, dt), "up_grad",
-        (jax.ShapeDtypeStruct((feats, units), F32), token_t), (core, pg, pg_far, x_near, x_far),
-        in_specs=[smem()] + [vmem()] * 4, out_specs=(anywhere(), vmem()),
+    up_grad = call(
+        functools.partial(up_kernel, dt), "up_grad", jax.ShapeDtypeStruct((feats, units), F32), (pg_all, x_near, x_far),
+        in_specs=[vmem()] * 3, out_specs=anywhere(),
         scratch=[pltpu.VMEM((SLOTS, dt, units), F32), pltpu.SemaphoreType.DMA((SLOTS,))], after=(share,),
     )
     in_grad = tree_sum(terms).astype(BF16)

time: 60.3 us -> 58.6 us (0.972)
  Pallas kernels: 30.8 us -> 28.8 us
    pallas_call x14, Pallas kernels: 30.8 us -> 28.8 us  [call(): pl.pallas_call(body, out_shape=out_shape, in_specs=in_specs + [anywhere()...]
  transfers between devices with their start and end apart: 15 -> 15, of which waited for: 6 -> 7; matrix products, arithmetic and copies ran while one was open for 0% -> 0% of each run, Pallas kernels for 42% -> 35%
where the time goes in v4:
time: 58.6 us; the launch traced here: 58.4 us
  Pallas kernels  28.8 us (49%)
  starting transfers between devices  16.2 us (28%)
  waiting for transfers between devices  11.7 us (20%)
  between operations  0.85 us (1%)
  other arithmetic  0.66 us (1%)
    pallas_call x14, Pallas kernels, call(): pl.pallas_call(body, out_shape=out_shape, in_specs=in_specs + [anywhere()...  28.8 us
    ppermute x8, starting transfers between devices, row_swap(): return lax.ppermute(x, 'row', [(i, i ^ k) for i in range(rows)])  13.2 us
    ppermute x7, waiting for transfers between devices, col_swap(): return lax.ppermute(x, 'col', [(i, i ^ k) for i in range(cols)])  8.89 us
    ppermute x7, starting transfers between devices, col_swap(): return lax.ppermute(x, 'col', [(i, i ^ k) for i in range(cols)])  2.99 us
    ppermute x8, waiting for transfers between devices, row_swap(): return lax.ppermute(x, 'row', [(i, i ^ k) for i in range(rows)])  2.86 us
  transfers between devices with their start and end apart: 15, of which 7 were waited for; matrix products, arithmetic and copies ran while one was open for 0% of the time, Pallas kernels for 35%

profile of v4, /device:TPU:0, one launch (start us, length us, event | category | flops | bytes accessed | tf_op | source)
XLA Modules:
  0.0 58.4 jit_solution(6085403989020465721)
XLA Ops:
  0.6 0.8 %stack.21 = bf16[2,8,1536]{2,1,0:T(8,128)(2,1)S(1)} custom-call(bf16[8,1536]{1,0:T(8,128)(2,1)} %a_ref.1, bf16[8,1536]{1,0:T(8,128)(2,1)} %b_ref.1), custom_call_target="tpu_custom_call" | custom-call | tf_op jit(solution)/shard_map/stack/pallas_call | solution.py:41
  1.4 3.1 %collective-permute-start = (bf16[2,8,1536]{2,1,0:T(8,128)(2,1)S(1)}, bf16[2,8,1536]{2,1,0:T(8,128)(2,1)S(1)}, u32[]{:S(2)}, u32[]{:S(2)}) collective-permute-start(bf16[2,8,1536]{2,1,0:T(8,128)(2,1)S(1)} %stack.21), channel_id=1, source_target_pairs={{0,8},{4,12},{8,0},{12,4},{16,24},{20,28},{24,16},{28,20},{1,9},{5... | collective-permute-start | bytes 147464 | tf_op jit(solution)/shard_map/ppermute | solution.py:217
  4.5 2.6 %collective-permute-start.1 = (bf16[2,8,1536]{2,1,0:T(8,128)(2,1)S(1)}, bf16[2,8,1536]{2,1,0:T(8,128)(2,1)S(1)}, u32[]{:S(2)}, u32[]{:S(2)}) collective-permute-start(bf16[2,8,1536]{2,1,0:T(8,128)(2,1)S(1)} %stack.21), channel_id=1, source_target_pairs={{0,16},{4,20},{8,24},{12,28},{16,0},{20,4},{24,8},{28,12},{1,17},{... | collective-permute-start | bytes 147464 | tf_op jit(solution)/shard_map/ppermute | solution.py:217
  7.1 3.7 %load_up.1.refs_3_.w_ref = bf16[1536,3072]{1,0:T(8,128)(2,1)S(1)} custom-call(bf16[1536,3072]{1,0:T(8,128)(2,1)} %w_ref.1), custom_call_target="tpu_custom_call" | custom-call | tf_op jit(solution)/shard_map/load_up/pallas_call | solution.py:41
  10.8 2.2 %collective-permute-done.2 = bf16[2,8,1536]{2,1,0:T(8,128)(2,1)S(1)} collective-permute-done((bf16[2,8,1536]{2,1,0:T(8,128)(2,1)S(1)}, bf16[2,8,1536]{2,1,0:T(8,128)(2,1)S(1)}, u32[]{:S(2)}, u32[]{:S(2)}) %collective-permute-start.2) | collective-permute-done | bytes 49184 | tf_op jit(solution)/shard_map/ppermute | solution.py:217
  13.0 1.6 %collective-permute-start.3 = (bf16[2,32,1536]{2,1,0:T(8,128)(2,1)S(1)}, bf16[2,32,1536]{2,1,0:T(8,128)(2,1)S(1)}, u32[]{:S(2)}, u32[]{:S(2)}) collective-permute-start(bf16[2,32,1536]{2,1,0:T(8,128)(2,1)S(1)} %copy_bitcast_fusion.refs_1_), channel_id=1, source_target_pairs={{0,4},{4,0},{8,12},{12,8},{16,20},{20,16},{24,28},{28,24},{1,5},{5... | collective-permute-start | bytes 589832 | tf_op jit(solution)/shard_map/ppermute | solution.py:217
  14.6 3.7 %load_down.1.w_ref.refs_4_.refs_3_ = bf16[3072,1536]{1,0:T(8,128)(2,1)S(1)} custom-call(bf16[3072,1536]{1,0:T(8,128)(2,1)} %refs_0_.1, bf16[2,32,1536]{2,1,0:T(8,128)(2,1)S(1)} %copy_bitcast_fusion.refs_1_), custom_call_target="tpu_custom_call" | custom-call | tf_op jit(solution)/shard_map/load_down/pallas_call | solution.py:41
  18.8 1.7 %pre.1 = (f32[32,3072]{1,0:T(8,128)S(1)}, f32[32,3072]{1,0:T(8,128)S(1)}) custom-call(s32[1]{0:T(128)} %bitcast.core_ref.refs_0_, bf16[32,1536]{1,0:T(8,128)(2,1)S(1)} %get-tuple-element.39.refs_1_, bf16[32,1536]{1,0:T(8,128)(2,1)S(1)} %get-tuple-element.37.refs_2_, bf16[1536,3072]{1,0:T(8,128)(2,1)S(1)} %load_up.1.refs_3_.w_ref, ...), custom_call_target="tpu_custom_call" | custom-call | tf_op jit(solution)/shard_map/pre/pallas_call | solution.py:41
  20.6 1.9 %hid.2 = (f32[32,2048]{1,0:T(8,128)S(1)}, f32[32,2048]{1,0:T(8,128)S(1)}) custom-call(s32[1]{0:T(128)} %bitcast.core_ref.refs_0_, bf16[32,1536]{1,0:T(8,128)(2,1)S(1)} %get-tuple-element.40.near_ref.refs_1_.refs_3_, bf16[32,1536]{1,0:T(8,128)(2,1)S(1)} %get-tuple-element.38.far_ref.refs_2_.refs_4_, bf16[3072,1536]{1,0:T(8,128)(2,1)S(1)} %load_down.1.w_ref.refs_4_.refs_3_), custom_call_target="tpu_custom_call" | custom-call | tf_op jit(solution)/shard_map/hid/pallas_call | solution.py:41
  22.5 0.5 collective-permute-start.5
  23.1 1.6 %collective-permute-start.8 = (bf16[32,3072]{1,0:T(8,128)(2,1)S(1)}, bf16[32,3072]{1,0:T(8,128)(2,1)S(1)}, u32[]{:S(2)}, u32[]{:S(2)}) collective-permute-start(bf16[32,3072]{1,0:T(8,128)(2,1)S(1)} %add_pre.1.refs_4_.refs_0_), channel_id=1, source_target_pairs={{0,2},{1,3},{2,0},{3,1},{4,6},{5,7},{6,4},{7,5},{8,10},{9,11},{10,... | collective-permute-start | bytes 589832 | tf_op jit(solution)/shard_map/ppermute | solution.py:220
  24.7 1.0 %hid.3 = (f32[32,1024]{1,0:T(8,128)S(1)}, f32[32,1024]{1,0:T(8,128)S(1)}) custom-call(s32[1]{0:T(128)} %bitcast.core_ref.refs_0_, bf16[32,1536]{1,0:T(8,128)(2,1)S(1)} %get-tuple-element.40.near_ref.refs_1_.refs_3_, bf16[32,1536]{1,0:T(8,128)(2,1)S(1)} %get-tuple-element.38.far_ref.refs_2_.refs_4_, bf16[3072,1536]{1,0:T(8,128)(2,1)S(1)} %load_down.1.w_ref.refs_4_.refs_3_, ...), custom_call_target="tpu_custom_call" | custom-call | tf_op jit(solution)/shard_map/hid/pallas_call | solution.py:41
  25.8 1.3 %collective-permute-done.6.refs_3_ = f32[32,1024]{1,0:T(8,128)S(1)} collective-permute-done((f32[32,1024]{1,0:T(8,128)S(1)}, f32[32,1024]{1,0:T(8,128)S(1)}, u32[]{:S(2)}, u32[]{:S(2)}) %collective-permute-start.6) | collective-permute-done | bytes 131104 | tf_op jit(solution)/shard_map/ppermute | solution.py:220
  27.1 0.6 collective-permute-start.7
  27.7 2.3 %collective-permute-done.8.refs_1_ = bf16[32,3072]{1,0:T(8,128)(2,1)S(1)} collective-permute-done((bf16[32,3072]{1,0:T(8,128)(2,1)S(1)}, bf16[32,3072]{1,0:T(8,128)(2,1)S(1)}, u32[]{:S(2)}, u32[]{:S(2)}) %collective-permute-start.8) | collective-permute-done | bytes 196640 | tf_op jit(solution)/shard_map/ppermute | solution.py:220
  30.3 3.9 %collective-permute-done.7.refs_1_ = bf16[32,3072]{1,0:T(8,128)(2,1)S(1)} collective-permute-done((bf16[32,3072]{1,0:T(8,128)(2,1)S(1)}, bf16[32,3072]{1,0:T(8,128)(2,1)S(1)}, u32[]{:S(2)}, u32[]{:S(2)}) %collective-permute-start.7) | collective-permute-done | bytes 196640 | tf_op jit(solution)/shard_map/ppermute | solution.py:220
  34.3 1.4 %collective-permute-done.10.p1_ref = bf16[32,3072]{1,0:T(8,128)(2,1)S(1)} collective-permute-done((bf16[32,3072]{1,0:T(8,128)(2,1)S(1)}, bf16[32,3072]{1,0:T(8,128)(2,1)S(1)}, u32[]{:S(2)}, u32[]{:S(2)}) %collective-permute-start.10) | collective-permute-done | bytes 196640 | tf_op jit(solution)/shard_map/ppermute | solution.py:220
  35.8 5.6 %down_in.1 = (f32[3072,1536]{1,0:T(8,128)}, f32[32,1536]{1,0:T(8,128)S(1)}, bf16[32,1536]{1,0:T(8,128)(2,1)S(1)}, f32[1,3072]{1,0:T(1,128)}, bf16[64,3072]{1,0:T(8,128)(2,1)S(1)}) custom-call(s32[1]{0:T(128)} %bitcast.core_ref.refs_0_, bf16[32,3072]{1,0:T(8,128)(2,1)S(1)} %pre_grad.1.p0_ref, bf16[32,3072]{1,0:T(8,128)(2,1)S(1)} %collective-permute-done.10.p1_ref, ...), custom_call_target="tpu_custom_call" | custom-call | tf_op jit(solution)/shard_map/down_in/pallas_call | solution.py:41
  41.4 1.6 %collective-permute-start.11 = (bf16[32,1536]{1,0:T(8,128)(2,1)S(1)}, bf16[32,1536]{1,0:T(8,128)(2,1)S(1)}, u32[]{:S(2)}, u32[]{:S(2)}) collective-permute-start(bf16[32,1536]{1,0:T(8,128)(2,1)S(1)} %get-tuple-element.28.refs_6_), channel_id=1, source_target_pairs={{0,4},{4,0},{8,12},{12,8},{16,20},{20,16},{24,28},{28,24},{1,5},{5... | collective-permute-start | bytes 294920 | tf_op jit(solution)/shard_map/ppermute | solution.py:217
  43.0 3.1 %down_grad.1 = (f32[3072,1536]{1,0:T(8,128)}, f32[8,128]{1,0:T(8,128)S(1)}) custom-call(s32[1]{0:T(128)} %bitcast.core_ref.refs_0_, bf16[32,3072]{1,0:T(8,128)(2,1)S(1)} %get-tuple-element.26.h0_ref.refs_1_, bf16[32,3072]{1,0:T(8,128)(2,1)S(1)} %collective-permute-done.9.refs_3_.h1_ref.refs_2_, ...), custom_call_target="tpu_custom_call", output_to_operand_aliasing={{0}: (5, {})} | custom-call | tf_op jit(solution)/shard_map/down_grad/pallas_call | solution.py:41
  46.5 2.3 %collective-permute-start.13 = (f32[8,1536]{1,0:T(8,128)S(1)}, f32[8,1536]{1,0:T(8,128)S(1)}, u32[]{:S(2)}, u32[]{:S(2)}) collective-permute-start(f32[8,1536]{1,0:T(8,128)S(1)} %get-tuple-element.35), channel_id=1, source_target_pairs={{0,16},{4,20},{8,24},{12,28},{16,0},{20,4},{24,8},{28,12},{1,17},{... | collective-permute-start | bytes 147464 | tf_op jit(solution)/shard_map/ppermute | solution.py:217
  48.8 2.0 %collective-permute-start.14 = (f32[8,1536]{1,0:T(8,128)S(1)}, f32[8,1536]{1,0:T(8,128)S(1)}, u32[]{:S(2)}, u32[]{:S(2)}) collective-permute-start(f32[8,1536]{1,0:T(8,128)S(1)} %get-tuple-element.34), channel_id=1, source_target_pairs={{0,24},{4,28},{8,16},{12,20},{16,8},{20,12},{24,0},{28,4},{1,25},{... | collective-permute-start | bytes 147464 | tf_op jit(solution)/shard_map/ppermute | solution.py:217
  50.8 6.9 %up_grad.1 = f32[1536,3072]{1,0:T(8,128)} custom-call(bf16[64,3072]{1,0:T(8,128)(2,1)S(1)} %get-tuple-element.31.refs_0_, bf16[32,1536]{1,0:T(8,128)(2,1)S(1)} %get-tuple-element.39.refs_1_, bf16[32,1536]{1,0:T(8,128)(2,1)S(1)} %get-tuple-element.37.refs_2_, f32[4,8,1536]{2,1,0:T(8,128)S(1)} %bitcast.17), custom_call_target="tpu_custom_call" | custom-call | tf_op jit(solution)/shard_map/up_grad/pallas_call | solution.py:41
  57.8 0.6 %fusion.1 = bf16[8,1536]{1,0:T(8,128)(2,1)} fusion(f32[8,1536]{1,0:T(8,128)S(1)} %collective-permute-done.12, f32[32,1536]{1,0:T(8,128)S(1)} %share.1, f32[8,1536]{1,0:T(8,128)S(1)} %collective-permute-done.13, f32[8,1536]{1,0:T(8,128)S(1)} %collective-permute-done.14), kind=kLoop, calls=%fused_computation.8 | loop fusion | flops 49152 | bytes 221184 | tf_op jit(solution)/shard_map/convert_element_type | solution.py:293
  (29 shorter events, 1.5 us)
Async XLA Ops:
  1.4 9.4 %collective-permute-start = (bf16[2,8,1536]{2,1,0:T(8,128)(2,1)S(1)}, bf16[2,8,1536]{2,1,0:T(8,128)(2,1)S(1)}, u32[]{:S(2)}, u32[]{:S(2)}) collective-permute-start(bf16[2,8,1536]{2,1,0:T(8,128)(2,1)S(1)} %stack.21), channel_id=1, source_target_pairs={{0,8},{4,12},{8,0},{12,4},{16,24},{20,28},{24,16},{28,20},{1,9},{5... | collective-permute-start | bytes 147464 | tf_op jit(solution)/shard_map/ppermute | solution.py:217
  4.5 6.3 %collective-permute-start.1 = (bf16[2,8,1536]{2,1,0:T(8,128)(2,1)S(1)}, bf16[2,8,1536]{2,1,0:T(8,128)(2,1)S(1)}, u32[]{:S(2)}, u32[]{:S(2)}) collective-permute-start(bf16[2,8,1536]{2,1,0:T(8,128)(2,1)S(1)} %stack.21), channel_id=1, source_target_pairs={{0,16},{4,20},{8,24},{12,28},{16,0},{20,4},{24,8},{28,12},{1,17},{... | collective-permute-start | bytes 147464 | tf_op jit(solution)/shard_map/ppermute | solution.py:217
  7.1 5.9 %collective-permute-start.2 = (bf16[2,8,1536]{2,1,0:T(8,128)(2,1)S(1)}, bf16[2,8,1536]{2,1,0:T(8,128)(2,1)S(1)}, u32[]{:S(2)}, u32[]{:S(2)}) collective-permute-start(bf16[2,8,1536]{2,1,0:T(8,128)(2,1)S(1)} %stack.21), channel_id=1, source_target_pairs={{0,24},{4,28},{8,16},{12,20},{16,8},{20,12},{24,0},{28,4},{1,25},{... | collective-permute-start | bytes 147464 | tf_op jit(solution)/shard_map/ppermute | solution.py:217
  13.0 5.7 %collective-permute-start.3 = (bf16[2,32,1536]{2,1,0:T(8,128)(2,1)S(1)}, bf16[2,32,1536]{2,1,0:T(8,128)(2,1)S(1)}, u32[]{:S(2)}, u32[]{:S(2)}) collective-permute-start(bf16[2,32,1536]{2,1,0:T(8,128)(2,1)S(1)} %copy_bitcast_fusion.refs_1_), channel_id=1, source_target_pairs={{0,4},{4,0},{8,12},{12,8},{16,20},{20,16},{24,28},{28,24},{1,5},{5... | collective-permute-start | bytes 589832 | tf_op jit(solution)/shard_map/ppermute | solution.py:217
  20.5 2.5 %collective-permute-start.4 = (f32[32,3072]{1,0:T(8,128)S(1)}, f32[32,3072]{1,0:T(8,128)S(1)}, u32[]{:S(2)}, u32[]{:S(2)}) collective-permute-start(f32[32,3072]{1,0:T(8,128)S(1)} %get-tuple-element.21), channel_id=1, source_target_pairs={{0,1},{1,0},{2,3},{3,2},{4,5},{5,4},{6,7},{7,6},{8,9},{9,8},{10,11... | collective-permute-start | bytes 1179656 | tf_op jit(solution)/shard_map/ppermute | solution.py:220
  22.5 3.3 %collective-permute-start.5 = (f32[32,2048]{1,0:T(8,128)S(1)}, f32[32,2048]{1,0:T(8,128)S(1)}, u32[]{:S(2)}, u32[]{:S(2)}) collective-permute-start(f32[32,2048]{1,0:T(8,128)S(1)} %get-tuple-element.22.refs_2_), channel_id=1, source_target_pairs={{0,1},{1,0},{2,3},{3,2},{4,5},{5,4},{6,7},{7,6},{8,9},{9,8},{10,11... | collective-permute-start | bytes 786440 | tf_op jit(solution)/shard_map/ppermute | solution.py:220
  23.1 2.7 %copy-start = (bf16[3072]{0:T(1024)(128)(2,1)S(1)}, bf16[3072]{0:T(1024)(128)(2,1)}, u32[]{:S(2)}) copy-start(bf16[3072]{0:T(1024)(128)(2,1)} %param.8) | copy-start | bytes 18436
  23.1 6.9 %collective-permute-start.8 = (bf16[32,3072]{1,0:T(8,128)(2,1)S(1)}, bf16[32,3072]{1,0:T(8,128)(2,1)S(1)}, u32[]{:S(2)}, u32[]{:S(2)}) collective-permute-start(bf16[32,3072]{1,0:T(8,128)(2,1)S(1)} %add_pre.1.refs_4_.refs_0_), channel_id=1, source_target_pairs={{0,2},{1,3},{2,0},{3,1},{4,6},{5,7},{6,4},{7,5},{8,10},{9,11},{10,... | collective-permute-start | bytes 589832 | tf_op jit(solution)/shard_map/ppermute | solution.py:220
  25.7 1.4 %collective-permute-start.6 = (f32[32,1024]{1,0:T(8,128)S(1)}, f32[32,1024]{1,0:T(8,128)S(1)}, u32[]{:S(2)}, u32[]{:S(2)}) collective-permute-start(f32[32,1024]{1,0:T(8,128)S(1)} %get-tuple-element.24), channel_id=1, source_target_pairs={{0,1},{1,0},{2,3},{3,2},{4,5},{5,4},{6,7},{7,6},{8,9},{9,8},{10,11... | collective-permute-start | bytes 393224 | tf_op jit(solution)/shard_map/ppermute | solution.py:220
  27.1 7.0 %collective-permute-start.7 = (bf16[32,3072]{1,0:T(8,128)(2,1)S(1)}, bf16[32,3072]{1,0:T(8,128)(2,1)S(1)}, u32[]{:S(2)}, u32[]{:S(2)}) collective-permute-start(bf16[32,3072]{1,0:T(8,128)(2,1)S(1)} %add_hid.1.refs_0_), channel_id=1, source_target_pairs={{0,2},{1,3},{2,0},{3,1},{4,6},{5,7},{6,4},{7,5},{8,10},{9,11},{10,... | collective-permute-start | bytes 589832 | tf_op jit(solution)/shard_map/ppermute | solution.py:220
  30.2 4.0 %collective-permute-start.9 = (bf16[32,3072]{1,0:T(8,128)(2,1)S(1)}, bf16[32,3072]{1,0:T(8,128)(2,1)S(1)}, u32[]{:S(2)}, u32[]{:S(2)}) collective-permute-start(bf16[32,3072]{1,0:T(8,128)(2,1)S(1)} %get-tuple-element.26.h0_ref.refs_1_), channel_id=1, source_target_pairs={{0,1},{1,0},{2,3},{3,2},{4,5},{5,4},{6,7},{7,6},{8,9},{9,8},{10,11... | collective-permute-start | bytes 589832 | tf_op jit(solution)/shard_map/ppermute | solution.py:220
  34.3 1.5 %collective-permute-start.10 = (bf16[32,3072]{1,0:T(8,128)(2,1)S(1)}, bf16[32,3072]{1,0:T(8,128)(2,1)S(1)}, u32[]{:S(2)}, u32[]{:S(2)}) collective-permute-start(bf16[32,3072]{1,0:T(8,128)(2,1)S(1)} %pre_grad.1.p0_ref), channel_id=1, source_target_pairs={{0,1},{1,0},{2,3},{3,2},{4,5},{5,4},{6,7},{7,6},{8,9},{9,8},{10,11... | collective-permute-start | bytes 589832 | tf_op jit(solution)/shard_map/ppermute | solution.py:220
  41.4 4.9 %collective-permute-start.11 = (bf16[32,1536]{1,0:T(8,128)(2,1)S(1)}, bf16[32,1536]{1,0:T(8,128)(2,1)S(1)}, u32[]{:S(2)}, u32[]{:S(2)}) collective-permute-start(bf16[32,1536]{1,0:T(8,128)(2,1)S(1)} %get-tuple-element.28.refs_6_), channel_id=1, source_target_pairs={{0,4},{4,0},{8,12},{12,8},{16,20},{20,16},{24,28},{28,24},{1,5},{5... | collective-permute-start | bytes 294920 | tf_op jit(solution)/shard_map/ppermute | solution.py:217
  46.4 11.4 %collective-permute-start.12 = (f32[8,1536]{1,0:T(8,128)S(1)}, f32[8,1536]{1,0:T(8,128)S(1)}, u32[]{:S(2)}, u32[]{:S(2)}) collective-permute-start(f32[8,1536]{1,0:T(8,128)S(1)} %get-tuple-element.36), channel_id=1, source_target_pairs={{0,8},{4,12},{8,0},{12,4},{16,24},{20,28},{24,16},{28,20},{1,9},{5... | collective-permute-start | bytes 147464 | tf_op jit(solution)/shard_map/ppermute | solution.py:217
  46.5 11.3 %collective-permute-start.13 = (f32[8,1536]{1,0:T(8,128)S(1)}, f32[8,1536]{1,0:T(8,128)S(1)}, u32[]{:S(2)}, u32[]{:S(2)}) collective-permute-start(f32[8,1536]{1,0:T(8,128)S(1)} %get-tuple-element.35), channel_id=1, source_target_pairs={{0,16},{4,20},{8,24},{12,28},{16,0},{20,4},{24,8},{28,12},{1,17},{... | collective-permute-start | bytes 147464 | tf_op jit(solution)/shard_map/ppermute | solution.py:217
  48.8 9.0 %collective-permute-start.14 = (f32[8,1536]{1,0:T(8,128)S(1)}, f32[8,1536]{1,0:T(8,128)S(1)}, u32[]{:S(2)}, u32[]{:S(2)}) collective-permute-start(f32[8,1536]{1,0:T(8,128)S(1)} %get-tuple-element.34), channel_id=1, source_target_pairs={{0,24},{4,28},{8,16},{12,20},{16,8},{20,12},{24,0},{28,4},{1,25},{... | collective-permute-start | bytes 147464 | tf_op jit(solution)/shard_map/ppermute | solution.py:217

commit v5 on v4

--- a/solution.py
+++ b/solution.py
@@ -12,7 +12,7 @@
 BF16 = jnp.bfloat16
 MIB = 1024 * 1024
 SLOTS = 4
-DOWN_EARLY = 8
+UP_FIRST = 4
 EARLY = 16 * MIB
 SCALE = 1000
 
@@ -121,23 +121,31 @@
         at += width
 
 
+def add_cut_kernel(cut, a_ref, b_ref, first_ref, second_ref):
+    total = (a_ref[...] + b_ref[...]).astype(BF16)
+    first_ref[...] = total[:, :cut]
+    second_ref[...] = total[:, cut:]
+
+
 def sum_kernel(a_ref, b_ref, out_ref):
     out_ref[...] = a_ref[...] + b_ref[...].astype(F32)
 
 
-def act_kernel(*refs):
+def act_kernel(start, *refs):
     parts, bias_ref, act_ref, slope_ref = refs[:-3], refs[-3], refs[-2], refs[-1]
-    pre = tree_sum([r[...].astype(F32) for r in parts]) + bias_ref[...].astype(F32)
+    bias = bias_ref[:, start : start + act_ref.shape[1]].astype(F32)
+    pre = tree_sum([r[...].astype(F32) for r in parts]) + bias
     cdf = 0.5 * (1.0 + lax.erf(pre * (1.0 / math.sqrt(2.0))))
     dens = jnp.exp(-0.5 * pre * pre) * (1.0 / math.sqrt(2.0 * math.pi))
     act_ref[...] = (pre * cdf).astype(BF16)
     slope_ref[...] = cdf + pre * dens
 
 
-def grad_kernel(*refs):
-    parts, slope_ref, out_ref = refs[:-2], refs[-2], refs[-1]
+def grad_kernel(cut, *refs):
+    parts, (slope_a, slope_b, out_ref) = refs[:-3], refs[-3:]
     hid = tree_sum([r[...].astype(F32) for r in parts])
-    out_ref[...] = (hid * slope_ref[...]).astype(BF16)
+    out_ref[:, :cut] = (hid[:, :cut] * slope_a[...]).astype(BF16)
+    out_ref[:, cut:] = (hid[:, cut:] * slope_b[...]).astype(BF16)
 
 
 def write_tiles(first, last, rows, make, out_ref, buf, sems):
@@ -170,13 +178,13 @@
 
 
 def down_in_kernel(
-    last, rows, core_ref, p0_ref, p1_ref, w_ref, h0_ref, h1_ref, near_ref, far_ref, out_ref, keep_ref, send_ref, bias_ref, p_ref,
+    base, last, rows, core_ref, p0_ref, p1_ref, w_ref, h0_ref, h1_ref, near_ref, far_ref, _, out_ref, keep_ref, send_ref, bias_ref, p_ref,
     buf, sems,
 ):
     near_first = core_ref[0] == 0
     g = local_tokens(core_ref[0], near_ref, far_ref)
     copies = [
-        pltpu.make_async_copy(buf.at[t], out_ref.at[pl.ds(t * rows, rows), :], sems.at[t]) for t in range(last)
+        pltpu.make_async_copy(buf.at[t], out_ref.at[pl.ds(base + t * rows, rows), :], sems.at[t]) for t in range(last)
     ]
     for t in range(last):
         at = t * rows
@@ -198,13 +206,15 @@
         copies[t].wait()
 
 
-def up_kernel(rows, p_ref, near_ref, far_ref, out_ref, buf, sems):
+def up_kernel(first, last, rows, p_ref, near_ref, far_ref, *refs):
+    out_ref, done_ref, buf, sems = refs[-4:]
+    done_ref[...] = jnp.zeros_like(done_ref)
     p = p_ref[...]
 
     def make(at):
         return outer(jnp.concatenate([near_ref[:, at : at + rows], far_ref[:, at : at + rows]], axis=0), p)
 
-    write_tiles(0, out_ref.shape[0] // rows, rows, make, out_ref, buf, sems)
+    write_tiles(first, last, rows, make, out_ref, buf, sems)
 
 
 def on_device(rows, cols, normed, out_grad, up_weight, up_bias, down_weight):
@@ -239,7 +249,8 @@
     )
     other_pre = col_swap(send_pre, 1)
 
-    cut = units * 2 // 3 // 128 * 128
+    part = units * 2 // 3 // 128 * 128
+    cut = units // 2 // 128 * 128
 
     def hid_piece(start, width, after):
         piece_t = jax.ShapeDtypeStruct((half, width), F32)
@@ -248,47 +259,69 @@
             in_specs=[smem()] + [vmem()] * 3, after=after,
         )
 
-    hids = [hid_piece(0, cut, ())]
-    chip_pre = call(add_kernel, "add_pre", bf_t, (keep_pre, other_pre), after=(hids[0][1],), cost=EARLY)
-    pre_parts = [chip_pre] + [col_swap(chip_pre, k) for k in range(2, cols, 2)]
-    hids.append(hid_piece(cut, units - cut, (chip_pre,)))
-    act, slope = call(act_kernel, "act", (bf_t, keep_t), (*pre_parts, up_bias.reshape(1, units)), cost=EARLY)
-    act_far = col_swap(act, 1)
+    hids = [hid_piece(0, part, ())]
+    widths = (cut, units - cut)
+    chips = call(
+        functools.partial(add_cut_kernel, cut), "add_pre", tuple(jax.ShapeDtypeStruct((half, w), BF16) for w in widths),
+        (keep_pre, other_pre), after=(hids[0][1],), cost=EARLY,
+    )
+    pre_parts = [[c] + [col_swap(c, k) for k in range(2, cols, 2)] for c in chips]
+    hids.append(hid_piece(part, units - part, tuple(chips)))
     others = [col_swap(send, 1) for _, send in hids]
     chip_hid = call(add_kernel, "add_hid", bf_t, (*[k for k, _ in hids], *others))
     hid_parts = [chip_hid] + [col_swap(chip_hid, k) for k in range(2, cols, 2)]
-    pg = call(grad_kernel, "pre_grad", bf_t, (*hid_parts, slope), after=(act_far,))
-    pg_far = col_swap(pg, 1)
-
-    rt = divisor(units, 256)
-    tiles = units // rt
-    early = max(1, tiles * DOWN_EARLY // 12)
-    part_t = jax.ShapeDtypeStruct((half, feats), F32)
+
+    bias = up_bias.reshape(1, units)
+    acts, slopes = zip(*[
+        call(
+            functools.partial(act_kernel, start), "act",
+            (jax.ShapeDtypeStruct((half, w), BF16), jax.ShapeDtypeStruct((half, w), F32)), (*parts, bias),
+            cost=EARLY,
+        )
+        for start, w, parts in zip((0, cut), widths, pre_parts)
+    ])
+    acts_far = [col_swap(a, 1) for a in acts]
+
     token_t = jax.ShapeDtypeStruct((8, 128), F32)
     down_t = jax.ShapeDtypeStruct((units, feats), F32)
-    down_early, keep_in, send_in, bias_grad, pg_all = call(
-        functools.partial(down_in_kernel, early, rt), "down_in",
-        (down_t, part_t, jax.ShapeDtypeStruct((half, feats), BF16), jax.ShapeDtypeStruct((1, units), F32), jax.ShapeDtypeStruct((2 * half, units), BF16)),
-        (core, pg, pg_far, up_weight, act, act_far, g_near, g_far), in_specs=[smem()] + [vmem()] * 7,
-        out_specs=(anywhere(),) + (vmem(),) * 4, limit=24,
-        scratch=[pltpu.VMEM((early, rt, feats), F32), pltpu.SemaphoreType.DMA((early,))],
+    rt = divisor(cut, 256)
+    down_half, wrote = call(
+        functools.partial(down_kernel, 0, cut // rt, rt), "down_first", (down_t, token_t),
+        (core, acts[0], acts_far[0], g_near, g_far), in_specs=[smem()] + [vmem()] * 4, out_specs=(anywhere(), vmem()),
+        scratch=[pltpu.VMEM((SLOTS, rt, feats), F32), pltpu.SemaphoreType.DMA((SLOTS,))], after=(acts[1],),
+    )
+    pg = call(functools.partial(grad_kernel, cut), "pre_grad", bf_t, (*hid_parts, *slopes), after=(wrote, acts_far[1]))
+    pg_far = col_swap(pg, 1)
+
+    part_t = jax.ShapeDtypeStruct((half, feats), F32)
+    rt = divisor(units - cut, 256)
+    tiles = (units - cut) // rt
+    down_grad, keep_in, send_in, bias_grad, pg_all = call(
+        functools.partial(down_in_kernel, cut, tiles, rt), "down_last_in",
+        (
+            down_t, part_t, jax.ShapeDtypeStruct((half, feats), BF16), jax.ShapeDtypeStruct((1, units), F32),
+            jax.ShapeDtypeStruct((2 * half, units), BF16),
+        ),
+        (core, pg, pg_far, up_weight, acts[1], acts_far[1], g_near, g_far, down_half),
+        in_specs=[smem()] + [vmem()] * 7 + [anywhere()], out_specs=(anywhere(),) + (vmem(),) * 4, limit=24,
+        scratch=[pltpu.VMEM((tiles, rt, feats), F32), pltpu.SemaphoreType.DMA((tiles,))], aliases={8: 0},
     )
     far_in = row_swap(send_in, 1)
 
-    down_grad, wrote = call(
-        functools.partial(down_kernel, early, tiles, rt), "down_grad", (down_t, token_t),
-        (core, act, act_far, g_near, g_far, down_early), in_specs=[smem()] + [vmem()] * 4 + [anywhere()],
-        out_specs=(anywhere(), vmem()), scratch=[pltpu.VMEM((SLOTS, rt, feats), F32), pltpu.SemaphoreType.DMA((SLOTS,))],
-        aliases={5: 0}, after=(send_in,),
+    dt = divisor(feats, 128)
+    dtiles = feats // dt
+    first = max(1, dtiles * UP_FIRST // 12)
+    up_t = jax.ShapeDtypeStruct((feats, units), F32)
+    slots = [pltpu.VMEM((SLOTS, dt, units), F32), pltpu.SemaphoreType.DMA((SLOTS,))]
+    up_half, wrote = call(
+        functools.partial(up_kernel, 0, first, dt), "up_first", (up_t, token_t), (pg_all, x_near, x_far),
+        in_specs=[vmem()] * 3, out_specs=(anywhere(), vmem()), scratch=slots, after=(send_in,),
     )
     share = call(sum_kernel, "share", part_t, (keep_in, far_in), after=(wrote,)).reshape(blocks, mine, feats)
     terms = [share[0]] + [row_swap(share[k // 2], k) for k in range(2, rows, 2)]
-
-    dt = divisor(feats, 128)
-    up_grad = call(
-        functools.partial(up_kernel, dt), "up_grad", jax.ShapeDtypeStruct((feats, units), F32), (pg_all, x_near, x_far),
-        in_specs=[vmem()] * 3, out_specs=anywhere(),
-        scratch=[pltpu.VMEM((SLOTS, dt, units), F32), pltpu.SemaphoreType.DMA((SLOTS,))], after=(share,),
+    up_grad, _ = call(
+        functools.partial(up_kernel, first, dtiles, dt), "up_last", (up_t, token_t), (pg_all, x_near, x_far, up_half),
+        in_specs=[vmem()] * 3 + [anywhere()], out_specs=(anywhere(), vmem()), scratch=slots, aliases={3: 0}, after=(share,),
     )
     in_grad = tree_sum(terms).astype(BF16)
     return (in_grad, up_grad, bias_grad.reshape(units), down_grad)

time: 58.6 us -> 56.3 us (0.961)
  waiting for transfers between devices: 11.7 us -> 5.56 us
  starting transfers between devices: 16.2 us -> 18.3 us
  Pallas kernels: 28.8 us -> 30.7 us
    ppermute x7 -> x9, waiting for transfers between devices: 8.89 us -> 4.14 us  [col_swap(): return lax.ppermute(x, 'col', [(i, i ^ k) for i in range(cols)])]
    ppermute x7 -> x9, starting transfers between devices: 2.99 us -> 4.94 us  [col_swap(): return lax.ppermute(x, 'col', [(i, i ^ k) for i in range(cols)])]
    pallas_call x14 -> x16, Pallas kernels: 28.8 us -> 30.7 us  [call(): pl.pallas_call(body, out_shape=out_shape, in_specs=in_specs + [anywhere()...]
    ppermute x8, waiting for transfers between devices: 2.86 us -> 1.42 us  [row_swap(): return lax.ppermute(x, 'row', [(i, i ^ k) for i in range(rows)])]
  transfers between devices with their start and end apart: 15 -> 17, of which waited for: 7 -> 7; matrix products, arithmetic and copies ran while one was open for 0% -> 0% of each run, Pallas kernels for 35% -> 42%
where the time goes in v5:
time: 56.3 us; the launch traced here: 56.1 us
  Pallas kernels  30.7 us (55%)
  starting transfers between devices  18.3 us (33%)
  waiting for transfers between devices  5.56 us (10%)
  between operations  0.87 us (2%)
  other arithmetic  0.66 us (1%)
    pallas_call x16, Pallas kernels, call(): pl.pallas_call(body, out_shape=out_shape, in_specs=in_specs + [anywhere()...  30.7 us
    ppermute x8, starting transfers between devices, row_swap(): return lax.ppermute(x, 'row', [(i, i ^ k) for i in range(rows)])  13.3 us
    ppermute x9, starting transfers between devices, col_swap(): return lax.ppermute(x, 'col', [(i, i ^ k) for i in range(cols)])  4.94 us
    ppermute x9, waiting for transfers between devices, col_swap(): return lax.ppermute(x, 'col', [(i, i ^ k) for i in range(cols)])  4.14 us
    ppermute x8, waiting for transfers between devices, row_swap(): return lax.ppermute(x, 'row', [(i, i ^ k) for i in range(rows)])  1.42 us
  transfers between devices with their start and end apart: 17, of which 7 were waited for; matrix products, arithmetic and copies ran while one was open for 0% of the time, Pallas kernels for 42%

profile of v5, /device:TPU:0, one launch (start us, length us, event | category | flops | bytes accessed | tf_op | source)
XLA Modules:
  0.0 56.1 jit_solution(15102368011057073013)
XLA Ops:
  0.6 0.8 %stack.21 = bf16[2,8,1536]{2,1,0:T(8,128)(2,1)S(1)} custom-call(bf16[8,1536]{1,0:T(8,128)(2,1)} %a_ref.1, bf16[8,1536]{1,0:T(8,128)(2,1)} %b_ref.1), custom_call_target="tpu_custom_call" | custom-call | tf_op jit(solution)/shard_map/stack/pallas_call | solution.py:41
  1.4 5.1 %collective-permute-start.2 = (bf16[2,8,1536]{2,1,0:T(8,128)(2,1)S(1)}, bf16[2,8,1536]{2,1,0:T(8,128)(2,1)S(1)}, u32[]{:S(2)}, u32[]{:S(2)}) collective-permute-start(bf16[2,8,1536]{2,1,0:T(8,128)(2,1)S(1)} %stack.21), channel_id=1, source_target_pairs={{0,24},{4,28},{8,16},{12,20},{16,8},{20,12},{24,0},{28,4},{1,25},{... | collective-permute-start | bytes 147464 | tf_op jit(solution)/shard_map/ppermute | solution.py:227
  6.5 0.6 %collective-permute-start = (bf16[2,8,1536]{2,1,0:T(8,128)(2,1)S(1)}, bf16[2,8,1536]{2,1,0:T(8,128)(2,1)S(1)}, u32[]{:S(2)}, u32[]{:S(2)}) collective-permute-start(bf16[2,8,1536]{2,1,0:T(8,128)(2,1)S(1)} %stack.21), channel_id=1, source_target_pairs={{0,8},{4,12},{8,0},{12,4},{16,24},{20,28},{24,16},{28,20},{1,9},{5... | collective-permute-start | bytes 147464 | tf_op jit(solution)/shard_map/ppermute | solution.py:227
  7.2 3.7 %load_up.1.refs_3_.w_ref = bf16[1536,3072]{1,0:T(8,128)(2,1)S(1)} custom-call(bf16[1536,3072]{1,0:T(8,128)(2,1)} %w_ref.1), custom_call_target="tpu_custom_call" | custom-call | tf_op jit(solution)/shard_map/load_up/pallas_call | solution.py:41
  10.9 0.6 %collective-permute-done.1 = bf16[2,8,1536]{2,1,0:T(8,128)(2,1)S(1)} collective-permute-done((bf16[2,8,1536]{2,1,0:T(8,128)(2,1)S(1)}, bf16[2,8,1536]{2,1,0:T(8,128)(2,1)S(1)}, u32[]{:S(2)}, u32[]{:S(2)}) %collective-permute-start.1) | collective-permute-done | bytes 49184 | tf_op jit(solution)/shard_map/ppermute | solution.py:227
  11.6 1.6 %collective-permute-start.3 = (bf16[2,32,1536]{2,1,0:T(8,128)(2,1)S(1)}, bf16[2,32,1536]{2,1,0:T(8,128)(2,1)S(1)}, u32[]{:S(2)}, u32[]{:S(2)}) collective-permute-start(bf16[2,32,1536]{2,1,0:T(8,128)(2,1)S(1)} %copy_bitcast_fusion.refs_1_), channel_id=1, source_target_pairs={{0,4},{4,0},{8,12},{12,8},{16,20},{20,16},{24,28},{28,24},{1,5},{5... | collective-permute-start | bytes 589832 | tf_op jit(solution)/shard_map/ppermute | solution.py:227
  13.1 3.7 %load_down.1.w_ref.refs_4_.refs_3_ = bf16[3072,1536]{1,0:T(8,128)(2,1)S(1)} custom-call(bf16[3072,1536]{1,0:T(8,128)(2,1)} %refs_0_.1, bf16[2,32,1536]{2,1,0:T(8,128)(2,1)S(1)} %copy_bitcast_fusion.refs_1_), custom_call_target="tpu_custom_call" | custom-call | tf_op jit(solution)/shard_map/load_down/pallas_call | solution.py:41
  17.4 1.7 %pre.1 = (f32[32,3072]{1,0:T(8,128)S(1)}, f32[32,3072]{1,0:T(8,128)S(1)}) custom-call(s32[1]{0:T(128)} %bitcast.core_ref.refs_0_, bf16[32,1536]{1,0:T(8,128)(2,1)S(1)} %get-tuple-element.53.refs_1_, bf16[32,1536]{1,0:T(8,128)(2,1)S(1)} %get-tuple-element.51.refs_2_, bf16[1536,3072]{1,0:T(8,128)(2,1)S(1)} %load_up.1.refs_3_.w_ref, ...), custom_call_target="tpu_custom_call" | custom-call | tf_op jit(solution)/shard_map/pre/pallas_call | solution.py:41
  19.2 1.9 %hid.2 = (f32[32,2048]{1,0:T(8,128)S(1)}, f32[32,2048]{1,0:T(8,128)S(1)}) custom-call(s32[1]{0:T(128)} %bitcast.core_ref.refs_0_, bf16[32,1536]{1,0:T(8,128)(2,1)S(1)} %get-tuple-element.54.near_ref.refs_1_.refs_3_, bf16[32,1536]{1,0:T(8,128)(2,1)S(1)} %get-tuple-element.52.far_ref.refs_2_.refs_4_, bf16[3072,1536]{1,0:T(8,128)(2,1)S(1)} %load_down.1.w_ref.refs_4_.refs_3_), custom_call_target="tpu_custom_call" | custom-call | tf_op jit(solution)/shard_map/hid/pallas_call | solution.py:41
  21.2 1.6 %collective-permute-start.8 = (bf16[32,1536]{1,0:T(8,128)(2,1)S(1)}, bf16[32,1536]{1,0:T(8,128)(2,1)S(1)}, u32[]{:S(2)}, u32[]{:S(2)}) collective-permute-start(bf16[32,1536]{1,0:T(8,128)(2,1)S(1)} %get-tuple-element.30.refs_4_.refs_0_), channel_id=1, source_target_pairs={{0,2},{1,3},{2,0},{3,1},{4,6},{5,7},{6,4},{7,5},{8,10},{9,11},{10,... | collective-permute-start | bytes 294920 | tf_op jit(solution)/shard_map/ppermute | solution.py:230
  23.1 1.0 %hid.3 = (f32[32,1024]{1,0:T(8,128)S(1)}, f32[32,1024]{1,0:T(8,128)S(1)}) custom-call(s32[1]{0:T(128)} %bitcast.core_ref.refs_0_, bf16[32,1536]{1,0:T(8,128)(2,1)S(1)} %get-tuple-element.54.near_ref.refs_1_.refs_3_, bf16[32,1536]{1,0:T(8,128)(2,1)S(1)} %get-tuple-element.52.far_ref.refs_2_.refs_4_, bf16[3072,1536]{1,0:T(8,128)(2,1)S(1)} %load_down.1.w_ref.refs_4_.refs_3_, ...), custom_call_target="tpu_custom_call" | custom-call | tf_op jit(solution)/shard_map/hid/pallas_call | solution.py:41
  24.1 0.9 %collective-permute-start.9 = (bf16[32,1536]{1,0:T(8,128)(2,1)S(1)}, bf16[32,1536]{1,0:T(8,128)(2,1)S(1)}, u32[]{:S(2)}, u32[]{:S(2)}) collective-permute-start(bf16[32,1536]{1,0:T(8,128)(2,1)S(1)} %get-tuple-element.31.refs_5_.refs_0_), channel_id=1, source_target_pairs={{0,2},{1,3},{2,0},{3,1},{4,6},{5,7},{6,4},{7,5},{8,10},{9,11},{10,... | collective-permute-start | bytes 294920 | tf_op jit(solution)/shard_map/ppermute | solution.py:230
  25.0 1.5 %collective-permute-done.8.refs_1_ = bf16[32,1536]{1,0:T(8,128)(2,1)S(1)} collective-permute-done((bf16[32,1536]{1,0:T(8,128)(2,1)S(1)}, bf16[32,1536]{1,0:T(8,128)(2,1)S(1)}, u32[]{:S(2)}, u32[]{:S(2)}) %collective-permute-start.8) | collective-permute-done | bytes 98336 | tf_op jit(solution)/shard_map/ppermute | solution.py:230
  26.7 1.9 %collective-permute-start.7 = (bf16[32,3072]{1,0:T(8,128)(2,1)S(1)}, bf16[32,3072]{1,0:T(8,128)(2,1)S(1)}, u32[]{:S(2)}, u32[]{:S(2)}) collective-permute-start(bf16[32,3072]{1,0:T(8,128)(2,1)S(1)} %add_hid.1.refs_0_), channel_id=1, source_target_pairs={{0,2},{1,3},{2,0},{3,1},{4,6},{5,7},{6,4},{7,5},{8,10},{9,11},{10,... | collective-permute-start | bytes 589832 | tf_op jit(solution)/shard_map/ppermute | solution.py:230
  29.4 4.1 %down_first.1 = (f32[3072,1536]{1,0:T(8,128)}, f32[8,128]{1,0:T(8,128)S(1)}) custom-call(s32[1]{0:T(128)} %bitcast.core_ref.refs_0_, bf16[32,1536]{1,0:T(8,128)(2,1)S(1)} %get-tuple-element.36.refs_1_, bf16[32,1536]{1,0:T(8,128)(2,1)S(1)} %collective-permute-done.10.refs_2_, bf16[32,1536]{1,0:T(8,128)(2,1)S(1)} %get-tuple-element.54.near_ref.refs_1_.refs_3_, ...), custom_call_target="tpu_custom_call" | custom-call | tf_op jit(solution)/shard_map/down_first/pallas_call | solution.py:41
  33.4 0.7 %collective-permute-done.7.refs_1_ = bf16[32,3072]{1,0:T(8,128)(2,1)S(1)} collective-permute-done((bf16[32,3072]{1,0:T(8,128)(2,1)S(1)}, bf16[32,3072]{1,0:T(8,128)(2,1)S(1)}, u32[]{:S(2)}, u32[]{:S(2)}) %collective-permute-start.7) | collective-permute-done | bytes 196640 | tf_op jit(solution)/shard_map/ppermute | solution.py:230
  34.3 1.4 %collective-permute-done.12.p1_ref = bf16[32,3072]{1,0:T(8,128)(2,1)S(1)} collective-permute-done((bf16[32,3072]{1,0:T(8,128)(2,1)S(1)}, bf16[32,3072]{1,0:T(8,128)(2,1)S(1)}, u32[]{:S(2)}, u32[]{:S(2)}) %collective-permute-start.12) | collective-permute-done | bytes 196640 | tf_op jit(solution)/shard_map/ppermute | solution.py:230
  35.7 4.7 %down_last_in.1 = (f32[3072,1536]{1,0:T(8,128)}, f32[32,1536]{1,0:T(8,128)S(1)}, bf16[32,1536]{1,0:T(8,128)(2,1)S(1)}, f32[1,3072]{1,0:T(1,128)}, bf16[64,3072]{1,0:T(8,128)(2,1)S(1)}) custom-call(s32[1]{0:T(128)} %bitcast.core_ref.refs_0_, bf16[32,3072]{1,0:T(8,128)(2,1)S(1)} %pre_grad.1.p0_ref, ...), custom_call_target="tpu_custom_call", output_to_operand_aliasing={{0}: (8, {})} | custom-call | tf_op jit(solution)/shard_map/down_last_in/pallas_call | solution.py:41
  40.4 1.6 %collective-permute-start.13 = (bf16[32,1536]{1,0:T(8,128)(2,1)S(1)}, bf16[32,1536]{1,0:T(8,128)(2,1)S(1)}, u32[]{:S(2)}, u32[]{:S(2)}) collective-permute-start(bf16[32,1536]{1,0:T(8,128)(2,1)S(1)} %get-tuple-element.41.refs_3_), channel_id=1, source_target_pairs={{0,4},{4,0},{8,12},{12,8},{16,20},{20,16},{24,28},{28,24},{1,5},{5... | collective-permute-start | bytes 294920 | tf_op jit(solution)/shard_map/ppermute | solution.py:227
  42.0 3.1 %up_first.1 = (f32[1536,3072]{1,0:T(8,128)}, f32[8,128]{1,0:T(8,128)S(1)}) custom-call(bf16[64,3072]{1,0:T(8,128)(2,1)S(1)} %get-tuple-element.42.refs_0_, bf16[32,1536]{1,0:T(8,128)(2,1)S(1)} %get-tuple-element.53.refs_1_, bf16[32,1536]{1,0:T(8,128)(2,1)S(1)} %get-tuple-element.51.refs_2_, bf16[32,1536]{1,0:T(8,128)(2,1)S(1)} %get-tuple-element.41.refs_3_), custom_call_target="tpu_custom_call" | custom-call | tf_op jit(solution)/shard_map/up_first/pallas_call | solution.py:41
  45.4 3.2 %collective-permute-start.16 = (f32[8,1536]{1,0:T(8,128)S(1)}, f32[8,1536]{1,0:T(8,128)S(1)}, u32[]{:S(2)}, u32[]{:S(2)}) collective-permute-start(f32[8,1536]{1,0:T(8,128)S(1)} %get-tuple-element.48), channel_id=1, source_target_pairs={{0,24},{4,28},{8,16},{12,20},{16,8},{20,12},{24,0},{28,4},{1,25},{... | collective-permute-start | bytes 147464 | tf_op jit(solution)/shard_map/ppermute | solution.py:227
  48.6 1.2 %collective-permute-start.14 = (f32[8,1536]{1,0:T(8,128)S(1)}, f32[8,1536]{1,0:T(8,128)S(1)}, u32[]{:S(2)}, u32[]{:S(2)}) collective-permute-start(f32[8,1536]{1,0:T(8,128)S(1)} %get-tuple-element.50), channel_id=1, source_target_pairs={{0,8},{4,12},{8,0},{12,4},{16,24},{20,28},{24,16},{28,20},{1,9},{5... | collective-permute-start | bytes 147464 | tf_op jit(solution)/shard_map/ppermute | solution.py:227
  49.8 5.6 %up_last.1 = (f32[1536,3072]{1,0:T(8,128)}, f32[8,128]{1,0:T(8,128)}) custom-call(bf16[64,3072]{1,0:T(8,128)(2,1)S(1)} %get-tuple-element.42.refs_0_, bf16[32,1536]{1,0:T(8,128)(2,1)S(1)} %get-tuple-element.53.refs_1_, bf16[32,1536]{1,0:T(8,128)(2,1)S(1)} %get-tuple-element.51.refs_2_, ...), custom_call_target="tpu_custom_call", output_to_operand_aliasing={{0}: (3, {})} | custom-call | tf_op jit(solution)/shard_map/up_last/pallas_call | solution.py:41
  55.5 0.6 %fusion.1 = bf16[8,1536]{1,0:T(8,128)(2,1)} fusion(f32[8,1536]{1,0:T(8,128)S(1)} %collective-permute-done.14, f32[32,1536]{1,0:T(8,128)S(1)} %share.1, f32[8,1536]{1,0:T(8,128)S(1)} %collective-permute-done.15, f32[8,1536]{1,0:T(8,128)S(1)} %collective-permute-done.16), kind=kLoop, calls=%fused_computation.8 | loop fusion | flops 49152 | bytes 221184 | tf_op jit(solution)/shard_map/convert_element_type | solution.py:326
  (35 shorter events, 2.4 us)
Async XLA Ops:
  1.4 9.5 %collective-permute-start.2 = (bf16[2,8,1536]{2,1,0:T(8,128)(2,1)S(1)}, bf16[2,8,1536]{2,1,0:T(8,128)(2,1)S(1)}, u32[]{:S(2)}, u32[]{:S(2)}) collective-permute-start(bf16[2,8,1536]{2,1,0:T(8,128)(2,1)S(1)} %stack.21), channel_id=1, source_target_pairs={{0,24},{4,28},{8,16},{12,20},{16,8},{20,12},{24,0},{28,4},{1,25},{... | collective-permute-start | bytes 147464 | tf_op jit(solution)/shard_map/ppermute | solution.py:227
  6.5 5.0 %collective-permute-start.1 = (bf16[2,8,1536]{2,1,0:T(8,128)(2,1)S(1)}, bf16[2,8,1536]{2,1,0:T(8,128)(2,1)S(1)}, u32[]{:S(2)}, u32[]{:S(2)}) collective-permute-start(bf16[2,8,1536]{2,1,0:T(8,128)(2,1)S(1)} %stack.21), channel_id=1, source_target_pairs={{0,16},{4,20},{8,24},{12,28},{16,0},{20,4},{24,8},{28,12},{1,17},{... | collective-permute-start | bytes 147464 | tf_op jit(solution)/shard_map/ppermute | solution.py:227
  6.5 5.0 %collective-permute-start = (bf16[2,8,1536]{2,1,0:T(8,128)(2,1)S(1)}, bf16[2,8,1536]{2,1,0:T(8,128)(2,1)S(1)}, u32[]{:S(2)}, u32[]{:S(2)}) collective-permute-start(bf16[2,8,1536]{2,1,0:T(8,128)(2,1)S(1)} %stack.21), channel_id=1, source_target_pairs={{0,8},{4,12},{8,0},{12,4},{16,24},{20,28},{24,16},{28,20},{1,9},{5... | collective-permute-start | bytes 147464 | tf_op jit(solution)/shard_map/ppermute | solution.py:227
  11.6 5.8 %collective-permute-start.3 = (bf16[2,32,1536]{2,1,0:T(8,128)(2,1)S(1)}, bf16[2,32,1536]{2,1,0:T(8,128)(2,1)S(1)}, u32[]{:S(2)}, u32[]{:S(2)}) collective-permute-start(bf16[2,32,1536]{2,1,0:T(8,128)(2,1)S(1)} %copy_bitcast_fusion.refs_1_), channel_id=1, source_target_pairs={{0,4},{4,0},{8,12},{12,8},{16,20},{20,16},{24,28},{28,24},{1,5},{5... | collective-permute-start | bytes 589832 | tf_op jit(solution)/shard_map/ppermute | solution.py:227
  19.2 1.9 %collective-permute-start.4 = (f32[32,3072]{1,0:T(8,128)S(1)}, f32[32,3072]{1,0:T(8,128)S(1)}, u32[]{:S(2)}, u32[]{:S(2)}) collective-permute-start(f32[32,3072]{1,0:T(8,128)S(1)} %get-tuple-element.28), channel_id=1, source_target_pairs={{0,1},{1,0},{2,3},{3,2},{4,5},{5,4},{6,7},{7,6},{8,9},{9,8},{10,11... | collective-permute-start | bytes 1179656 | tf_op jit(solution)/shard_map/ppermute | solution.py:230
  21.1 1.7 %copy-start = (bf16[3072]{0:T(1024)(128)(2,1)S(1)}, bf16[3072]{0:T(1024)(128)(2,1)}, u32[]{:S(2)}) copy-start(bf16[3072]{0:T(1024)(128)(2,1)} %param.8) | copy-start | bytes 18436
  21.2 5.3 %collective-permute-start.8 = (bf16[32,1536]{1,0:T(8,128)(2,1)S(1)}, bf16[32,1536]{1,0:T(8,128)(2,1)S(1)}, u32[]{:S(2)}, u32[]{:S(2)}) collective-permute-start(bf16[32,1536]{1,0:T(8,128)(2,1)S(1)} %get-tuple-element.30.refs_4_.refs_0_), channel_id=1, source_target_pairs={{0,2},{1,3},{2,0},{3,1},{4,6},{5,7},{6,4},{7,5},{8,10},{9,11},{10,... | collective-permute-start | bytes 294920 | tf_op jit(solution)/shard_map/ppermute | solution.py:230
  22.8 3.9 %collective-permute-start.5 = (f32[32,2048]{1,0:T(8,128)S(1)}, f32[32,2048]{1,0:T(8,128)S(1)}, u32[]{:S(2)}, u32[]{:S(2)}) collective-permute-start(f32[32,2048]{1,0:T(8,128)S(1)} %get-tuple-element.29.refs_2_), channel_id=1, source_target_pairs={{0,1},{1,0},{2,3},{3,2},{4,5},{5,4},{6,7},{7,6},{8,9},{9,8},{10,11... | collective-permute-start | bytes 786440 | tf_op jit(solution)/shard_map/ppermute | solution.py:230
  24.1 5.0 %collective-permute-start.9 = (bf16[32,1536]{1,0:T(8,128)(2,1)S(1)}, bf16[32,1536]{1,0:T(8,128)(2,1)S(1)}, u32[]{:S(2)}, u32[]{:S(2)}) collective-permute-start(bf16[32,1536]{1,0:T(8,128)(2,1)S(1)} %get-tuple-element.31.refs_5_.refs_0_), channel_id=1, source_target_pairs={{0,2},{1,3},{2,0},{3,1},{4,6},{5,7},{6,4},{7,5},{8,10},{9,11},{10,... | collective-permute-start | bytes 294920 | tf_op jit(solution)/shard_map/ppermute | solution.py:230
  25.0 1.7 %collective-permute-start.6 = (f32[32,1024]{1,0:T(8,128)S(1)}, f32[32,1024]{1,0:T(8,128)S(1)}, u32[]{:S(2)}, u32[]{:S(2)}) collective-permute-start(f32[32,1024]{1,0:T(8,128)S(1)} %get-tuple-element.33), channel_id=1, source_target_pairs={{0,1},{1,0},{2,3},{3,2},{4,5},{5,4},{6,7},{7,6},{8,9},{9,8},{10,11... | collective-permute-start | bytes 393224 | tf_op jit(solution)/shard_map/ppermute | solution.py:230
  26.6 2.8 %collective-permute-start.10 = (bf16[32,1536]{1,0:T(8,128)(2,1)S(1)}, bf16[32,1536]{1,0:T(8,128)(2,1)S(1)}, u32[]{:S(2)}, u32[]{:S(2)}) collective-permute-start(bf16[32,1536]{1,0:T(8,128)(2,1)S(1)} %get-tuple-element.36.refs_1_), channel_id=1, source_target_pairs={{0,1},{1,0},{2,3},{3,2},{4,5},{5,4},{6,7},{7,6},{8,9},{9,8},{10,11... | collective-permute-start | bytes 294920 | tf_op jit(solution)/shard_map/ppermute | solution.py:230
  26.7 7.5 %collective-permute-start.7 = (bf16[32,3072]{1,0:T(8,128)(2,1)S(1)}, bf16[32,3072]{1,0:T(8,128)(2,1)S(1)}, u32[]{:S(2)}, u32[]{:S(2)}) collective-permute-start(bf16[32,3072]{1,0:T(8,128)(2,1)S(1)} %add_hid.1.refs_0_), channel_id=1, source_target_pairs={{0,2},{1,3},{2,0},{3,1},{4,6},{5,7},{6,4},{7,5},{8,10},{9,11},{10,... | collective-permute-start | bytes 589832 | tf_op jit(solution)/shard_map/ppermute | solution.py:230
  29.3 4.2 %collective-permute-start.11 = (bf16[32,1536]{1,0:T(8,128)(2,1)S(1)}, bf16[32,1536]{1,0:T(8,128)(2,1)S(1)}, u32[]{:S(2)}, u32[]{:S(2)}) collective-permute-start(bf16[32,1536]{1,0:T(8,128)(2,1)S(1)} %get-tuple-element.37.refs_5_.h0_ref), channel_id=1, source_target_pairs={{0,1},{1,0},{2,3},{3,2},{4,5},{5,4},{6,7},{7,6},{8,9},{9,8},{10,11... | collective-permute-start | bytes 294920 | tf_op jit(solution)/shard_map/ppermute | solution.py:230
  34.2 1.5 %collective-permute-start.12 = (bf16[32,3072]{1,0:T(8,128)(2,1)S(1)}, bf16[32,3072]{1,0:T(8,128)(2,1)S(1)}, u32[]{:S(2)}, u32[]{:S(2)}) collective-permute-start(bf16[32,3072]{1,0:T(8,128)(2,1)S(1)} %pre_grad.1.p0_ref), channel_id=1, source_target_pairs={{0,1},{1,0},{2,3},{3,2},{4,5},{5,4},{6,7},{7,6},{8,9},{9,8},{10,11... | collective-permute-start | bytes 589832 | tf_op jit(solution)/shard_map/ppermute | solution.py:230
  40.4 4.9 %collective-permute-start.13 = (bf16[32,1536]{1,0:T(8,128)(2,1)S(1)}, bf16[32,1536]{1,0:T(8,128)(2,1)S(1)}, u32[]{:S(2)}, u32[]{:S(2)}) collective-permute-start(bf16[32,1536]{1,0:T(8,128)(2,1)S(1)} %get-tuple-element.41.refs_3_), channel_id=1, source_target_pairs={{0,4},{4,0},{8,12},{12,8},{16,20},{20,16},{24,28},{28,24},{1,5},{5... | collective-permute-start | bytes 294920 | tf_op jit(solution)/shard_map/ppermute | solution.py:227
  45.4 10.1 %collective-permute-start.16 = (f32[8,1536]{1,0:T(8,128)S(1)}, f32[8,1536]{1,0:T(8,128)S(1)}, u32[]{:S(2)}, u32[]{:S(2)}) collective-permute-start(f32[8,1536]{1,0:T(8,128)S(1)} %get-tuple-element.48), channel_id=1, source_target_pairs={{0,24},{4,28},{8,16},{12,20},{16,8},{20,12},{24,0},{28,4},{1,25},{... | collective-permute-start | bytes 147464 | tf_op jit(solution)/shard_map/ppermute | solution.py:227
  48.6 6.8 %collective-permute-start.15 = (f32[8,1536]{1,0:T(8,128)S(1)}, f32[8,1536]{1,0:T(8,128)S(1)}, u32[]{:S(2)}, u32[]{:S(2)}) collective-permute-start(f32[8,1536]{1,0:T(8,128)S(1)} %get-tuple-element.49), channel_id=1, source_target_pairs={{0,16},{4,20},{8,24},{12,28},{16,0},{20,4},{24,8},{28,12},{1,17},{... | collective-permute-start | bytes 147464 | tf_op jit(solution)/shard_map/ppermute | solution.py:227
  48.6 6.8 %collective-permute-start.14 = (f32[8,1536]{1,0:T(8,128)S(1)}, f32[8,1536]{1,0:T(8,128)S(1)}, u32[]{:S(2)}, u32[]{:S(2)}) collective-permute-start(f32[8,1536]{1,0:T(8,128)S(1)} %get-tuple-element.50), channel_id=1, source_target_pairs={{0,8},{4,12},{8,0},{12,4},{16,24},{20,28},{24,16},{28,20},{1,9},{5... | collective-permute-start | bytes 147464 | tf_op jit(solution)/shard_map/ppermute | solution.py:227

commit v6 on v5

--- a/solution.py
+++ b/solution.py
@@ -207,14 +207,21 @@
 
 
 def up_kernel(first, last, rows, p_ref, near_ref, far_ref, *refs):
-    out_ref, done_ref, buf, sems = refs[-4:]
-    done_ref[...] = jnp.zeros_like(done_ref)
+    if first == 0:
+        bias_ref, out_ref, done_ref, bias_out, buf, sems, bias_sem = refs
+        done_ref[...] = jnp.zeros_like(done_ref)
+        bias_copy = pltpu.make_async_copy(bias_ref, bias_out, bias_sem)
+        bias_copy.start()
+    else:
+        _, out_ref, buf, sems = refs
     p = p_ref[...]
 
     def make(at):
         return outer(jnp.concatenate([near_ref[:, at : at + rows], far_ref[:, at : at + rows]], axis=0), p)
 
     write_tiles(first, last, rows, make, out_ref, buf, sems)
+    if first == 0:
+        bias_copy.wait()
 
 
 def on_device(rows, cols, normed, out_grad, up_weight, up_bias, down_weight):
@@ -296,15 +303,16 @@
     part_t = jax.ShapeDtypeStruct((half, feats), F32)
     rt = divisor(units - cut, 256)
     tiles = (units - cut) // rt
-    down_grad, keep_in, send_in, bias_grad, pg_all = call(
+    down_grad, keep_in, send_in, bias_sum, pg_all = call(
         functools.partial(down_in_kernel, cut, tiles, rt), "down_last_in",
         (
-            down_t, part_t, jax.ShapeDtypeStruct((half, feats), BF16), jax.ShapeDtypeStruct((1, units), F32),
+            down_t, part_t, jax.ShapeDtypeStruct((half, feats), BF16), pltpu.VMEM((1, units), F32),
             jax.ShapeDtypeStruct((2 * half, units), BF16),
         ),
         (core, pg, pg_far, up_weight, acts[1], acts_far[1], g_near, g_far, down_half),
         in_specs=[smem()] + [vmem()] * 7 + [anywhere()], out_specs=(anywhere(),) + (vmem(),) * 4, limit=24,
-        scratch=[pltpu.VMEM((tiles, rt, feats), F32), pltpu.SemaphoreType.DMA((tiles,))], aliases={8: 0},
+        scratch=[pltpu.VMEM((tiles, rt, feats), F32), pltpu.SemaphoreType.DMA((tiles,))],
+        aliases={8: 0},
     )
     far_in = row_swap(send_in, 1)
 
@@ -313,15 +321,16 @@
     first = max(1, dtiles * UP_FIRST // 12)
     up_t = jax.ShapeDtypeStruct((feats, units), F32)
     slots = [pltpu.VMEM((SLOTS, dt, units), F32), pltpu.SemaphoreType.DMA((SLOTS,))]
-    up_half, wrote = call(
-        functools.partial(up_kernel, 0, first, dt), "up_first", (up_t, token_t), (pg_all, x_near, x_far),
-        in_specs=[vmem()] * 3, out_specs=(anywhere(), vmem()), scratch=slots, after=(send_in,),
+    up_half, wrote, bias_grad = call(
+        functools.partial(up_kernel, 0, first, dt), "up_first", (up_t, token_t, jax.ShapeDtypeStruct((1, units), F32)),
+        (pg_all, x_near, x_far, bias_sum), in_specs=[vmem()] * 4, out_specs=(anywhere(), vmem(), anywhere()),
+        scratch=slots + [pltpu.SemaphoreType.DMA(())], after=(send_in,),
     )
     share = call(sum_kernel, "share", part_t, (keep_in, far_in), after=(wrote,)).reshape(blocks, mine, feats)
     terms = [share[0]] + [row_swap(share[k // 2], k) for k in range(2, rows, 2)]
-    up_grad, _ = call(
-        functools.partial(up_kernel, first, dtiles, dt), "up_last", (up_t, token_t), (pg_all, x_near, x_far, up_half),
-        in_specs=[vmem()] * 3 + [anywhere()], out_specs=(anywhere(), vmem()), scratch=slots, aliases={3: 0}, after=(share,),
+    up_grad = call(
+        functools.partial(up_kernel, first, dtiles, dt), "up_last", up_t, (pg_all, x_near, x_far, up_half),
+        in_specs=[vmem()] * 3 + [anywhere()], out_specs=anywhere(), scratch=slots, aliases={3: 0}, after=(share,),
     )
     in_grad = tree_sum(terms).astype(BF16)
     return (in_grad, up_grad, bias_grad.reshape(units), down_grad)

time: 56.3 us -> 55.2 us (0.980)
  Pallas kernels: 30.7 us -> 29.5 us
    pallas_call x16, Pallas kernels: 30.7 us -> 29.5 us  [call(): pl.pallas_call(body, out_shape=out_shape, in_specs=in_specs + [anywhere()...]
  transfers between devices with their start and end apart: 17 -> 17, of which waited for: 7 -> 7; matrix products, arithmetic and copies ran while one was open for 0% -> 0% of each run, Pallas kernels for 42% -> 41%
where the time goes in v6:
time: 55.2 us; the launch traced here: 54.9 us
  Pallas kernels  29.5 us (53%)
  starting transfers between devices  18.3 us (33%)
  waiting for transfers between devices  5.56 us (10%)
  between operations  0.86 us (2%)
  other arithmetic  0.66 us (1%)
    pallas_call x16, Pallas kernels, call(): pl.pallas_call(body, out_shape=out_shape, in_specs=in_specs + [anywhere()...  29.5 us
    ppermute x8, starting transfers between devices, row_swap(): return lax.ppermute(x, 'row', [(i, i ^ k) for i in range(rows)])  13.3 us
    ppermute x9, starting transfers between devices, col_swap(): return lax.ppermute(x, 'col', [(i, i ^ k) for i in range(cols)])  4.93 us
    ppermute x9, waiting for transfers between devices, col_swap(): return lax.ppermute(x, 'col', [(i, i ^ k) for i in range(cols)])  4.15 us
    ppermute x8, waiting for transfers between devices, row_swap(): return lax.ppermute(x, 'row', [(i, i ^ k) for i in range(rows)])  1.41 us
  transfers between devices with their start and end apart: 17, of which 7 were waited for; matrix products, arithmetic and copies ran while one was open for 0% of the time, Pallas kernels for 41%

profile of v6, /device:TPU:0, one launch (start us, length us, event | category | flops | bytes accessed | tf_op | source)
XLA Modules:
  0.0 54.9 jit_solution(14456644395248915914)
XLA Ops:
  0.6 0.8 %stack.21 = bf16[2,8,1536]{2,1,0:T(8,128)(2,1)S(1)} custom-call(bf16[8,1536]{1,0:T(8,128)(2,1)} %a_ref.1, bf16[8,1536]{1,0:T(8,128)(2,1)} %b_ref.1), custom_call_target="tpu_custom_call" | custom-call | tf_op jit(solution)/shard_map/stack/pallas_call | solution.py:41
  1.4 5.1 %collective-permute-start.2 = (bf16[2,8,1536]{2,1,0:T(8,128)(2,1)S(1)}, bf16[2,8,1536]{2,1,0:T(8,128)(2,1)S(1)}, u32[]{:S(2)}, u32[]{:S(2)}) collective-permute-start(bf16[2,8,1536]{2,1,0:T(8,128)(2,1)S(1)} %stack.21), channel_id=1, source_target_pairs={{0,24},{4,28},{8,16},{12,20},{16,8},{20,12},{24,0},{28,4},{1,25},{... | collective-permute-start | bytes 147464 | tf_op jit(solution)/shard_map/ppermute | solution.py:234
  6.5 0.6 %collective-permute-start = (bf16[2,8,1536]{2,1,0:T(8,128)(2,1)S(1)}, bf16[2,8,1536]{2,1,0:T(8,128)(2,1)S(1)}, u32[]{:S(2)}, u32[]{:S(2)}) collective-permute-start(bf16[2,8,1536]{2,1,0:T(8,128)(2,1)S(1)} %stack.21), channel_id=1, source_target_pairs={{0,8},{4,12},{8,0},{12,4},{16,24},{20,28},{24,16},{28,20},{1,9},{5... | collective-permute-start | bytes 147464 | tf_op jit(solution)/shard_map/ppermute | solution.py:234
  7.2 3.7 %load_up.1.refs_3_.w_ref = bf16[1536,3072]{1,0:T(8,128)(2,1)S(1)} custom-call(bf16[1536,3072]{1,0:T(8,128)(2,1)} %w_ref.1), custom_call_target="tpu_custom_call" | custom-call | tf_op jit(solution)/shard_map/load_up/pallas_call | solution.py:41
  10.9 0.6 %collective-permute-done.1 = bf16[2,8,1536]{2,1,0:T(8,128)(2,1)S(1)} collective-permute-done((bf16[2,8,1536]{2,1,0:T(8,128)(2,1)S(1)}, bf16[2,8,1536]{2,1,0:T(8,128)(2,1)S(1)}, u32[]{:S(2)}, u32[]{:S(2)}) %collective-permute-start.1) | collective-permute-done | bytes 49184 | tf_op jit(solution)/shard_map/ppermute | solution.py:234
  11.6 1.6 %collective-permute-start.3 = (bf16[2,32,1536]{2,1,0:T(8,128)(2,1)S(1)}, bf16[2,32,1536]{2,1,0:T(8,128)(2,1)S(1)}, u32[]{:S(2)}, u32[]{:S(2)}) collective-permute-start(bf16[2,32,1536]{2,1,0:T(8,128)(2,1)S(1)} %copy_bitcast_fusion.refs_1_), channel_id=1, source_target_pairs={{0,4},{4,0},{8,12},{12,8},{16,20},{20,16},{24,28},{28,24},{1,5},{5... | collective-permute-start | bytes 589832 | tf_op jit(solution)/shard_map/ppermute | solution.py:234
  13.1 3.7 %load_down.1.w_ref.refs_4_.refs_3_ = bf16[3072,1536]{1,0:T(8,128)(2,1)S(1)} custom-call(bf16[3072,1536]{1,0:T(8,128)(2,1)} %refs_0_.1, bf16[2,32,1536]{2,1,0:T(8,128)(2,1)S(1)} %copy_bitcast_fusion.refs_1_), custom_call_target="tpu_custom_call" | custom-call | tf_op jit(solution)/shard_map/load_down/pallas_call | solution.py:41
  17.4 1.7 %pre.1 = (f32[32,3072]{1,0:T(8,128)S(1)}, f32[32,3072]{1,0:T(8,128)S(1)}) custom-call(s32[1]{0:T(128)} %bitcast.core_ref.refs_0_, bf16[32,1536]{1,0:T(8,128)(2,1)S(1)} %get-tuple-element.53.refs_1_, bf16[32,1536]{1,0:T(8,128)(2,1)S(1)} %get-tuple-element.51.refs_2_, bf16[1536,3072]{1,0:T(8,128)(2,1)S(1)} %load_up.1.refs_3_.w_ref, ...), custom_call_target="tpu_custom_call" | custom-call | tf_op jit(solution)/shard_map/pre/pallas_call | solution.py:41
  19.2 1.9 %hid.2 = (f32[32,2048]{1,0:T(8,128)S(1)}, f32[32,2048]{1,0:T(8,128)S(1)}) custom-call(s32[1]{0:T(128)} %bitcast.core_ref.refs_0_, bf16[32,1536]{1,0:T(8,128)(2,1)S(1)} %get-tuple-element.54.near_ref.refs_1_.refs_3_, bf16[32,1536]{1,0:T(8,128)(2,1)S(1)} %get-tuple-element.52.far_ref.refs_2_.refs_4_, bf16[3072,1536]{1,0:T(8,128)(2,1)S(1)} %load_down.1.w_ref.refs_4_.refs_3_), custom_call_target="tpu_custom_call" | custom-call | tf_op jit(solution)/shard_map/hid/pallas_call | solution.py:41
  21.2 1.6 %collective-permute-start.8 = (bf16[32,1536]{1,0:T(8,128)(2,1)S(1)}, bf16[32,1536]{1,0:T(8,128)(2,1)S(1)}, u32[]{:S(2)}, u32[]{:S(2)}) collective-permute-start(bf16[32,1536]{1,0:T(8,128)(2,1)S(1)} %get-tuple-element.30.refs_4_.refs_0_), channel_id=1, source_target_pairs={{0,2},{1,3},{2,0},{3,1},{4,6},{5,7},{6,4},{7,5},{8,10},{9,11},{10,... | collective-permute-start | bytes 294920 | tf_op jit(solution)/shard_map/ppermute | solution.py:237
  23.1 1.0 %hid.3 = (f32[32,1024]{1,0:T(8,128)S(1)}, f32[32,1024]{1,0:T(8,128)S(1)}) custom-call(s32[1]{0:T(128)} %bitcast.core_ref.refs_0_, bf16[32,1536]{1,0:T(8,128)(2,1)S(1)} %get-tuple-element.54.near_ref.refs_1_.refs_3_, bf16[32,1536]{1,0:T(8,128)(2,1)S(1)} %get-tuple-element.52.far_ref.refs_2_.refs_4_, bf16[3072,1536]{1,0:T(8,128)(2,1)S(1)} %load_down.1.w_ref.refs_4_.refs_3_, ...), custom_call_target="tpu_custom_call" | custom-call | tf_op jit(solution)/shard_map/hid/pallas_call | solution.py:41
  24.1 0.9 %collective-permute-start.9 = (bf16[32,1536]{1,0:T(8,128)(2,1)S(1)}, bf16[32,1536]{1,0:T(8,128)(2,1)S(1)}, u32[]{:S(2)}, u32[]{:S(2)}) collective-permute-start(bf16[32,1536]{1,0:T(8,128)(2,1)S(1)} %get-tuple-element.31.refs_5_.refs_0_), channel_id=1, source_target_pairs={{0,2},{1,3},{2,0},{3,1},{4,6},{5,7},{6,4},{7,5},{8,10},{9,11},{10,... | collective-permute-start | bytes 294920 | tf_op jit(solution)/shard_map/ppermute | solution.py:237
  25.0 1.5 %collective-permute-done.8.refs_1_ = bf16[32,1536]{1,0:T(8,128)(2,1)S(1)} collective-permute-done((bf16[32,1536]{1,0:T(8,128)(2,1)S(1)}, bf16[32,1536]{1,0:T(8,128)(2,1)S(1)}, u32[]{:S(2)}, u32[]{:S(2)}) %collective-permute-start.8) | collective-permute-done | bytes 98336 | tf_op jit(solution)/shard_map/ppermute | solution.py:237
  26.7 1.9 %collective-permute-start.7 = (bf16[32,3072]{1,0:T(8,128)(2,1)S(1)}, bf16[32,3072]{1,0:T(8,128)(2,1)S(1)}, u32[]{:S(2)}, u32[]{:S(2)}) collective-permute-start(bf16[32,3072]{1,0:T(8,128)(2,1)S(1)} %add_hid.1.refs_0_), channel_id=1, source_target_pairs={{0,2},{1,3},{2,0},{3,1},{4,6},{5,7},{6,4},{7,5},{8,10},{9,11},{10,... | collective-permute-start | bytes 589832 | tf_op jit(solution)/shard_map/ppermute | solution.py:237
  29.4 4.1 %down_first.1 = (f32[3072,1536]{1,0:T(8,128)}, f32[8,128]{1,0:T(8,128)S(1)}) custom-call(s32[1]{0:T(128)} %bitcast.core_ref.refs_0_, bf16[32,1536]{1,0:T(8,128)(2,1)S(1)} %get-tuple-element.36.refs_1_, bf16[32,1536]{1,0:T(8,128)(2,1)S(1)} %collective-permute-done.10.refs_2_, bf16[32,1536]{1,0:T(8,128)(2,1)S(1)} %get-tuple-element.54.near_ref.refs_1_.refs_3_, ...), custom_call_target="tpu_custom_call" | custom-call | tf_op jit(solution)/shard_map/down_first/pallas_call | solution.py:41
  33.5 0.7 %collective-permute-done.7.refs_1_ = bf16[32,3072]{1,0:T(8,128)(2,1)S(1)} collective-permute-done((bf16[32,3072]{1,0:T(8,128)(2,1)S(1)}, bf16[32,3072]{1,0:T(8,128)(2,1)S(1)}, u32[]{:S(2)}, u32[]{:S(2)}) %collective-permute-start.7) | collective-permute-done | bytes 196640 | tf_op jit(solution)/shard_map/ppermute | solution.py:237
  34.3 1.4 %collective-permute-done.12.p1_ref = bf16[32,3072]{1,0:T(8,128)(2,1)S(1)} collective-permute-done((bf16[32,3072]{1,0:T(8,128)(2,1)S(1)}, bf16[32,3072]{1,0:T(8,128)(2,1)S(1)}, u32[]{:S(2)}, u32[]{:S(2)}) %collective-permute-start.12) | collective-permute-done | bytes 196640 | tf_op jit(solution)/shard_map/ppermute | solution.py:237
  35.7 4.1 %down_last_in.1 = (f32[3072,1536]{1,0:T(8,128)}, f32[32,1536]{1,0:T(8,128)S(1)}, bf16[32,1536]{1,0:T(8,128)(2,1)S(1)}, f32[1,3072]{1,0:T(1,128)S(1)}, bf16[64,3072]{1,0:T(8,128)(2,1)S(1)}) custom-call(s32[1]{0:T(128)} %bitcast.core_ref.refs_0_, bf16[32,3072]{1,0:T(8,128)(2,1)S(1)} %pre_grad.1.p0_ref, ...), custom_call_target="tpu_custom_call", output_to_operand_aliasing={{0}: (8, {})} | custom-call | tf_op jit(solution)/shard_map/down_last_in/pallas_call | solution.py:41
  39.8 1.6 %collective-permute-start.13 = (bf16[32,1536]{1,0:T(8,128)(2,1)S(1)}, bf16[32,1536]{1,0:T(8,128)(2,1)S(1)}, u32[]{:S(2)}, u32[]{:S(2)}) collective-permute-start(bf16[32,1536]{1,0:T(8,128)(2,1)S(1)} %get-tuple-element.41.refs_4_), channel_id=1, source_target_pairs={{0,4},{4,0},{8,12},{12,8},{16,20},{20,16},{24,28},{28,24},{1,5},{5... | collective-permute-start | bytes 294920 | tf_op jit(solution)/shard_map/ppermute | solution.py:234
  41.4 3.1 %up_first.1 = (f32[1536,3072]{1,0:T(8,128)}, f32[8,128]{1,0:T(8,128)S(1)}, f32[1,3072]{1,0:T(1,128)}) custom-call(bf16[64,3072]{1,0:T(8,128)(2,1)S(1)} %get-tuple-element.42.refs_0_, bf16[32,1536]{1,0:T(8,128)(2,1)S(1)} %get-tuple-element.53.refs_1_, bf16[32,1536]{1,0:T(8,128)(2,1)S(1)} %get-tuple-element.51.refs_2_, ...), custom_call_target="tpu_custom_call" | custom-call | tf_op jit(solution)/shard_map/up_first/pallas_call | solution.py:41
  44.8 3.2 %collective-permute-start.16 = (f32[8,1536]{1,0:T(8,128)S(1)}, f32[8,1536]{1,0:T(8,128)S(1)}, u32[]{:S(2)}, u32[]{:S(2)}) collective-permute-start(f32[8,1536]{1,0:T(8,128)S(1)} %get-tuple-element.48), channel_id=1, source_target_pairs={{0,24},{4,28},{8,16},{12,20},{16,8},{20,12},{24,0},{28,4},{1,25},{... | collective-permute-start | bytes 147464 | tf_op jit(solution)/shard_map/ppermute | solution.py:234
  48.0 1.2 %collective-permute-start.14 = (f32[8,1536]{1,0:T(8,128)S(1)}, f32[8,1536]{1,0:T(8,128)S(1)}, u32[]{:S(2)}, u32[]{:S(2)}) collective-permute-start(f32[8,1536]{1,0:T(8,128)S(1)} %get-tuple-element.50), channel_id=1, source_target_pairs={{0,8},{4,12},{8,0},{12,4},{16,24},{20,28},{24,16},{28,20},{1,9},{5... | collective-permute-start | bytes 147464 | tf_op jit(solution)/shard_map/ppermute | solution.py:234
  49.2 5.0 %up_last.1 = f32[1536,3072]{1,0:T(8,128)} custom-call(bf16[64,3072]{1,0:T(8,128)(2,1)S(1)} %get-tuple-element.42.refs_0_, bf16[32,1536]{1,0:T(8,128)(2,1)S(1)} %get-tuple-element.53.refs_1_, bf16[32,1536]{1,0:T(8,128)(2,1)S(1)} %get-tuple-element.51.refs_2_, f32[1536,3072]{1,0:T(8,128)} %get-tuple-element.45.refs_3_, ...), custom_call_target="tpu_custom_call", output_to_operand_aliasing={{}: (3, {})} | custom-call | tf_op jit(solution)/shard_map/up_last/pallas_call | solution.py:41
  54.3 0.6 %fusion.1 = bf16[8,1536]{1,0:T(8,128)(2,1)} fusion(f32[8,1536]{1,0:T(8,128)S(1)} %collective-permute-done.14, f32[32,1536]{1,0:T(8,128)S(1)} %share.1, f32[8,1536]{1,0:T(8,128)S(1)} %collective-permute-done.15, f32[8,1536]{1,0:T(8,128)S(1)} %collective-permute-done.16), kind=kLoop, calls=%fused_computation.8 | loop fusion | flops 49152 | bytes 221184 | tf_op jit(solution)/shard_map/convert_element_type | solution.py:335
  (35 shorter events, 2.4 us)
Async XLA Ops:
  1.4 9.5 %collective-permute-start.2 = (bf16[2,8,1536]{2,1,0:T(8,128)(2,1)S(1)}, bf16[2,8,1536]{2,1,0:T(8,128)(2,1)S(1)}, u32[]{:S(2)}, u32[]{:S(2)}) collective-permute-start(bf16[2,8,1536]{2,1,0:T(8,128)(2,1)S(1)} %stack.21), channel_id=1, source_target_pairs={{0,24},{4,28},{8,16},{12,20},{16,8},{20,12},{24,0},{28,4},{1,25},{... | collective-permute-start | bytes 147464 | tf_op jit(solution)/shard_map/ppermute | solution.py:234
  6.5 5.0 %collective-permute-start.1 = (bf16[2,8,1536]{2,1,0:T(8,128)(2,1)S(1)}, bf16[2,8,1536]{2,1,0:T(8,128)(2,1)S(1)}, u32[]{:S(2)}, u32[]{:S(2)}) collective-permute-start(bf16[2,8,1536]{2,1,0:T(8,128)(2,1)S(1)} %stack.21), channel_id=1, source_target_pairs={{0,16},{4,20},{8,24},{12,28},{16,0},{20,4},{24,8},{28,12},{1,17},{... | collective-permute-start | bytes 147464 | tf_op jit(solution)/shard_map/ppermute | solution.py:234
  6.5 5.0 %collective-permute-start = (bf16[2,8,1536]{2,1,0:T(8,128)(2,1)S(1)}, bf16[2,8,1536]{2,1,0:T(8,128)(2,1)S(1)}, u32[]{:S(2)}, u32[]{:S(2)}) collective-permute-start(bf16[2,8,1536]{2,1,0:T(8,128)(2,1)S(1)} %stack.21), channel_id=1, source_target_pairs={{0,8},{4,12},{8,0},{12,4},{16,24},{20,28},{24,16},{28,20},{1,9},{5... | collective-permute-start | bytes 147464 | tf_op jit(solution)/shard_map/ppermute | solution.py:234
  11.6 5.8 %collective-permute-start.3 = (bf16[2,32,1536]{2,1,0:T(8,128)(2,1)S(1)}, bf16[2,32,1536]{2,1,0:T(8,128)(2,1)S(1)}, u32[]{:S(2)}, u32[]{:S(2)}) collective-permute-start(bf16[2,32,1536]{2,1,0:T(8,128)(2,1)S(1)} %copy_bitcast_fusion.refs_1_), channel_id=1, source_target_pairs={{0,4},{4,0},{8,12},{12,8},{16,20},{20,16},{24,28},{28,24},{1,5},{5... | collective-permute-start | bytes 589832 | tf_op jit(solution)/shard_map/ppermute | solution.py:234
  19.2 1.9 %collective-permute-start.4 = (f32[32,3072]{1,0:T(8,128)S(1)}, f32[32,3072]{1,0:T(8,128)S(1)}, u32[]{:S(2)}, u32[]{:S(2)}) collective-permute-start(f32[32,3072]{1,0:T(8,128)S(1)} %get-tuple-element.28), channel_id=1, source_target_pairs={{0,1},{1,0},{2,3},{3,2},{4,5},{5,4},{6,7},{7,6},{8,9},{9,8},{10,11... | collective-permute-start | bytes 1179656 | tf_op jit(solution)/shard_map/ppermute | solution.py:237
  21.1 1.7 %copy-start = (bf16[3072]{0:T(1024)(128)(2,1)S(1)}, bf16[3072]{0:T(1024)(128)(2,1)}, u32[]{:S(2)}) copy-start(bf16[3072]{0:T(1024)(128)(2,1)} %param.8) | copy-start | bytes 18436
  21.2 5.3 %collective-permute-start.8 = (bf16[32,1536]{1,0:T(8,128)(2,1)S(1)}, bf16[32,1536]{1,0:T(8,128)(2,1)S(1)}, u32[]{:S(2)}, u32[]{:S(2)}) collective-permute-start(bf16[32,1536]{1,0:T(8,128)(2,1)S(1)} %get-tuple-element.30.refs_4_.refs_0_), channel_id=1, source_target_pairs={{0,2},{1,3},{2,0},{3,1},{4,6},{5,7},{6,4},{7,5},{8,10},{9,11},{10,... | collective-permute-start | bytes 294920 | tf_op jit(solution)/shard_map/ppermute | solution.py:237
  22.8 3.9 %collective-permute-start.5 = (f32[32,2048]{1,0:T(8,128)S(1)}, f32[32,2048]{1,0:T(8,128)S(1)}, u32[]{:S(2)}, u32[]{:S(2)}) collective-permute-start(f32[32,2048]{1,0:T(8,128)S(1)} %get-tuple-element.29.refs_2_), channel_id=1, source_target_pairs={{0,1},{1,0},{2,3},{3,2},{4,5},{5,4},{6,7},{7,6},{8,9},{9,8},{10,11... | collective-permute-start | bytes 786440 | tf_op jit(solution)/shard_map/ppermute | solution.py:237
  24.1 5.1 %collective-permute-start.9 = (bf16[32,1536]{1,0:T(8,128)(2,1)S(1)}, bf16[32,1536]{1,0:T(8,128)(2,1)S(1)}, u32[]{:S(2)}, u32[]{:S(2)}) collective-permute-start(bf16[32,1536]{1,0:T(8,128)(2,1)S(1)} %get-tuple-element.31.refs_5_.refs_0_), channel_id=1, source_target_pairs={{0,2},{1,3},{2,0},{3,1},{4,6},{5,7},{6,4},{7,5},{8,10},{9,11},{10,... | collective-permute-start | bytes 294920 | tf_op jit(solution)/shard_map/ppermute | solution.py:237
  25.0 1.7 %collective-permute-start.6 = (f32[32,1024]{1,0:T(8,128)S(1)}, f32[32,1024]{1,0:T(8,128)S(1)}, u32[]{:S(2)}, u32[]{:S(2)}) collective-permute-start(f32[32,1024]{1,0:T(8,128)S(1)} %get-tuple-element.33), channel_id=1, source_target_pairs={{0,1},{1,0},{2,3},{3,2},{4,5},{5,4},{6,7},{7,6},{8,9},{9,8},{10,11... | collective-permute-start | bytes 393224 | tf_op jit(solution)/shard_map/ppermute | solution.py:237
  26.6 2.8 %collective-permute-start.10 = (bf16[32,1536]{1,0:T(8,128)(2,1)S(1)}, bf16[32,1536]{1,0:T(8,128)(2,1)S(1)}, u32[]{:S(2)}, u32[]{:S(2)}) collective-permute-start(bf16[32,1536]{1,0:T(8,128)(2,1)S(1)} %get-tuple-element.36.refs_1_), channel_id=1, source_target_pairs={{0,1},{1,0},{2,3},{3,2},{4,5},{5,4},{6,7},{7,6},{8,9},{9,8},{10,11... | collective-permute-start | bytes 294920 | tf_op jit(solution)/shard_map/ppermute | solution.py:237
  26.7 7.5 %collective-permute-start.7 = (bf16[32,3072]{1,0:T(8,128)(2,1)S(1)}, bf16[32,3072]{1,0:T(8,128)(2,1)S(1)}, u32[]{:S(2)}, u32[]{:S(2)}) collective-permute-start(bf16[32,3072]{1,0:T(8,128)(2,1)S(1)} %add_hid.1.refs_0_), channel_id=1, source_target_pairs={{0,2},{1,3},{2,0},{3,1},{4,6},{5,7},{6,4},{7,5},{8,10},{9,11},{10,... | collective-permute-start | bytes 589832 | tf_op jit(solution)/shard_map/ppermute | solution.py:237
  29.3 4.2 %collective-permute-start.11 = (bf16[32,1536]{1,0:T(8,128)(2,1)S(1)}, bf16[32,1536]{1,0:T(8,128)(2,1)S(1)}, u32[]{:S(2)}, u32[]{:S(2)}) collective-permute-start(bf16[32,1536]{1,0:T(8,128)(2,1)S(1)} %get-tuple-element.37.refs_5_.h0_ref), channel_id=1, source_target_pairs={{0,1},{1,0},{2,3},{3,2},{4,5},{5,4},{6,7},{7,6},{8,9},{9,8},{10,11... | collective-permute-start | bytes 294920 | tf_op jit(solution)/shard_map/ppermute | solution.py:237
  34.2 1.5 %collective-permute-start.12 = (bf16[32,3072]{1,0:T(8,128)(2,1)S(1)}, bf16[32,3072]{1,0:T(8,128)(2,1)S(1)}, u32[]{:S(2)}, u32[]{:S(2)}) collective-permute-start(bf16[32,3072]{1,0:T(8,128)(2,1)S(1)} %pre_grad.1.p0_ref), channel_id=1, source_target_pairs={{0,1},{1,0},{2,3},{3,2},{4,5},{5,4},{6,7},{7,6},{8,9},{9,8},{10,11... | collective-permute-start | bytes 589832 | tf_op jit(solution)/shard_map/ppermute | solution.py:237
  39.8 4.9 %collective-permute-start.13 = (bf16[32,1536]{1,0:T(8,128)(2,1)S(1)}, bf16[32,1536]{1,0:T(8,128)(2,1)S(1)}, u32[]{:S(2)}, u32[]{:S(2)}) collective-permute-start(bf16[32,1536]{1,0:T(8,128)(2,1)S(1)} %get-tuple-element.41.refs_4_), channel_id=1, source_target_pairs={{0,4},{4,0},{8,12},{12,8},{16,20},{20,16},{24,28},{28,24},{1,5},{5... | collective-permute-start | bytes 294920 | tf_op jit(solution)/shard_map/ppermute | solution.py:234
  44.8 9.5 %collective-permute-start.16 = (f32[8,1536]{1,0:T(8,128)S(1)}, f32[8,1536]{1,0:T(8,128)S(1)}, u32[]{:S(2)}, u32[]{:S(2)}) collective-permute-start(f32[8,1536]{1,0:T(8,128)S(1)} %get-tuple-element.48), channel_id=1, source_target_pairs={{0,24},{4,28},{8,16},{12,20},{16,8},{20,12},{24,0},{28,4},{1,25},{... | collective-permute-start | bytes 147464 | tf_op jit(solution)/shard_map/ppermute | solution.py:234
  48.0 6.2 %collective-permute-start.15 = (f32[8,1536]{1,0:T(8,128)S(1)}, f32[8,1536]{1,0:T(8,128)S(1)}, u32[]{:S(2)}, u32[]{:S(2)}) collective-permute-start(f32[8,1536]{1,0:T(8,128)S(1)} %get-tuple-element.49), channel_id=1, source_target_pairs={{0,16},{4,20},{8,24},{12,28},{16,0},{20,4},{24,8},{28,12},{1,17},{... | collective-permute-start | bytes 147464 | tf_op jit(solution)/shard_map/ppermute | solution.py:234
  48.0 6.2 %collective-permute-start.14 = (f32[8,1536]{1,0:T(8,128)S(1)}, f32[8,1536]{1,0:T(8,128)S(1)}, u32[]{:S(2)}, u32[]{:S(2)}) collective-permute-start(f32[8,1536]{1,0:T(8,128)S(1)} %get-tuple-element.50), channel_id=1, source_target_pairs={{0,8},{4,12},{8,0},{12,4},{16,24},{20,28},{24,16},{28,20},{1,9},{5... | collective-permute-start | bytes 147464 | tf_op jit(solution)/shard_map/ppermute | solution.py:234

commit v7 on v6

--- a/solution.py
+++ b/solution.py
@@ -153,13 +153,33 @@
         s = (t - first) % SLOTS
         return pltpu.make_async_copy(buf.at[s], out_ref.at[pl.ds(t * rows, rows), :], sems.at[s])
 
-    for t in range(first, last):
+    width = out_ref.shape[1]
+    cut = width // 4 // 128 * 128 or 128
+    early = pltpu.make_async_copy(
+        buf.at[0, :, pl.ds(0, cut)], out_ref.at[pl.ds(first * rows, rows), pl.ds(0, cut)], sems.at[SLOTS]
+    )
+    rest = pltpu.make_async_copy(
+        buf.at[0, :, pl.ds(cut, width - cut)], out_ref.at[pl.ds(first * rows, rows), pl.ds(cut, width - cut)], sems.at[0]
+    )
+    buf[0, :, :cut] = make(first * rows, 0, cut)
+    early.start()
+    buf[0, :, cut:] = make(first * rows, cut, width)
+    rest.start()
+
+    def finish(t):
+        if t == first:
+            early.wait()
+            rest.wait()
+        else:
+            copy(t).wait()
+
+    for t in range(first + 1, last):
         if t - first >= SLOTS:
-            copy(t - SLOTS).wait()
-        buf[(t - first) % SLOTS] = make(t * rows)
+            finish(t - SLOTS)
+        buf[(t - first) % SLOTS] = make(t * rows, 0, width)
         copy(t).start()
     for t in range(max(first, last - SLOTS), last):
-        copy(t).wait()
+        finish(t)
 
 
 def outer(a, b):
@@ -171,8 +191,8 @@
     done_ref[...] = jnp.zeros_like(done_ref)
     g = local_tokens(core_ref[0], near_ref, far_ref)
 
-    def make(at):
-        return outer(jnp.concatenate([h0_ref[:, at : at + rows], h1_ref[:, at : at + rows]], axis=0), g)
+    def make(at, lo, hi):
+        return outer(jnp.concatenate([h0_ref[:, at : at + rows], h1_ref[:, at : at + rows]], axis=0), g[:, lo:hi])
 
     write_tiles(first, last, rows, make, out_ref, buf, sems)
 
@@ -216,8 +236,9 @@
         _, out_ref, buf, sems = refs
     p = p_ref[...]
 
-    def make(at):
-        return outer(jnp.concatenate([near_ref[:, at : at + rows], far_ref[:, at : at + rows]], axis=0), p)
+    def make(at, lo, hi):
+        x = jnp.concatenate([near_ref[:, at : at + rows], far_ref[:, at : at + rows]], axis=0)
+        return outer(x, p[:, lo:hi])
 
     write_tiles(first, last, rows, make, out_ref, buf, sems)
     if first == 0:
@@ -295,7 +316,7 @@
     down_half, wrote = call(
         functools.partial(down_kernel, 0, cut // rt, rt), "down_first", (down_t, token_t),
         (core, acts[0], acts_far[0], g_near, g_far), in_specs=[smem()] + [vmem()] * 4, out_specs=(anywhere(), vmem()),
-        scratch=[pltpu.VMEM((SLOTS, rt, feats), F32), pltpu.SemaphoreType.DMA((SLOTS,))], after=(acts[1],),
+        scratch=[pltpu.VMEM((SLOTS, rt, feats), F32), pltpu.SemaphoreType.DMA((SLOTS + 1,))], after=(acts[1],),
     )
     pg = call(functools.partial(grad_kernel, cut), "pre_grad", bf_t, (*hid_parts, *slopes), after=(wrote, acts_far[1]))
     pg_far = col_swap(pg, 1)
@@ -320,7 +341,7 @@
     dtiles = feats // dt
     first = max(1, dtiles * UP_FIRST // 12)
     up_t = jax.ShapeDtypeStruct((feats, units), F32)
-    slots = [pltpu.VMEM((SLOTS, dt, units), F32), pltpu.SemaphoreType.DMA((SLOTS,))]
+    slots = [pltpu.VMEM((SLOTS, dt, units), F32), pltpu.SemaphoreType.DMA((SLOTS + 1,))]
     up_half, wrote, bias_grad = call(
         functools.partial(up_kernel, 0, first, dt), "up_first", (up_t, token_t, jax.ShapeDtypeStruct((1, units), F32)),
         (pg_all, x_near, x_far, bias_sum), in_specs=[vmem()] * 4, out_specs=(anywhere(), vmem(), anywhere()),

time: 55.2 us -> 55 us (level)
  no operation moved by 1% of the time
where the time goes in v7:
time: 55 us; the launch traced here: 54.8 us
  Pallas kernels  29.2 us (53%)
  starting transfers between devices  18.3 us (33%)
  waiting for transfers between devices  5.8 us (11%)
  between operations  0.86 us (2%)
  other arithmetic  0.66 us (1%)
    pallas_call x16, Pallas kernels, call(): pl.pallas_call(body, out_shape=out_shape, in_specs=in_specs + [anywhere()...  29.2 us
    ppermute x8, starting transfers between devices, row_swap(): return lax.ppermute(x, 'row', [(i, i ^ k) for i in range(rows)])  13.3 us
    ppermute x9, starting transfers between devices, col_swap(): return lax.ppermute(x, 'col', [(i, i ^ k) for i in range(cols)])  4.93 us
    ppermute x9, waiting for transfers between devices, col_swap(): return lax.ppermute(x, 'col', [(i, i ^ k) for i in range(cols)])  4.27 us
    ppermute x8, waiting for transfers between devices, row_swap(): return lax.ppermute(x, 'row', [(i, i ^ k) for i in range(rows)])  1.53 us
  transfers between devices with their start and end apart: 17, of which 7 were waited for; matrix products, arithmetic and copies ran while one was open for 0% of the time, Pallas kernels for 41%

profile of v7, /device:TPU:0, one launch (start us, length us, event | category | flops | bytes accessed | tf_op | source)
XLA Modules:
  0.0 54.8 jit_solution(15452664835749918868)
XLA Ops:
  0.6 0.8 %stack.21 = bf16[2,8,1536]{2,1,0:T(8,128)(2,1)S(1)} custom-call(bf16[8,1536]{1,0:T(8,128)(2,1)} %a_ref.1, bf16[8,1536]{1,0:T(8,128)(2,1)} %b_ref.1), custom_call_target="tpu_custom_call" | custom-call | tf_op jit(solution)/shard_map/stack/pallas_call | solution.py:41
  1.4 5.1 %collective-permute-start.2 = (bf16[2,8,1536]{2,1,0:T(8,128)(2,1)S(1)}, bf16[2,8,1536]{2,1,0:T(8,128)(2,1)S(1)}, u32[]{:S(2)}, u32[]{:S(2)}) collective-permute-start(bf16[2,8,1536]{2,1,0:T(8,128)(2,1)S(1)} %stack.21), channel_id=1, source_target_pairs={{0,24},{4,28},{8,16},{12,20},{16,8},{20,12},{24,0},{28,4},{1,25},{... | collective-permute-start | bytes 147464 | tf_op jit(solution)/shard_map/ppermute | solution.py:255
  6.5 0.6 %collective-permute-start = (bf16[2,8,1536]{2,1,0:T(8,128)(2,1)S(1)}, bf16[2,8,1536]{2,1,0:T(8,128)(2,1)S(1)}, u32[]{:S(2)}, u32[]{:S(2)}) collective-permute-start(bf16[2,8,1536]{2,1,0:T(8,128)(2,1)S(1)} %stack.21), channel_id=1, source_target_pairs={{0,8},{4,12},{8,0},{12,4},{16,24},{20,28},{24,16},{28,20},{1,9},{5... | collective-permute-start | bytes 147464 | tf_op jit(solution)/shard_map/ppermute | solution.py:255
  7.2 3.7 %load_up.1.refs_3_.w_ref = bf16[1536,3072]{1,0:T(8,128)(2,1)S(1)} custom-call(bf16[1536,3072]{1,0:T(8,128)(2,1)} %w_ref.1), custom_call_target="tpu_custom_call" | custom-call | tf_op jit(solution)/shard_map/load_up/pallas_call | solution.py:41
  10.9 0.6 %collective-permute-done.1 = bf16[2,8,1536]{2,1,0:T(8,128)(2,1)S(1)} collective-permute-done((bf16[2,8,1536]{2,1,0:T(8,128)(2,1)S(1)}, bf16[2,8,1536]{2,1,0:T(8,128)(2,1)S(1)}, u32[]{:S(2)}, u32[]{:S(2)}) %collective-permute-start.1) | collective-permute-done | bytes 49184 | tf_op jit(solution)/shard_map/ppermute | solution.py:255
  11.6 1.6 %collective-permute-start.3 = (bf16[2,32,1536]{2,1,0:T(8,128)(2,1)S(1)}, bf16[2,32,1536]{2,1,0:T(8,128)(2,1)S(1)}, u32[]{:S(2)}, u32[]{:S(2)}) collective-permute-start(bf16[2,32,1536]{2,1,0:T(8,128)(2,1)S(1)} %copy_bitcast_fusion.refs_1_), channel_id=1, source_target_pairs={{0,4},{4,0},{8,12},{12,8},{16,20},{20,16},{24,28},{28,24},{1,5},{5... | collective-permute-start | bytes 589832 | tf_op jit(solution)/shard_map/ppermute | solution.py:255
  13.1 3.7 %load_down.1.w_ref.refs_4_.refs_3_ = bf16[3072,1536]{1,0:T(8,128)(2,1)S(1)} custom-call(bf16[3072,1536]{1,0:T(8,128)(2,1)} %refs_0_.1, bf16[2,32,1536]{2,1,0:T(8,128)(2,1)S(1)} %copy_bitcast_fusion.refs_1_), custom_call_target="tpu_custom_call" | custom-call | tf_op jit(solution)/shard_map/load_down/pallas_call | solution.py:41
  17.4 1.7 %pre.1 = (f32[32,3072]{1,0:T(8,128)S(1)}, f32[32,3072]{1,0:T(8,128)S(1)}) custom-call(s32[1]{0:T(128)} %bitcast.core_ref.refs_0_, bf16[32,1536]{1,0:T(8,128)(2,1)S(1)} %get-tuple-element.53.refs_1_, bf16[32,1536]{1,0:T(8,128)(2,1)S(1)} %get-tuple-element.51.refs_2_, bf16[1536,3072]{1,0:T(8,128)(2,1)S(1)} %load_up.1.refs_3_.w_ref, ...), custom_call_target="tpu_custom_call" | custom-call | tf_op jit(solution)/shard_map/pre/pallas_call | solution.py:41
  19.2 1.9 %hid.2 = (f32[32,2048]{1,0:T(8,128)S(1)}, f32[32,2048]{1,0:T(8,128)S(1)}) custom-call(s32[1]{0:T(128)} %bitcast.core_ref.refs_0_, bf16[32,1536]{1,0:T(8,128)(2,1)S(1)} %get-tuple-element.54.near_ref.refs_1_.refs_3_, bf16[32,1536]{1,0:T(8,128)(2,1)S(1)} %get-tuple-element.52.far_ref.refs_2_.refs_4_, bf16[3072,1536]{1,0:T(8,128)(2,1)S(1)} %load_down.1.w_ref.refs_4_.refs_3_), custom_call_target="tpu_custom_call" | custom-call | tf_op jit(solution)/shard_map/hid/pallas_call | solution.py:41
  21.2 1.6 %collective-permute-start.8 = (bf16[32,1536]{1,0:T(8,128)(2,1)S(1)}, bf16[32,1536]{1,0:T(8,128)(2,1)S(1)}, u32[]{:S(2)}, u32[]{:S(2)}) collective-permute-start(bf16[32,1536]{1,0:T(8,128)(2,1)S(1)} %get-tuple-element.30.refs_4_.refs_0_), channel_id=1, source_target_pairs={{0,2},{1,3},{2,0},{3,1},{4,6},{5,7},{6,4},{7,5},{8,10},{9,11},{10,... | collective-permute-start | bytes 294920 | tf_op jit(solution)/shard_map/ppermute | solution.py:258
  23.1 1.0 %hid.3 = (f32[32,1024]{1,0:T(8,128)S(1)}, f32[32,1024]{1,0:T(8,128)S(1)}) custom-call(s32[1]{0:T(128)} %bitcast.core_ref.refs_0_, bf16[32,1536]{1,0:T(8,128)(2,1)S(1)} %get-tuple-element.54.near_ref.refs_1_.refs_3_, bf16[32,1536]{1,0:T(8,128)(2,1)S(1)} %get-tuple-element.52.far_ref.refs_2_.refs_4_, bf16[3072,1536]{1,0:T(8,128)(2,1)S(1)} %load_down.1.w_ref.refs_4_.refs_3_, ...), custom_call_target="tpu_custom_call" | custom-call | tf_op jit(solution)/shard_map/hid/pallas_call | solution.py:41
  24.1 0.9 %collective-permute-start.9 = (bf16[32,1536]{1,0:T(8,128)(2,1)S(1)}, bf16[32,1536]{1,0:T(8,128)(2,1)S(1)}, u32[]{:S(2)}, u32[]{:S(2)}) collective-permute-start(bf16[32,1536]{1,0:T(8,128)(2,1)S(1)} %get-tuple-element.31.refs_5_.refs_0_), channel_id=1, source_target_pairs={{0,2},{1,3},{2,0},{3,1},{4,6},{5,7},{6,4},{7,5},{8,10},{9,11},{10,... | collective-permute-start | bytes 294920 | tf_op jit(solution)/shard_map/ppermute | solution.py:258
  25.0 1.5 %collective-permute-done.8.refs_1_ = bf16[32,1536]{1,0:T(8,128)(2,1)S(1)} collective-permute-done((bf16[32,1536]{1,0:T(8,128)(2,1)S(1)}, bf16[32,1536]{1,0:T(8,128)(2,1)S(1)}, u32[]{:S(2)}, u32[]{:S(2)}) %collective-permute-start.8) | collective-permute-done | bytes 98336 | tf_op jit(solution)/shard_map/ppermute | solution.py:258
  26.7 1.9 %collective-permute-start.7 = (bf16[32,3072]{1,0:T(8,128)(2,1)S(1)}, bf16[32,3072]{1,0:T(8,128)(2,1)S(1)}, u32[]{:S(2)}, u32[]{:S(2)}) collective-permute-start(bf16[32,3072]{1,0:T(8,128)(2,1)S(1)} %add_hid.1.refs_0_), channel_id=1, source_target_pairs={{0,2},{1,3},{2,0},{3,1},{4,6},{5,7},{6,4},{7,5},{8,10},{9,11},{10,... | collective-permute-start | bytes 589832 | tf_op jit(solution)/shard_map/ppermute | solution.py:258
  29.4 4.0 %down_first.1 = (f32[3072,1536]{1,0:T(8,128)}, f32[8,128]{1,0:T(8,128)S(1)}) custom-call(s32[1]{0:T(128)} %bitcast.core_ref.refs_0_, bf16[32,1536]{1,0:T(8,128)(2,1)S(1)} %get-tuple-element.36.refs_1_, bf16[32,1536]{1,0:T(8,128)(2,1)S(1)} %collective-permute-done.10.refs_2_, bf16[32,1536]{1,0:T(8,128)(2,1)S(1)} %get-tuple-element.54.near_ref.refs_1_.refs_3_, ...), custom_call_target="tpu_custom_call" | custom-call | tf_op jit(solution)/shard_map/down_first/pallas_call | solution.py:41
  33.3 0.8 %collective-permute-done.7.refs_1_ = bf16[32,3072]{1,0:T(8,128)(2,1)S(1)} collective-permute-done((bf16[32,3072]{1,0:T(8,128)(2,1)S(1)}, bf16[32,3072]{1,0:T(8,128)(2,1)S(1)}, u32[]{:S(2)}, u32[]{:S(2)}) %collective-permute-start.7) | collective-permute-done | bytes 196640 | tf_op jit(solution)/shard_map/ppermute | solution.py:258
  34.3 1.4 %collective-permute-done.12.p1_ref = bf16[32,3072]{1,0:T(8,128)(2,1)S(1)} collective-permute-done((bf16[32,3072]{1,0:T(8,128)(2,1)S(1)}, bf16[32,3072]{1,0:T(8,128)(2,1)S(1)}, u32[]{:S(2)}, u32[]{:S(2)}) %collective-permute-start.12) | collective-permute-done | bytes 196640 | tf_op jit(solution)/shard_map/ppermute | solution.py:258
  35.7 4.1 %down_last_in.1 = (f32[3072,1536]{1,0:T(8,128)}, f32[32,1536]{1,0:T(8,128)S(1)}, bf16[32,1536]{1,0:T(8,128)(2,1)S(1)}, f32[1,3072]{1,0:T(1,128)S(1)}, bf16[64,3072]{1,0:T(8,128)(2,1)S(1)}) custom-call(s32[1]{0:T(128)} %bitcast.core_ref.refs_0_, bf16[32,3072]{1,0:T(8,128)(2,1)S(1)} %pre_grad.1.p0_ref, ...), custom_call_target="tpu_custom_call", output_to_operand_aliasing={{0}: (8, {})} | custom-call | tf_op jit(solution)/shard_map/down_last_in/pallas_call | solution.py:41
  39.8 1.6 %collective-permute-start.13 = (bf16[32,1536]{1,0:T(8,128)(2,1)S(1)}, bf16[32,1536]{1,0:T(8,128)(2,1)S(1)}, u32[]{:S(2)}, u32[]{:S(2)}) collective-permute-start(bf16[32,1536]{1,0:T(8,128)(2,1)S(1)} %get-tuple-element.41.refs_4_), channel_id=1, source_target_pairs={{0,4},{4,0},{8,12},{12,8},{16,20},{20,16},{24,28},{28,24},{1,5},{5... | collective-permute-start | bytes 294920 | tf_op jit(solution)/shard_map/ppermute | solution.py:255
  41.4 3.0 %up_first.1 = (f32[1536,3072]{1,0:T(8,128)}, f32[8,128]{1,0:T(8,128)S(1)}, f32[1,3072]{1,0:T(1,128)}) custom-call(bf16[64,3072]{1,0:T(8,128)(2,1)S(1)} %get-tuple-element.42.refs_0_, bf16[32,1536]{1,0:T(8,128)(2,1)S(1)} %get-tuple-element.53.refs_1_, bf16[32,1536]{1,0:T(8,128)(2,1)S(1)} %get-tuple-element.51.refs_2_, ...), custom_call_target="tpu_custom_call" | custom-call | tf_op jit(solution)/shard_map/up_first/pallas_call | solution.py:41
  44.8 3.2 %collective-permute-start.16 = (f32[8,1536]{1,0:T(8,128)S(1)}, f32[8,1536]{1,0:T(8,128)S(1)}, u32[]{:S(2)}, u32[]{:S(2)}) collective-permute-start(f32[8,1536]{1,0:T(8,128)S(1)} %get-tuple-element.48), channel_id=1, source_target_pairs={{0,24},{4,28},{8,16},{12,20},{16,8},{20,12},{24,0},{28,4},{1,25},{... | collective-permute-start | bytes 147464 | tf_op jit(solution)/shard_map/ppermute | solution.py:255
  48.0 1.2 %collective-permute-start.14 = (f32[8,1536]{1,0:T(8,128)S(1)}, f32[8,1536]{1,0:T(8,128)S(1)}, u32[]{:S(2)}, u32[]{:S(2)}) collective-permute-start(f32[8,1536]{1,0:T(8,128)S(1)} %get-tuple-element.50), channel_id=1, source_target_pairs={{0,8},{4,12},{8,0},{12,4},{16,24},{20,28},{24,16},{28,20},{1,9},{5... | collective-permute-start | bytes 147464 | tf_op jit(solution)/shard_map/ppermute | solution.py:255
  49.2 4.9 %up_last.1 = f32[1536,3072]{1,0:T(8,128)} custom-call(bf16[64,3072]{1,0:T(8,128)(2,1)S(1)} %get-tuple-element.42.refs_0_, bf16[32,1536]{1,0:T(8,128)(2,1)S(1)} %get-tuple-element.53.refs_1_, bf16[32,1536]{1,0:T(8,128)(2,1)S(1)} %get-tuple-element.51.refs_2_, f32[1536,3072]{1,0:T(8,128)} %get-tuple-element.45.refs_3_, ...), custom_call_target="tpu_custom_call", output_to_operand_aliasing={{}: (3, {})} | custom-call | tf_op jit(solution)/shard_map/up_last/pallas_call | solution.py:41
  54.2 0.6 %fusion.1 = bf16[8,1536]{1,0:T(8,128)(2,1)} fusion(f32[8,1536]{1,0:T(8,128)S(1)} %collective-permute-done.14, f32[32,1536]{1,0:T(8,128)S(1)} %share.1, f32[8,1536]{1,0:T(8,128)S(1)} %collective-permute-done.15, f32[8,1536]{1,0:T(8,128)S(1)} %collective-permute-done.16), kind=kLoop, calls=%fused_computation.8 | loop fusion | flops 49152 | bytes 221184 | tf_op jit(solution)/shard_map/convert_element_type | solution.py:356
  (35 shorter events, 2.5 us)
Async XLA Ops:
  1.4 9.5 %collective-permute-start.2 = (bf16[2,8,1536]{2,1,0:T(8,128)(2,1)S(1)}, bf16[2,8,1536]{2,1,0:T(8,128)(2,1)S(1)}, u32[]{:S(2)}, u32[]{:S(2)}) collective-permute-start(bf16[2,8,1536]{2,1,0:T(8,128)(2,1)S(1)} %stack.21), channel_id=1, source_target_pairs={{0,24},{4,28},{8,16},{12,20},{16,8},{20,12},{24,0},{28,4},{1,25},{... | collective-permute-start | bytes 147464 | tf_op jit(solution)/shard_map/ppermute | solution.py:255
  6.5 5.0 %collective-permute-start.1 = (bf16[2,8,1536]{2,1,0:T(8,128)(2,1)S(1)}, bf16[2,8,1536]{2,1,0:T(8,128)(2,1)S(1)}, u32[]{:S(2)}, u32[]{:S(2)}) collective-permute-start(bf16[2,8,1536]{2,1,0:T(8,128)(2,1)S(1)} %stack.21), channel_id=1, source_target_pairs={{0,16},{4,20},{8,24},{12,28},{16,0},{20,4},{24,8},{28,12},{1,17},{... | collective-permute-start | bytes 147464 | tf_op jit(solution)/shard_map/ppermute | solution.py:255
  6.5 5.0 %collective-permute-start = (bf16[2,8,1536]{2,1,0:T(8,128)(2,1)S(1)}, bf16[2,8,1536]{2,1,0:T(8,128)(2,1)S(1)}, u32[]{:S(2)}, u32[]{:S(2)}) collective-permute-start(bf16[2,8,1536]{2,1,0:T(8,128)(2,1)S(1)} %stack.21), channel_id=1, source_target_pairs={{0,8},{4,12},{8,0},{12,4},{16,24},{20,28},{24,16},{28,20},{1,9},{5... | collective-permute-start | bytes 147464 | tf_op jit(solution)/shard_map/ppermute | solution.py:255
  11.6 5.8 %collective-permute-start.3 = (bf16[2,32,1536]{2,1,0:T(8,128)(2,1)S(1)}, bf16[2,32,1536]{2,1,0:T(8,128)(2,1)S(1)}, u32[]{:S(2)}, u32[]{:S(2)}) collective-permute-start(bf16[2,32,1536]{2,1,0:T(8,128)(2,1)S(1)} %copy_bitcast_fusion.refs_1_), channel_id=1, source_target_pairs={{0,4},{4,0},{8,12},{12,8},{16,20},{20,16},{24,28},{28,24},{1,5},{5... | collective-permute-start | bytes 589832 | tf_op jit(solution)/shard_map/ppermute | solution.py:255
  19.2 1.9 %collective-permute-start.4 = (f32[32,3072]{1,0:T(8,128)S(1)}, f32[32,3072]{1,0:T(8,128)S(1)}, u32[]{:S(2)}, u32[]{:S(2)}) collective-permute-start(f32[32,3072]{1,0:T(8,128)S(1)} %get-tuple-element.28), channel_id=1, source_target_pairs={{0,1},{1,0},{2,3},{3,2},{4,5},{5,4},{6,7},{7,6},{8,9},{9,8},{10,11... | collective-permute-start | bytes 1179656 | tf_op jit(solution)/shard_map/ppermute | solution.py:258
  21.1 1.7 %copy-start = (bf16[3072]{0:T(1024)(128)(2,1)S(1)}, bf16[3072]{0:T(1024)(128)(2,1)}, u32[]{:S(2)}) copy-start(bf16[3072]{0:T(1024)(128)(2,1)} %param.8) | copy-start | bytes 18436
  21.2 5.3 %collective-permute-start.8 = (bf16[32,1536]{1,0:T(8,128)(2,1)S(1)}, bf16[32,1536]{1,0:T(8,128)(2,1)S(1)}, u32[]{:S(2)}, u32[]{:S(2)}) collective-permute-start(bf16[32,1536]{1,0:T(8,128)(2,1)S(1)} %get-tuple-element.30.refs_4_.refs_0_), channel_id=1, source_target_pairs={{0,2},{1,3},{2,0},{3,1},{4,6},{5,7},{6,4},{7,5},{8,10},{9,11},{10,... | collective-permute-start | bytes 294920 | tf_op jit(solution)/shard_map/ppermute | solution.py:258
  22.8 3.9 %collective-permute-start.5 = (f32[32,2048]{1,0:T(8,128)S(1)}, f32[32,2048]{1,0:T(8,128)S(1)}, u32[]{:S(2)}, u32[]{:S(2)}) collective-permute-start(f32[32,2048]{1,0:T(8,128)S(1)} %get-tuple-element.29.refs_2_), channel_id=1, source_target_pairs={{0,1},{1,0},{2,3},{3,2},{4,5},{5,4},{6,7},{7,6},{8,9},{9,8},{10,11... | collective-permute-start | bytes 786440 | tf_op jit(solution)/shard_map/ppermute | solution.py:258
  24.1 5.1 %collective-permute-start.9 = (bf16[32,1536]{1,0:T(8,128)(2,1)S(1)}, bf16[32,1536]{1,0:T(8,128)(2,1)S(1)}, u32[]{:S(2)}, u32[]{:S(2)}) collective-permute-start(bf16[32,1536]{1,0:T(8,128)(2,1)S(1)} %get-tuple-element.31.refs_5_.refs_0_), channel_id=1, source_target_pairs={{0,2},{1,3},{2,0},{3,1},{4,6},{5,7},{6,4},{7,5},{8,10},{9,11},{10,... | collective-permute-start | bytes 294920 | tf_op jit(solution)/shard_map/ppermute | solution.py:258
  25.0 1.7 %collective-permute-start.6 = (f32[32,1024]{1,0:T(8,128)S(1)}, f32[32,1024]{1,0:T(8,128)S(1)}, u32[]{:S(2)}, u32[]{:S(2)}) collective-permute-start(f32[32,1024]{1,0:T(8,128)S(1)} %get-tuple-element.33), channel_id=1, source_target_pairs={{0,1},{1,0},{2,3},{3,2},{4,5},{5,4},{6,7},{7,6},{8,9},{9,8},{10,11... | collective-permute-start | bytes 393224 | tf_op jit(solution)/shard_map/ppermute | solution.py:258
  26.6 2.8 %collective-permute-start.10 = (bf16[32,1536]{1,0:T(8,128)(2,1)S(1)}, bf16[32,1536]{1,0:T(8,128)(2,1)S(1)}, u32[]{:S(2)}, u32[]{:S(2)}) collective-permute-start(bf16[32,1536]{1,0:T(8,128)(2,1)S(1)} %get-tuple-element.36.refs_1_), channel_id=1, source_target_pairs={{0,1},{1,0},{2,3},{3,2},{4,5},{5,4},{6,7},{7,6},{8,9},{9,8},{10,11... | collective-permute-start | bytes 294920 | tf_op jit(solution)/shard_map/ppermute | solution.py:258
  26.7 7.5 %collective-permute-start.7 = (bf16[32,3072]{1,0:T(8,128)(2,1)S(1)}, bf16[32,3072]{1,0:T(8,128)(2,1)S(1)}, u32[]{:S(2)}, u32[]{:S(2)}) collective-permute-start(bf16[32,3072]{1,0:T(8,128)(2,1)S(1)} %add_hid.1.refs_0_), channel_id=1, source_target_pairs={{0,2},{1,3},{2,0},{3,1},{4,6},{5,7},{6,4},{7,5},{8,10},{9,11},{10,... | collective-permute-start | bytes 589832 | tf_op jit(solution)/shard_map/ppermute | solution.py:258
  29.3 4.1 %collective-permute-start.11 = (bf16[32,1536]{1,0:T(8,128)(2,1)S(1)}, bf16[32,1536]{1,0:T(8,128)(2,1)S(1)}, u32[]{:S(2)}, u32[]{:S(2)}) collective-permute-start(bf16[32,1536]{1,0:T(8,128)(2,1)S(1)} %get-tuple-element.37.refs_5_.h0_ref), channel_id=1, source_target_pairs={{0,1},{1,0},{2,3},{3,2},{4,5},{5,4},{6,7},{7,6},{8,9},{9,8},{10,11... | collective-permute-start | bytes 294920 | tf_op jit(solution)/shard_map/ppermute | solution.py:258
  34.2 1.5 %collective-permute-start.12 = (bf16[32,3072]{1,0:T(8,128)(2,1)S(1)}, bf16[32,3072]{1,0:T(8,128)(2,1)S(1)}, u32[]{:S(2)}, u32[]{:S(2)}) collective-permute-start(bf16[32,3072]{1,0:T(8,128)(2,1)S(1)} %pre_grad.1.p0_ref), channel_id=1, source_target_pairs={{0,1},{1,0},{2,3},{3,2},{4,5},{5,4},{6,7},{7,6},{8,9},{9,8},{10,11... | collective-permute-start | bytes 589832 | tf_op jit(solution)/shard_map/ppermute | solution.py:258
  39.8 4.9 %collective-permute-start.13 = (bf16[32,1536]{1,0:T(8,128)(2,1)S(1)}, bf16[32,1536]{1,0:T(8,128)(2,1)S(1)}, u32[]{:S(2)}, u32[]{:S(2)}) collective-permute-start(bf16[32,1536]{1,0:T(8,128)(2,1)S(1)} %get-tuple-element.41.refs_4_), channel_id=1, source_target_pairs={{0,4},{4,0},{8,12},{12,8},{16,20},{20,16},{24,28},{28,24},{1,5},{5... | collective-permute-start | bytes 294920 | tf_op jit(solution)/shard_map/ppermute | solution.py:255
  44.8 9.3 %collective-permute-start.16 = (f32[8,1536]{1,0:T(8,128)S(1)}, f32[8,1536]{1,0:T(8,128)S(1)}, u32[]{:S(2)}, u32[]{:S(2)}) collective-permute-start(f32[8,1536]{1,0:T(8,128)S(1)} %get-tuple-element.48), channel_id=1, source_target_pairs={{0,24},{4,28},{8,16},{12,20},{16,8},{20,12},{24,0},{28,4},{1,25},{... | collective-permute-start | bytes 147464 | tf_op jit(solution)/shard_map/ppermute | solution.py:255
  48.0 6.1 %collective-permute-start.15 = (f32[8,1536]{1,0:T(8,128)S(1)}, f32[8,1536]{1,0:T(8,128)S(1)}, u32[]{:S(2)}, u32[]{:S(2)}) collective-permute-start(f32[8,1536]{1,0:T(8,128)S(1)} %get-tuple-element.49), channel_id=1, source_target_pairs={{0,16},{4,20},{8,24},{12,28},{16,0},{20,4},{24,8},{28,12},{1,17},{... | collective-permute-start | bytes 147464 | tf_op jit(solution)/shard_map/ppermute | solution.py:255
  48.0 6.1 %collective-permute-start.14 = (f32[8,1536]{1,0:T(8,128)S(1)}, f32[8,1536]{1,0:T(8,128)S(1)}, u32[]{:S(2)}, u32[]{:S(2)}) collective-permute-start(f32[8,1536]{1,0:T(8,128)S(1)} %get-tuple-element.50), channel_id=1, source_target_pairs={{0,8},{4,12},{8,0},{12,4},{16,24},{20,28},{24,16},{28,20},{1,9},{5... | collective-permute-start | bytes 147464 | tf_op jit(solution)/shard_map/ppermute | solution.py:255
